TPU v7x, 256 devices: a whole 4x4x8 slice. The times are simulated.
256 devices in a mesh: depth: 8 (over z), rows: 32 (over x, y, core).
Axes of the slice: x: 4, y: 4, z: 8, core: 2. Of those that a mesh axis runs over, the one named last changes fastest.
Arguments:
- grad_arriving: float32 [8, 2, 2048, 2048], P('depth', None, 'rows'), may hold values from -6 to 6
- loss_grad: float32 [2, 2048, 2048], P(None, 'rows'), may hold values from -6 to 6
- t_entry: float32 [8, 2, 2048, 2048], P('depth', None, 'rows'), may hold values from -6 to 6
- t_exit: float32 [8, 2, 2048, 2048], P('depth', None, 'rows'), may hold values from -6 to 6
- fields_entry: float32 [8, 2, 2048, 2048], P('depth', None, 'rows'), may hold values from -6 to 6
- fields_exit: float32 [8, 2, 2048, 2048], P('depth', None, 'rows'), may hold values from -6 to 6
- led_index: int32 [8, 2], P('depth'), may hold values from 0 to 224
Outputs:
- grad_entry: float32 [8, 2, 2048, 2048], P('depth', None, 'rows')
- grad_exit: float32 [8, 2, 2048, 2048], P('depth', None, 'rows')
- leaving: float32 [8, 2, 2048, 2048], P('depth', None, 'rows')
All inputs are finite; a program needn't handle non-finite values.
Results may differ from a plain program's by a relative error of at most 0.0001.
Values sent between devices are 32-bit elements; how exact they have to be, the bound alone decides.
No kernel may reach another device: no remote copies, remote signals or barrier semaphores. Data moves between devices by JAX's collectives and lax.ppermute only.
A program may use at most 128 MiB of HBM per device.

v0:
```python
import functools
import math

import jax
import jax.numpy as jnp
import numpy as np
from jax import lax
from jax.experimental import pallas as pl
from jax.experimental.pallas import tpu as pltpu
from jax.sharding import PartitionSpec as P

LED_SIDE = 15
SPREAD = 3
BLOCKS = 32
N = 2048
WIDTH = N // BLOCKS
LANES = 2 * WIDTH
CLASSES = 1
VMEM_LIMIT = 24 * 1024 * 1024

INVERSE = pow(SPREAD, -1, N)
_k = np.arange(N, dtype=np.int64)
GAUSS = np.exp(-2j * np.pi * ((SPREAD * _k * _k) % N) / N).sum() / N


def chirp_gain(distance):
    return complex(GAUSS * np.exp(2j * np.pi * ((INVERSE * distance * distance) % N) / N))


def shift_of(freq):
    return SPREAD * (freq - BLOCKS // 2) % BLOCKS


def lane_tables():
    own = np.zeros((BLOCKS, LANES), np.float32)
    other = np.zeros((BLOCKS, LANES), np.float32)
    for freq in range(BLOCKS):
        shift = shift_of(freq)
        plain = chirp_gain(-shift)
        wrapped = chirp_gain(BLOCKS - shift)
        for lane in range(LANES):
            sign = -1.0 if lane < WIDTH else 1.0
            if lane % WIDTH >= 2 * shift:
                own[freq, lane] = plain.real
                other[freq, lane] = plain.imag * sign
            else:
                own[freq, lane] = wrapped.imag * sign
                other[freq, lane] = wrapped.real
    return own, other


def lane_ids():
    return lax.broadcasted_iota(jnp.int32, (8, LANES), 1)


def times_i(value):
    sign = jnp.where(lane_ids() < WIDTH, -1.0, 1.0).astype(jnp.float32)
    return pltpu.roll(value, WIDTH, 1) * sign


def scaled(value, factor):
    return value * np.float32(factor.real) + times_i(value) * np.float32(factor.imag)


def turned(value, step, count, sign):
    step %= count
    if step == 0:
        return value
    if 4 * step == count:
        return times_i(value) if sign > 0 else -times_i(value)
    angle = 2.0 * math.pi * sign * step / count
    return scaled(value, complex(math.cos(angle), math.sin(angle)))


def small_dft(values, sign):
    count = len(values)
    if count == 1:
        return values
    if count == 2:
        return [values[0] + values[1], values[0] - values[1]]
    quarter = count // 4
    parts = [small_dft(values[phase::4], sign) for phase in range(4)]
    result = [None] * count
    for j in range(quarter):
        a = parts[0][j]
        b = turned(parts[1][j], j, count, sign)
        c = turned(parts[2][j], 2 * j, count, sign)
        d = turned(parts[3][j], 3 * j, count, sign)
        sum_ac, dif_ac, sum_bd = a + c, a - c, b + d
        dif_bd = times_i(b - d)
        result[j] = sum_ac + sum_bd
        result[j + 2 * quarter] = sum_ac - sum_bd
        if sign > 0:
            result[j + quarter] = dif_ac + dif_bd
            result[j + 3 * quarter] = dif_ac - dif_bd
        else:
            result[j + quarter] = dif_ac - dif_bd
            result[j + 3 * quarter] = dif_ac + dif_bd
    return result


def pack(real, imag):
    low = lane_ids() < WIDTH
    return (
        jnp.where(low, real, pltpu.roll(imag, WIDTH, 1)),
        jnp.where(low, pltpu.roll(real, WIDTH, 1), imag),
    )


def unpack(first, second):
    low = lane_ids() < WIDTH
    return (
        jnp.where(low, first, pltpu.roll(second, WIDTH, 1)),
        jnp.where(low, pltpu.roll(first, WIDTH, 1), second),
    )


def along_lanes(blocks, own_ref, other_ref):
    spectrum = small_dft(blocks, -1)
    moved = []
    for freq, value in enumerate(spectrum):
        shift = 2 * shift_of(freq)
        straight = pltpu.roll(value, shift, 1) if shift else value
        crossed = pltpu.roll(value, shift + WIDTH, 1)
        moved.append(
            straight * own_ref[freq : freq + 1, :] + crossed * other_ref[freq : freq + 1, :]
        )
    return small_dft(moved, 1)


def rows_at(group):
    return pl.ds(pl.multiple_of(group * 8, 8), 8)


def natural_rows(group, parity):
    if CLASSES == 1:
        return rows_at(group)
    return pl.ds(group * 8 * CLASSES + parity, 8, stride=CLASSES)


def enter_kernel(parity, field_ref, own_ref, other_ref, out_ref):
    def step(group, carry):
        rows = natural_rows(group, parity)
        blocks = []
        for pair in range(BLOCKS // 2):
            cols = pl.ds(pair * LANES, LANES)
            blocks += pack(field_ref[0, rows, cols], field_ref[1, rows, cols])
        for block, value in enumerate(along_lanes(blocks, own_ref, other_ref)):
            out_ref[block, rows_at(group), :] = value
        return carry

    lax.fori_loop(0, out_ref.shape[1] // 8, step, 0)


def column_kernel(in_ref, out_ref, held):
    height = in_ref.shape[1]
    unit = height // BLOCKS

    def forward(group, carry):
        spectrum = small_dft([in_ref[r, rows_at(group), :] for r in range(BLOCKS)], -1)
        for freq, value in enumerate(spectrum):
            shift = shift_of(freq)
            turned_value = times_i(value)
            for copy, gain in enumerate((chirp_gain(BLOCKS - shift), chirp_gain(-shift))):
                held[freq, pl.ds(pl.multiple_of(group * 8 + copy * height, 8), 8), :] = (
                    value * np.float32(gain.real) + turned_value * np.float32(gain.imag)
                )
        return carry

    lax.fori_loop(0, height // 8, forward, 0)

    for group in range(height // 8):
        blocks = []
        for freq in range(BLOCKS):
            start = group * 8 + height - unit * shift_of(freq)
            blocks.append(held[freq, pl.ds(start, 8), :])
        for block, value in enumerate(small_dft(blocks, 1)):
            out_ref[block, rows_at(group), :] = value


def turn_kernel(parity, first_ref, wave_ref, t_ref, loss_ref, own_ref, other_ref, out_ref):
    use_loss = first_ref[0] == 1

    def step(group, carry):
        rows = natural_rows(group, parity)
        blocks = []
        for pair in range(BLOCKS // 2):
            cols = pl.ds(pair * LANES, LANES)
            real, imag = unpack(
                wave_ref[2 * pair, rows_at(group), :], wave_ref[2 * pair + 1, rows_at(group), :]
            )
            t_real, t_imag = t_ref[0, rows, cols], t_ref[1, rows, cols]
            pass_real = real * t_real + imag * t_imag
            pass_imag = imag * t_real - real * t_imag
            pass_real = jnp.where(use_loss, loss_ref[0, rows, cols], pass_real)
            pass_imag = jnp.where(use_loss, loss_ref[1, rows, cols], pass_imag)
            blocks += pack(pass_real, pass_imag)
        for block, value in enumerate(along_lanes(blocks, own_ref, other_ref)):
            out_ref[block, rows_at(group), :] = value
        return carry

    lax.fori_loop(0, out_ref.shape[1] // 8, step, 0)


def products_kernel(plain, lit_x_ref, lit_y_ref, field_ref, *refs):
    if plain:
        t_ref, *refs = refs
    wave_refs, out_refs = refs[:CLASSES], refs[CLASSES:]

    def step(group, carry):
        for parity, wave_ref in enumerate(wave_refs):
            rows = natural_rows(group, parity)
            y_real, y_imag = lit_y_ref[0, rows, :], lit_y_ref[1, rows, :]
            for pair in range(BLOCKS // 2):
                cols = pl.ds(pair * LANES, LANES)
                real, imag = unpack(
                    wave_ref[2 * pair, rows_at(group), :],
                    wave_ref[2 * pair + 1, rows_at(group), :],
                )
                if plain:
                    t_real, t_imag = t_ref[0, rows, cols], t_ref[1, rows, cols]
                    out_refs[1][0, rows, cols] = real * t_real + imag * t_imag
                    out_refs[1][1, rows, cols] = imag * t_real - real * t_imag
                x_real, x_imag = lit_x_ref[0:1, cols], lit_x_ref[1:2, cols]
                e_real = x_real * y_real - x_imag * y_imag
                e_imag = x_real * y_imag + x_imag * y_real
                f_real, f_imag = field_ref[0, rows, cols], field_ref[1, rows, cols]
                l_real = f_real * e_real - f_imag * e_imag
                l_imag = f_real * e_imag + f_imag * e_real
                out_refs[0][0, rows, cols] = real * l_real + imag * l_imag
                out_refs[0][1, rows, cols] = imag * l_real - real * l_imag
        return carry

    lax.fori_loop(0, WIDTH // 8 // CLASSES, step, 0)


WHOLE = pl.BlockSpec(memory_space=pltpu.VMEM)
SCALAR = pl.BlockSpec(memory_space=pltpu.SMEM)
HEIGHT = WIDTH // CLASSES
PACKED = jax.ShapeDtypeStruct((BLOCKS, HEIGHT, LANES), jnp.float32)
FIELD = jax.ShapeDtypeStruct((2, WIDTH, N), jnp.float32)


def call(kernel, out_shape, operands, name, scratch=(), scalars=0):
    outs = jax.tree.leaves(out_shape)
    size = sum(4 * math.prod(x.shape) for x in outs) + sum(4 * x.size for x in operands)
    return pl.pallas_call(
        kernel,
        out_shape=out_shape,
        in_specs=[SCALAR] * scalars + [WHOLE] * (len(operands) - scalars),
        out_specs=jax.tree.map(lambda _: WHOLE, out_shape),
        scratch_shapes=list(scratch),
        compiler_params=pltpu.CompilerParams(vmem_limit_bytes=VMEM_LIMIT),
        cost_estimate=pl.CostEstimate(flops=20 * size, bytes_accessed=size, transcendentals=0),
        name=name,
    )(*operands)


def exchange(packed):
    return lax.all_to_all(packed, "rows", split_axis=0, concat_axis=0, tiled=True)


def along_columns(packed):
    return call(
        column_kernel,
        PACKED,
        [packed],
        "columns",
        scratch=[pltpu.VMEM((BLOCKS, 2 * HEIGHT, LANES), jnp.float32)],
    )


def to_previous(value):
    count = lax.axis_size("depth")
    return lax.ppermute(value, "depth", [(s, (s - 1) % count) for s in range(count)])


def light(led_number, row_start):
    shift_col = led_number // LED_SIDE - LED_SIDE // 2
    shift_row = led_number % LED_SIDE - LED_SIDE // 2
    cols = shift_col * jnp.arange(N, dtype=jnp.int32) % N
    rows = shift_row * (row_start + jnp.arange(WIDTH, dtype=jnp.int32)) % N
    angle_x = 2.0 * math.pi / N * cols.astype(jnp.float32)
    angle_y = 2.0 * math.pi / N * rows.astype(jnp.float32)
    lit_x = jnp.stack([jnp.cos(angle_x), jnp.sin(angle_x)])
    lit_y = jnp.stack([jnp.cos(angle_y), jnp.sin(angle_y)])
    return lit_x, jnp.broadcast_to(lit_y[:, :, None], (2, WIDTH, LANES))


def per_device(grad_arriving, loss_grad, t_entry, t_exit, fields_entry, fields_exit, led_index):
    own, other = (jnp.asarray(table) for table in lane_tables())
    row_start = lax.axis_index("rows") * WIDTH
    first = (lax.axis_index("depth") == 0).astype(jnp.int32).reshape(1)
    waves, packed = [], []
    for parity in range(CLASSES):
        sent = call(
            functools.partial(enter_kernel, parity),
            PACKED,
            [grad_arriving[0], own, other],
            "enter",
        )
        waves.append(exchange(along_columns(exchange(sent))))
    for parity in range(CLASSES):
        packed.append(
            call(
                functools.partial(turn_kernel, parity),
                PACKED,
                [first, waves[parity], t_entry[0], loss_grad, own, other],
                "turn",
                scalars=1,
            )
        )
    grad_entry = call(
        functools.partial(products_kernel, False),
        FIELD,
        [*light(led_index[0, 0], row_start), fields_entry[0], *waves],
        "products",
    )
    seconds = [exchange(along_columns(exchange(to_previous(value)))) for value in packed]
    grad_exit, leaving = call(
        functools.partial(products_kernel, True),
        (FIELD, FIELD),
        [*light(led_index[0, 1], row_start), fields_exit[0], t_exit[0], *seconds],
        "products",
    )
    return (grad_entry[None], grad_exit[None], leaving[None])


def solution(mesh):
    spread = P("depth", None, "rows", None)
    return jax.shard_map(
        per_device,
        mesh=mesh,
        in_specs=(spread, P(None, "rows", None), spread, spread, spread, spread, P("depth", None)),
        out_specs=(spread, spread, spread),
        check_vma=False,
    )
```

profile of v0, /device:TPU:1, one launch (start us, length us, event | category | flops | bytes accessed | tf_op | source)
XLA Modules:
  0.0 149.6 jit_solution(18139209627364167897)
XLA Ops:
  0.6 0.7 copy-done.6
  1.4 1.2 copy-done.5
  2.6 0.7 copy-done.7
  3.3 6.0 %enter.1 = f32[32,64,128]{2,1,0:T(8,128)S(1)} custom-call(f32[2,64,2048]{2,1,0:T(8,128)S(1)} %bitcast.19, f32[32,128]{1,0:T(8,128)S(1)} %copy-done.7, f32[32,128]{1,0:T(8,128)S(1)} %copy-done.6), custom_call_target="tpu_custom_call" | custom-call | flops 42598400 | bytes 2129920 | tf_op jit(solution)/shard_map/enter/pallas_call | solution.py:247
  9.3 25.3 %all_to_all.20.in_ref = f32[32,64,128]{2,1,0:T(8,128)S(1)} all-to-all(f32[32,64,128]{2,1,0:T(8,128)S(1)} %enter.1), channel_id=1, replica_groups=mesh['depth'=8,'rows'=32] {'rows'}, dimensions={0} | all-to-all | bytes 2097152 | tf_op jit(solution)/shard_map/all_to_all | solution.py:260
  34.6 6.0 %columns.2 = f32[32,64,128]{2,1,0:T(8,128)} custom-call(f32[32,64,128]{2,1,0:T(8,128)S(1)} %all_to_all.20.in_ref), custom_call_target="tpu_custom_call" | custom-call | flops 41943040 | bytes 2097152 | tf_op jit(solution)/shard_map/columns/pallas_call | solution.py:247
  40.6 4.1 %all-to-all-start.1 = ((f32[32,64,128]{2,1,0:T(8,128)}), f32[32,64,128]{2,1,0:T(8,128)S(1)}, u32[]{:S(2)}, u32[]{:S(2)}) async-start(f32[32,64,128]{2,1,0:T(8,128)} %columns.2), calls=%async_computation.1 | async-start | bytes 2097152 | tf_op jit(solution)/shard_map/all_to_all | solution.py:260
  44.7 16.9 %all-to-all-done.1.refs_0_.wave_ref = f32[32,64,128]{2,1,0:T(8,128)S(1)} async-done(((f32[32,64,128]{2,1,0:T(8,128)}), f32[32,64,128]{2,1,0:T(8,128)S(1)}, u32[]{:S(2)}, u32[]{:S(2)}) %all-to-all-start.1) | async-done | bytes 1048608 | tf_op jit(solution)/shard_map/all_to_all | solution.py:260
  61.6 6.6 %turn.1 = f32[32,64,128]{2,1,0:T(8,128)S(1)} custom-call(s32[1]{0:T(128)} %bitcast.11.first_ref, f32[32,64,128]{2,1,0:T(8,128)S(1)} %all-to-all-done.1.refs_0_.wave_ref, f32[2,64,2048]{2,1,0:T(8,128)S(1)} %bitcast.15, f32[2,64,2048]{2,1,0:T(8,128)S(1)} %copy-done.1, f32[32,128]{1,0:T(8,128)S(1)} %copy-done.8, f32[32,128]{1,0:T(8,128)S(1)} %copy-done.6), custom_call_target="tpu_custom_call" | custom-call | flops 84541520 | bytes 4227076 | tf_op jit(solution)/shard_map/turn/pallas_call | solution.py:247
  68.2 5.7 %collective-permute-start = (f32[32,64,128]{2,1,0:T(8,128)S(1)}, f32[32,64,128]{2,1,0:T(8,128)}, u32[]{:S(2)}, u32[]{:S(2)}) collective-permute-start(f32[32,64,128]{2,1,0:T(8,128)S(1)} %turn.1), channel_id=1, source_target_pairs={{0,224},{32,0},{64,32},{96,64},{128,96},{160,128},{192,160},{224,1... | collective-permute-start | bytes 3145736 | tf_op jit(solution)/shard_map/ppermute | solution.py:275
  73.9 22.4 %collective-permute-done = f32[32,64,128]{2,1,0:T(8,128)} collective-permute-done((f32[32,64,128]{2,1,0:T(8,128)S(1)}, f32[32,64,128]{2,1,0:T(8,128)}, u32[]{:S(2)}, u32[]{:S(2)}) %collective-permute-start) | collective-permute-done | bytes 1048608 | tf_op jit(solution)/shard_map/ppermute | solution.py:275
  96.3 4.5 %all-to-all-start.2 = ((f32[32,64,128]{2,1,0:T(8,128)}), f32[32,64,128]{2,1,0:T(8,128)S(1)}, u32[]{:S(2)}, u32[]{:S(2)}) async-start(f32[32,64,128]{2,1,0:T(8,128)} %collective-permute-done), calls=%async_computation.2 | async-start | bytes 2097152 | tf_op jit(solution)/shard_map/all_to_all | solution.py:260
  100.8 0.6 fusion.20
  105.5 12.3 %all-to-all-done.2.in_ref = f32[32,64,128]{2,1,0:T(8,128)S(1)} async-done(((f32[32,64,128]{2,1,0:T(8,128)}), f32[32,64,128]{2,1,0:T(8,128)S(1)}, u32[]{:S(2)}, u32[]{:S(2)}) %all-to-all-start.2) | async-done | bytes 1048608 | tf_op jit(solution)/shard_map/all_to_all | solution.py:260
  117.8 6.0 %columns.3 = f32[32,64,128]{2,1,0:T(8,128)} custom-call(f32[32,64,128]{2,1,0:T(8,128)S(1)} %all-to-all-done.2.in_ref), custom_call_target="tpu_custom_call" | custom-call | flops 41943040 | bytes 2097152 | tf_op jit(solution)/shard_map/columns/pallas_call | solution.py:247
  123.8 4.1 %all-to-all-start.3 = ((f32[32,64,128]{2,1,0:T(8,128)}), f32[32,64,128]{2,1,0:T(8,128)S(1)}, u32[]{:S(2)}, u32[]{:S(2)}) async-start(f32[32,64,128]{2,1,0:T(8,128)} %columns.3), calls=%async_computation.3 | async-start | bytes 2097152 | tf_op jit(solution)/shard_map/all_to_all | solution.py:260
  127.9 0.3 fusion.6
  128.2 0.3 fusion.8
  128.6 0.1 broadcast_in_dim.10.lit_y_ref
  128.6 1.8 %products.2 = f32[2,64,2048]{2,1,0:T(8,128)} custom-call(f32[2,2048]{1,0:T(2,128)S(1)} %pad_maximum_fusion.lit_x_ref, f32[2,64,128]{2,1,0:T(8,128)S(1)} %broadcast_in_dim.10.lit_y_ref, f32[2,64,2048]{2,1,0:T(8,128)S(1)} %bitcast.16, f32[32,64,128]{2,1,0:T(8,128)S(1)} %all-to-all-done.1.refs_0_.wave_ref), custom_call_target="tpu_custom_call" | custom-call | flops 64552960 | bytes 3227648 | tf_op jit(solution)/shard_map/products/pallas_call | solution.py:247
  130.5 14.4 %all-to-all-done.3.refs_1_ = f32[32,64,128]{2,1,0:T(8,128)S(1)} async-done(((f32[32,64,128]{2,1,0:T(8,128)}), f32[32,64,128]{2,1,0:T(8,128)S(1)}, u32[]{:S(2)}, u32[]{:S(2)}) %all-to-all-start.3) | async-done | bytes 1048608 | tf_op jit(solution)/shard_map/all_to_all | solution.py:260
  144.9 1.2 copy-done.3
  146.1 1.2 copy-done.4
  147.4 2.2 %products.3 = (f32[2,64,2048]{2,1,0:T(8,128)}, f32[2,64,2048]{2,1,0:T(8,128)}) custom-call(f32[2,2048]{1,0:T(2,128)S(1)} %pad_maximum_fusion.1.lit_x_ref, f32[2,64,128]{2,1,0:T(8,128)S(1)} %broadcast_in_dim.23.lit_y_ref, f32[2,64,2048]{2,1,0:T(8,128)S(1)} %bitcast.17, f32[2,64,2048]{2,1,0:T(8,128)S(1)} %bitcast.18, f32[32,64,128]{2,1,0:T(8,128)S(1)} %all-to-all-done.3.refs_1_), custom_call_target="tpu_custom_call" | custom-call | flops 106496000 | bytes 5324800 | tf_op jit(solution)/shard_map/products/pallas_call | solution.py:247
  (22 shorter events, 0.3 us)
Async XLA Ops:
  0.6 0.7 copy-start.6
  1.4 1.2 copy-start.5
  2.6 0.7 copy-start.7
  34.6 27.0 %copy-start.8 = (f32[32,128]{1,0:T(8,128)S(1)}, f32[32,128]{1,0:T(8,128)}, u32[]{:S(2)}) copy-start(f32[32,128]{1,0:T(8,128)} %constant.87.clone.own_ref) | copy-start | bytes 49156
  40.6 21.0 %copy-start = (f32[1,2,64,2048]{3,2,1,0:T(8,128)S(1)}, f32[1,2,64,2048]{3,2,1,0:T(8,128)}, u32[]{:S(2)}) copy-start(f32[1,2,64,2048]{3,2,1,0:T(8,128)} %param.11) | copy-start | bytes 3145732
  40.6 21.0 %copy-start.1 = (f32[2,64,2048]{2,1,0:T(8,128)S(1)}, f32[2,64,2048]{2,1,0:T(8,128)}, u32[]{:S(2)}) copy-start(f32[2,64,2048]{2,1,0:T(8,128)} %loss_ref.1) | copy-start | bytes 3145732
  40.6 21.0 %all-to-all-start.1 = ((f32[32,64,128]{2,1,0:T(8,128)}), f32[32,64,128]{2,1,0:T(8,128)S(1)}, u32[]{:S(2)}, u32[]{:S(2)}) async-start(f32[32,64,128]{2,1,0:T(8,128)} %columns.2), calls=%async_computation.1 | async-start | bytes 2097152 | tf_op jit(solution)/shard_map/all_to_all | solution.py:260
  68.2 32.6 %copy-start.9 = (s32[1,2]{1,0:T(1,128)S(1)}, s32[1,2]{1,0:T(1,128)}, u32[]{:S(2)}) copy-start(s32[1,2]{1,0:T(1,128)} %param.15) | copy-start | bytes 28
  68.2 28.1 %collective-permute-start = (f32[32,64,128]{2,1,0:T(8,128)S(1)}, f32[32,64,128]{2,1,0:T(8,128)}, u32[]{:S(2)}, u32[]{:S(2)}) collective-permute-start(f32[32,64,128]{2,1,0:T(8,128)S(1)} %turn.1), channel_id=1, source_target_pairs={{0,224},{32,0},{64,32},{96,64},{128,96},{160,128},{192,160},{224,1... | collective-permute-start | bytes 3145736 | tf_op jit(solution)/shard_map/ppermute | solution.py:275
  96.3 21.5 %all-to-all-start.2 = ((f32[32,64,128]{2,1,0:T(8,128)}), f32[32,64,128]{2,1,0:T(8,128)S(1)}, u32[]{:S(2)}, u32[]{:S(2)}) async-start(f32[32,64,128]{2,1,0:T(8,128)} %collective-permute-done), calls=%async_computation.2 | async-start | bytes 2097152 | tf_op jit(solution)/shard_map/all_to_all | solution.py:260
  123.8 4.8 %copy-start.2 = (f32[1,2,64,2048]{3,2,1,0:T(8,128)S(1)}, f32[1,2,64,2048]{3,2,1,0:T(8,128)}, u32[]{:S(2)}) copy-start(f32[1,2,64,2048]{3,2,1,0:T(8,128)} %param.13) | copy-start | bytes 3145732
  123.8 21.0 %all-to-all-start.3 = ((f32[32,64,128]{2,1,0:T(8,128)}), f32[32,64,128]{2,1,0:T(8,128)S(1)}, u32[]{:S(2)}, u32[]{:S(2)}) async-start(f32[32,64,128]{2,1,0:T(8,128)} %columns.3), calls=%async_computation.3 | async-start | bytes 2097152 | tf_op jit(solution)/shard_map/all_to_all | solution.py:260
  144.9 1.2 copy-start.3
  146.1 1.2 copy-start.4
where the time goes:
time: 150 us
  waiting for transfers between devices  66 us (44%)
  Pallas kernels  28.6 us (19%)
  blocking collectives  25.3 us (17%)
  starting transfers between devices  18.3 us (12%)
  local copies, waits for them, and re-layouts  5.86 us (4%)
  between operations  4.71 us (3%)
    all_to_all x3, waiting for transfers between devices, exchange(): lax.all_to_all(packed, 'rows', split_axis=0, concat_axis=0, tiled=True)  43.6 us
    pallas_call x6, Pallas kernels, call(): pl.pallas_call(kernel, out_shape=out_shape, in_specs=[SCALAR] * scalars +...  28.6 us
    all_to_all x1, blocking collectives, exchange(): lax.all_to_all(packed, 'rows', split_axis=0, concat_axis=0, tiled=True)  25.3 us
    ppermute x1, waiting for transfers between devices, to_previous(): lax.ppermute(value, 'depth', [(s, (s - 1) % count) for s in range(count)])  22.4 us
    all_to_all x3, starting transfers between devices, exchange(): lax.all_to_all(packed, 'rows', split_axis=0, concat_axis=0, tiled=True)  12.7 us
    ppermute x1, starting transfers between devices, to_previous(): lax.ppermute(value, 'depth', [(s, (s - 1) % count) for s in range(count)])  5.65 us
    unnamed x20, local copies, waits for them, and re-layouts  5.13 us
  transfers between devices with their start and end apart: 4, of which 4 were waited for; matrix products, arithmetic and copies ran while one was open for 1% of the time, Pallas kernels for 1%

commit v1 on v0

v1 whole, which is shorter than its diff:
```python
import functools
import math

import jax
import jax.numpy as jnp
import numpy as np
from jax import lax
from jax.experimental import pallas as pl
from jax.experimental.pallas import tpu as pltpu
from jax.sharding import PartitionSpec as P

LED_SIDE = 15
SPREAD = 3
BLOCKS = 32
N = 2048
WIDTH = N // BLOCKS
LANES = 2 * WIDTH
HALF = WIDTH // 4
TILES = HALF // 8
VMEM_LIMIT = 24 * 1024 * 1024

INVERSE = pow(SPREAD, -1, N)
_k = np.arange(N, dtype=np.int64)
GAUSS = np.exp(-2j * np.pi * ((SPREAD * _k * _k) % N) / N).sum() / N


def chirp_gain(distance):
    return complex(GAUSS * np.exp(2j * np.pi * ((INVERSE * distance * distance) % N) / N))


def shift_of(freq):
    return SPREAD * (freq - BLOCKS // 2) % BLOCKS


def plus(a, b):
    return (a[0] + b[0], a[1] + b[1])


def minus(a, b):
    return (a[0] - b[0], a[1] - b[1])


def times_i(a):
    return (-a[1], a[0])


def times(a, real, imag):
    return (a[0] * real - a[1] * imag, a[0] * imag + a[1] * real)


def scaled(a, factor):
    return times(a, np.float32(factor.real), np.float32(factor.imag))


def turned(a, step, count, sign):
    step = step * sign % count
    if step == 0:
        return a
    if 2 * step == count:
        return (-a[0], -a[1])
    if 4 * step == count:
        return times_i(a)
    if 4 * step == 3 * count:
        return (a[1], -a[0])
    if 8 * step % count == 0:
        root = np.float32(math.sqrt(0.5))
        eighth = 8 * step // count
        added, taken = (a[0] + a[1]) * root, (a[0] - a[1]) * root
        return {
            1: (taken, added),
            3: (-added, taken),
            5: (-taken, -added),
            7: (added, -taken),
        }[eighth]
    angle = 2.0 * math.pi * step / count
    return scaled(a, complex(math.cos(angle), math.sin(angle)))


def small_dft(values, sign):
    count = len(values)
    if count == 1:
        return values
    if count == 2:
        return [plus(*values), minus(*values)]
    quarter = count // 4
    parts = [small_dft(values[phase::4], sign) for phase in range(4)]
    result = [None] * count
    for j in range(quarter):
        a, b, c, d = (turned(parts[k][j], j * k, count, sign) for k in range(4))
        sum_ac, dif_ac, sum_bd, dif_bd = plus(a, c), minus(a, c), plus(b, d), minus(b, d)
        result[j] = plus(sum_ac, sum_bd)
        result[j + 2 * quarter] = minus(sum_ac, sum_bd)
        up = (dif_ac[0] - dif_bd[1], dif_ac[1] + dif_bd[0])
        down = (dif_ac[0] + dif_bd[1], dif_ac[1] - dif_bd[0])
        result[j + quarter], result[j + 3 * quarter] = (up, down) if sign > 0 else (down, up)
    return result


def lane_ids():
    return lax.broadcasted_iota(jnp.int32, (8, LANES), 1)


def halves(first, second):
    low = lane_ids() < WIDTH
    return (
        jnp.where(low, first, pltpu.roll(second, WIDTH, 1)),
        jnp.where(low, pltpu.roll(first, WIDTH, 1), second),
    )


def tile(index):
    return pl.ds(8 * index, 8)


def get(ref, block, rows):
    return (ref[block, 0, rows, :], ref[block, 1, rows, :])


def put(ref, block, rows, value):
    ref[block, 0, rows, :] = value[0]
    ref[block, 1, rows, :] = value[1]


def block_dft(load, emit, stage, rows, sign):
    for k in range(4):
        for j, value in enumerate(small_dft([load(4 * n + k) for n in range(8)], sign)):
            put(stage, 8 * k + j, rows, turned(value, j * k, BLOCKS, sign))
    for j in range(8):
        outs = small_dft([get(stage, 8 * k + j, rows) for k in range(4)], sign)
        for step, value in enumerate(outs):
            emit(j + 8 * step, value)


def along_lanes(load, out_ref, stage, moved):
    inside = lane_ids() % WIDTH
    for index in range(TILES):
        rows = tile(index)

        def move(freq, value):
            shift = 2 * shift_of(freq)
            if shift:
                mask = inside >= shift
                value = tuple(
                    jnp.where(mask, pltpu.roll(v, shift, 1), pltpu.roll(v, shift + WIDTH, 1))
                    for v in value
                )
                plain, wrapped = chirp_gain(-(shift // 2)), chirp_gain(BLOCKS - shift // 2)
                real = jnp.where(mask, np.float32(plain.real), np.float32(wrapped.real))
                imag = jnp.where(mask, np.float32(plain.imag), np.float32(wrapped.imag))
                value = times(value, real, imag)
            else:
                value = scaled(value, chirp_gain(0))
            put(moved, freq, rows, value)

        block_dft(functools.partial(load, index), move, stage, rows, -1)
        block_dft(
            lambda freq: get(moved, freq, rows),
            lambda block, value: put(out_ref, block, rows, value),
            stage,
            rows,
            1,
        )


def split_rows(read, parity_outs, apart):
    for pair in range(BLOCKS // 2):
        for part in range(2):
            for quarter in range(4):
                slot = (pair * 2 + part) * 4 + quarter
                apart[slot] = read(part, quarter, pl.ds(pair * LANES, LANES))
    for parity, out in parity_outs:
        for pair in range(BLOCKS // 2):
            for part in range(2):
                slot = (pair * 2 + part) * 4
                for index in range(TILES):
                    upper, lower = (
                        apart[slot + index + TILES * half, pl.ds(parity, 8, stride=2), :]
                        for half in range(2)
                    )
                    left, right = halves(upper, lower)
                    out[2 * pair, part, tile(index), :] = left
                    out[2 * pair + 1, part, tile(index), :] = right


def enter_kernel(parity, field_ref, out_ref, apart, packed, stage, moved):
    def read(part, quarter, cols):
        return field_ref[part, pl.ds(16 * quarter, 16), cols]

    split_rows(read, [(parity, packed)], apart)
    along_lanes(
        lambda index, block: get(packed, block, tile(index)), out_ref, stage, moved
    )


def gather_kernel(first_ref, t_ref, loss_ref, even_ref, odd_ref, apart):
    use_loss = first_ref[0] == 1

    def read_from(ref):
        return lambda part, quarter, cols: ref[part, pl.ds(16 * quarter, 16), cols]

    @pl.when(use_loss)
    def _():
        split_rows(read_from(loss_ref), [(0, even_ref), (1, odd_ref)], apart)

    @pl.when(jnp.logical_not(use_loss))
    def _():
        split_rows(read_from(t_ref), [(0, even_ref), (1, odd_ref)], apart)


def turn_kernel(first_ref, wave_ref, other_ref, out_ref, stage, moved):
    use_loss = first_ref[0] == 1

    def load(index, block):
        real, imag = get(wave_ref, block, tile(index))
        t_real, t_imag = get(other_ref, block, tile(index))
        return (
            jnp.where(use_loss, t_real, real * t_real + imag * t_imag),
            jnp.where(use_loss, t_imag, imag * t_real - real * t_imag),
        )

    along_lanes(load, out_ref, stage, moved)


def column_kernel(in_ref, out_ref, stage, held):
    low = lane_ids() < WIDTH
    for index in range(TILES):
        rows = tile(index)

        def hold(freq, value):
            shift = shift_of(freq)
            plain = scaled(value, chirp_gain(-shift))
            wrapped = scaled(value, chirp_gain(BLOCKS - shift)) if shift else None
            if shift > HALF:
                put(held, freq, rows, wrapped)
            if shift < HALF:
                put(held, freq, pl.ds(2 * HALF + 8 * index, 8), plain)
            if shift:
                crossed = tuple(
                    pltpu.roll(jnp.where(low, p, w), WIDTH, 1) for p, w in zip(plain, wrapped)
                )
                put(held, freq, pl.ds(HALF + 8 * index, 8), crossed)

        block_dft(lambda block: get(in_ref, block, rows), hold, stage, rows, -1)
    for index in range(TILES):
        rows = tile(index)
        block_dft(
            lambda freq: get(held, freq, pl.ds(2 * HALF - shift_of(freq) + 8 * index, 8)),
            lambda block, value: put(out_ref, block, rows, value),
            stage,
            rows,
            1,
        )


def products_kernel(plain, lit_x_ref, lit_y_ref, field_ref, *refs):
    if plain:
        t_ref, *refs = refs
    even_ref, odd_ref, *out_refs, whole = refs
    for pair in range(BLOCKS // 2):
        for part in range(2):
            for parity, wave_ref in enumerate((even_ref, odd_ref)):
                for index in range(TILES):
                    upper, lower = halves(
                        wave_ref[2 * pair, part, tile(index), :],
                        wave_ref[2 * pair + 1, part, tile(index), :],
                    )
                    for half, value in enumerate((upper, lower)):
                        start = 16 * (index + TILES * half) + parity
                        whole[2 * pair + part, pl.ds(start, 8, stride=2), :] = value

    def step(group, carry):
        rows = pl.ds(pl.multiple_of(8 * group, 8), 8)
        y_real, y_imag = lit_y_ref[0, rows, :], lit_y_ref[1, rows, :]
        for pair in range(BLOCKS // 2):
            cols = pl.ds(pair * LANES, LANES)
            real, imag = whole[2 * pair, rows, :], whole[2 * pair + 1, rows, :]
            if plain:
                t_real, t_imag = t_ref[0, rows, cols], t_ref[1, rows, cols]
                out_refs[1][0, rows, cols] = real * t_real + imag * t_imag
                out_refs[1][1, rows, cols] = imag * t_real - real * t_imag
            x_real, x_imag = lit_x_ref[0:1, cols], lit_x_ref[1:2, cols]
            e_real = x_real * y_real - x_imag * y_imag
            e_imag = x_real * y_imag + x_imag * y_real
            f_real, f_imag = field_ref[0, rows, cols], field_ref[1, rows, cols]
            l_real = f_real * e_real - f_imag * e_imag
            l_imag = f_real * e_imag + f_imag * e_real
            out_refs[0][0, rows, cols] = real * l_real + imag * l_imag
            out_refs[0][1, rows, cols] = imag * l_real - real * l_imag
        return carry

    lax.fori_loop(0, WIDTH // 8, step, 0)


WHOLE = pl.BlockSpec(memory_space=pltpu.VMEM)
SCALAR = pl.BlockSpec(memory_space=pltpu.SMEM)
CHAIN = (BLOCKS, 2, HALF, LANES)
PACKED = jax.ShapeDtypeStruct(CHAIN, jnp.float32)
FIELD = jax.ShapeDtypeStruct((2, WIDTH, N), jnp.float32)
BUFFER = pltpu.VMEM(CHAIN, jnp.float32)
APART = pltpu.VMEM((8 * BLOCKS // 2, 16, LANES), jnp.float32)


def call(kernel, out_shape, operands, name, scratch=(), scalars=0):
    outs = jax.tree.leaves(out_shape)
    size = sum(4 * math.prod(x.shape) for x in outs) + sum(4 * x.size for x in operands)
    return pl.pallas_call(
        kernel,
        out_shape=out_shape,
        in_specs=[SCALAR] * scalars + [WHOLE] * (len(operands) - scalars),
        out_specs=jax.tree.map(lambda _: WHOLE, out_shape),
        scratch_shapes=list(scratch),
        compiler_params=pltpu.CompilerParams(vmem_limit_bytes=VMEM_LIMIT),
        cost_estimate=pl.CostEstimate(flops=20 * size, bytes_accessed=size, transcendentals=0),
        name=name,
    )(*operands)


def exchange(packed):
    return lax.all_to_all(packed, "rows", split_axis=0, concat_axis=0, tiled=True)


def along_columns(packed):
    held = pltpu.VMEM((BLOCKS, 2, 3 * HALF, LANES), jnp.float32)
    return call(column_kernel, PACKED, [packed], "columns", scratch=[BUFFER, held])


def to_previous(value):
    count = lax.axis_size("depth")
    return lax.ppermute(value, "depth", [(s, (s - 1) % count) for s in range(count)])


def light(led_number, row_start):
    shift_col = led_number // LED_SIDE - LED_SIDE // 2
    shift_row = led_number % LED_SIDE - LED_SIDE // 2
    cols = shift_col * jnp.arange(N, dtype=jnp.int32) % N
    rows = shift_row * (row_start + jnp.arange(WIDTH, dtype=jnp.int32)) % N
    angle_x = 2.0 * math.pi / N * cols.astype(jnp.float32)
    angle_y = 2.0 * math.pi / N * rows.astype(jnp.float32)
    lit_x = jnp.stack([jnp.cos(angle_x), jnp.sin(angle_x)])
    lit_y = jnp.stack([jnp.cos(angle_y), jnp.sin(angle_y)])
    return lit_x, jnp.broadcast_to(lit_y[:, :, None], (2, WIDTH, LANES))


def products(plain, operands):
    return call(
        functools.partial(products_kernel, plain),
        (FIELD, FIELD) if plain else FIELD,
        operands,
        "products",
        scratch=[pltpu.VMEM((BLOCKS, WIDTH, LANES), jnp.float32)],
    )


def per_device(grad_arriving, loss_grad, t_entry, t_exit, fields_entry, fields_exit, led_index):
    row_start = lax.axis_index("rows") * WIDTH
    first = (lax.axis_index("depth") == 0).astype(jnp.int32).reshape(1)
    others = call(
        gather_kernel, (PACKED, PACKED), [first, t_entry[0], loss_grad], "gather", [APART], 1
    )
    firsts, seconds = [], []
    for parity in range(2):
        sent = call(
            functools.partial(enter_kernel, parity),
            PACKED,
            [grad_arriving[0]],
            "enter",
            scratch=[APART, BUFFER, BUFFER, BUFFER],
        )
        firsts.append(exchange(along_columns(exchange(sent))))
    for parity in range(2):
        sent = call(
            turn_kernel,
            PACKED,
            [first, firsts[parity], others[parity]],
            "turn",
            scratch=[BUFFER, BUFFER],
            scalars=1,
        )
        if parity == 0:
            returned = along_columns(exchange(to_previous(sent)))
        else:
            returned = to_previous(along_columns(exchange(sent)))
        seconds.append(exchange(returned))
    grad_entry = products(
        False, [*light(led_index[0, 0], row_start), fields_entry[0], *firsts]
    )
    grad_exit, leaving = products(
        True, [*light(led_index[0, 1], row_start), fields_exit[0], t_exit[0], *seconds]
    )
    return (grad_entry[None], grad_exit[None], leaving[None])


def solution(mesh):
    spread = P("depth", None, "rows", None)
    return jax.shard_map(
        per_device,
        mesh=mesh,
        in_specs=(spread, P(None, "rows", None), spread, spread, spread, spread, P("depth", None)),
        out_specs=(spread, spread, spread),
        check_vma=False,
    )
```

time: 150 us -> 147 us (0.980)
  starting transfers between devices: 18.3 us -> 50.4 us
  blocking collectives: 25.3 us -> 0 us
  Pallas kernels: 28.6 us -> 13 us
  waiting for transfers between devices: 66 us -> 71.8 us
    all_to_all x3 -> x8, waiting for transfers between devices: 43.6 us -> 71.8 us  [exchange(): lax.all_to_all(packed, 'rows', split_axis=0, concat_axis=0, tiled=True)]
    all_to_all x3 -> x8, starting transfers between devices: 12.7 us -> 39.1 us  [exchange(): lax.all_to_all(packed, 'rows', split_axis=0, concat_axis=0, tiled=True)]
    all_to_all x1 -> x0, blocking collectives: 25.3 us -> none  [exchange(): lax.all_to_all(packed, 'rows', split_axis=0, concat_axis=0, tiled=True)]
    ppermute x1 -> x2, waiting for transfers between devices: 22.4 us -> 0.01 us  [to_previous(): lax.ppermute(value, 'depth', [(s, (s - 1) % count) for s in range(count)])]
    pallas_call x6 -> x11, Pallas kernels: 28.6 us -> 13 us  [call(): pl.pallas_call(kernel, out_shape=out_shape, in_specs=[SCALAR] * scalars +...]
    ppermute x1 -> x2, starting transfers between devices: 5.65 us -> 11.3 us  [to_previous(): lax.ppermute(value, 'depth', [(s, (s - 1) % count) for s in range(count)])]
  transfers between devices with their start and end apart: 4 -> 10, of which waited for: 4 -> 8; matrix products, arithmetic and copies ran while one was open for 1% -> 1% of each run, Pallas kernels for 1% -> 6%
where the time goes in v1:
time: 147 us; the launch traced here: 146 us
  waiting for transfers between devices  71.8 us (49%)
  starting transfers between devices  50.4 us (34%)
  Pallas kernels  13 us (9%)
  local copies, waits for them, and re-layouts  5.22 us (4%)
  between operations  4.82 us (3%)
    all_to_all x8, waiting for transfers between devices, exchange(): lax.all_to_all(packed, 'rows', split_axis=0, concat_axis=0, tiled=True)  71.8 us
    all_to_all x8, starting transfers between devices, exchange(): lax.all_to_all(packed, 'rows', split_axis=0, concat_axis=0, tiled=True)  39.1 us
    pallas_call x11, Pallas kernels, call(): pl.pallas_call(kernel, out_shape=out_shape, in_specs=[SCALAR] * scalars +...  13 us
    ppermute x2, starting transfers between devices, to_previous(): lax.ppermute(value, 'depth', [(s, (s - 1) % count) for s in range(count)])  11.3 us
    unnamed x20, local copies, waits for them, and re-layouts  4.49 us
  transfers between devices with their start and end apart: 10, of which 8 were waited for; matrix products, arithmetic and copies ran while one was open for 1% of the time, Pallas kernels for 6%

profile of v1, /device:TPU:1, one launch (start us, length us, event | category | flops | bytes accessed | tf_op | source)
XLA Modules:
  0.0 145.9 jit_solution(10955900956677781626)
XLA Ops:
  1.9 1.5 %enter.3 = f32[32,2,16,128]{3,2,1,0:T(8,128)} custom-call(f32[2,64,2048]{2,1,0:T(8,128)S(1)} %bitcast.15), custom_call_target="tpu_custom_call" | custom-call | flops 31457280 | bytes 1572864 | tf_op jit(solution)/shard_map/enter/pallas_call | solution.py:306
  3.3 8.6 %all-to-all-start.2 = ((f32[32,2,16,128]{3,2,1,0:T(8,128)}), f32[32,2,16,128]{3,2,1,0:T(8,128)S(1)}, u32[]{:S(2)}, u32[]{:S(2)}) async-start(f32[32,2,16,128]{3,2,1,0:T(8,128)} %enter.3), calls=%async_computation.2 | async-start | bytes 1048576 | tf_op jit(solution)/shard_map/all_to_all | solution.py:319
  11.9 1.5 %enter.2 = f32[32,2,16,128]{3,2,1,0:T(8,128)} custom-call(f32[2,64,2048]{2,1,0:T(8,128)S(1)} %bitcast.16), custom_call_target="tpu_custom_call" | custom-call | flops 31457280 | bytes 1572864 | tf_op jit(solution)/shard_map/enter/pallas_call | solution.py:306
  13.4 10.1 %all-to-all-done.2.in_ref = f32[32,2,16,128]{3,2,1,0:T(8,128)S(1)} async-done(((f32[32,2,16,128]{3,2,1,0:T(8,128)}), f32[32,2,16,128]{3,2,1,0:T(8,128)S(1)}, u32[]{:S(2)}, u32[]{:S(2)}) %all-to-all-start.2) | async-done | bytes 524320 | tf_op jit(solution)/shard_map/all_to_all | solution.py:319
  23.5 3.7 %all-to-all-start = ((f32[32,2,16,128]{3,2,1,0:T(8,128)}), f32[32,2,16,128]{3,2,1,0:T(8,128)S(1)}, u32[]{:S(2)}, u32[]{:S(2)}) async-start(f32[32,2,16,128]{3,2,1,0:T(8,128)} %enter.2), calls=%async_computation | async-start | bytes 1048576 | tf_op jit(solution)/shard_map/all_to_all | solution.py:319
  28.4 10.4 %all-to-all-done.in_ref = f32[32,2,16,128]{3,2,1,0:T(8,128)S(1)} async-done(((f32[32,2,16,128]{3,2,1,0:T(8,128)}), f32[32,2,16,128]{3,2,1,0:T(8,128)S(1)}, u32[]{:S(2)}, u32[]{:S(2)}) %all-to-all-start) | async-done | bytes 524320 | tf_op jit(solution)/shard_map/all_to_all | solution.py:319
  38.8 3.7 %all-to-all-start.3 = ((f32[32,2,16,128]{3,2,1,0:T(8,128)}), f32[32,2,16,128]{3,2,1,0:T(8,128)S(1)}, u32[]{:S(2)}, u32[]{:S(2)}) async-start(f32[32,2,16,128]{3,2,1,0:T(8,128)} %columns.5), calls=%async_computation.3 | async-start | bytes 1048576 | tf_op jit(solution)/shard_map/all_to_all | solution.py:319
  43.7 10.3 %all-to-all-done.3.refs_1_.wave_ref = f32[32,2,16,128]{3,2,1,0:T(8,128)S(1)} async-done(((f32[32,2,16,128]{3,2,1,0:T(8,128)}), f32[32,2,16,128]{3,2,1,0:T(8,128)S(1)}, u32[]{:S(2)}, u32[]{:S(2)}) %all-to-all-start.3) | async-done | bytes 524320 | tf_op jit(solution)/shard_map/all_to_all | solution.py:319
  54.1 3.7 %all-to-all-start.1 = ((f32[32,2,16,128]{3,2,1,0:T(8,128)}), f32[32,2,16,128]{3,2,1,0:T(8,128)S(1)}, u32[]{:S(2)}, u32[]{:S(2)}) async-start(f32[32,2,16,128]{3,2,1,0:T(8,128)} %columns.4), calls=%async_computation.1 | async-start | bytes 1048576 | tf_op jit(solution)/shard_map/all_to_all | solution.py:319
  58.9 1.3 turn.3
  60.2 9.1 %all-to-all-done.1.refs_0_.wave_ref = f32[32,2,16,128]{3,2,1,0:T(8,128)S(1)} async-done(((f32[32,2,16,128]{3,2,1,0:T(8,128)}), f32[32,2,16,128]{3,2,1,0:T(8,128)S(1)}, u32[]{:S(2)}, u32[]{:S(2)}) %all-to-all-start.1) | async-done | bytes 524320 | tf_op jit(solution)/shard_map/all_to_all | solution.py:319
  69.3 3.7 %all-to-all-start.6 = ((f32[32,2,16,128]{3,2,1,0:T(8,128)}), f32[32,2,16,128]{3,2,1,0:T(8,128)S(1)}, u32[]{:S(2)}, u32[]{:S(2)}) async-start(f32[32,2,16,128]{3,2,1,0:T(8,128)} %turn.3), calls=%async_computation.6 | async-start | bytes 1048576 | tf_op jit(solution)/shard_map/all_to_all | solution.py:319
  73.5 5.7 %collective-permute-start = (f32[32,2,16,128]{3,2,1,0:T(8,128)S(1)}, f32[32,2,16,128]{3,2,1,0:T(8,128)}, u32[]{:S(2)}, u32[]{:S(2)}) collective-permute-start(f32[32,2,16,128]{3,2,1,0:T(8,128)S(1)} %turn.2), channel_id=1, source_target_pairs={{0,224},{32,0},{64,32},{96,64},{128,96},{160,128},{192,160},{224,1... | collective-permute-start | bytes 1572872 | tf_op jit(solution)/shard_map/ppermute | solution.py:329
  79.2 5.4 %all-to-all-done.6.in_ref = f32[32,2,16,128]{3,2,1,0:T(8,128)S(1)} async-done(((f32[32,2,16,128]{3,2,1,0:T(8,128)}), f32[32,2,16,128]{3,2,1,0:T(8,128)S(1)}, u32[]{:S(2)}, u32[]{:S(2)}) %all-to-all-start.6) | async-done | bytes 524320 | tf_op jit(solution)/shard_map/all_to_all | solution.py:319
  85.0 5.7 %collective-permute-start.1 = (f32[32,2,16,128]{3,2,1,0:T(8,128)S(1)}, f32[32,2,16,128]{3,2,1,0:T(8,128)}, u32[]{:S(2)}, u32[]{:S(2)}) collective-permute-start(f32[32,2,16,128]{3,2,1,0:T(8,128)S(1)} %columns.7), channel_id=1, source_target_pairs={{0,224},{32,0},{64,32},{96,64},{128,96},{160,128},{192,160},{224,1... | collective-permute-start | bytes 1572872 | tf_op jit(solution)/shard_map/ppermute | solution.py:329
  90.7 8.4 %all-to-all-start.4 = ((f32[32,2,16,128]{3,2,1,0:T(8,128)}), f32[32,2,16,128]{3,2,1,0:T(8,128)S(1)}, u32[]{:S(2)}, u32[]{:S(2)}) async-start(f32[32,2,16,128]{3,2,1,0:T(8,128)} %collective-permute-done), calls=%async_computation.4 | async-start | bytes 1048576 | tf_op jit(solution)/shard_map/all_to_all | solution.py:319
  103.7 7.0 %all-to-all-done.4.in_ref = f32[32,2,16,128]{3,2,1,0:T(8,128)S(1)} async-done(((f32[32,2,16,128]{3,2,1,0:T(8,128)}), f32[32,2,16,128]{3,2,1,0:T(8,128)S(1)}, u32[]{:S(2)}, u32[]{:S(2)}) %all-to-all-start.4) | async-done | bytes 524320 | tf_op jit(solution)/shard_map/all_to_all | solution.py:319
  110.7 3.7 %all-to-all-start.7 = ((f32[32,2,16,128]{3,2,1,0:T(8,128)}), f32[32,2,16,128]{3,2,1,0:T(8,128)S(1)}, u32[]{:S(2)}, u32[]{:S(2)}) async-start(f32[32,2,16,128]{3,2,1,0:T(8,128)} %collective-permute-done.1), calls=%async_computation.7 | async-start | bytes 1048576 | tf_op jit(solution)/shard_map/all_to_all | solution.py:319
  116.2 9.8 %all-to-all-done.7.refs_2_ = f32[32,2,16,128]{3,2,1,0:T(8,128)S(1)} async-done(((f32[32,2,16,128]{3,2,1,0:T(8,128)}), f32[32,2,16,128]{3,2,1,0:T(8,128)S(1)}, u32[]{:S(2)}, u32[]{:S(2)}) %all-to-all-start.7) | async-done | bytes 524320 | tf_op jit(solution)/shard_map/all_to_all | solution.py:319
  126.0 3.7 %all-to-all-start.5 = ((f32[32,2,16,128]{3,2,1,0:T(8,128)}), f32[32,2,16,128]{3,2,1,0:T(8,128)S(1)}, u32[]{:S(2)}, u32[]{:S(2)}) async-start(f32[32,2,16,128]{3,2,1,0:T(8,128)} %columns.6), calls=%async_computation.5 | async-start | bytes 1048576 | tf_op jit(solution)/shard_map/all_to_all | solution.py:319
  129.8 1.7 %products.2 = f32[2,64,2048]{2,1,0:T(8,128)} custom-call(f32[2,2048]{1,0:T(2,128)S(1)} %pad_maximum_fusion.lit_x_ref, f32[2,64,128]{2,1,0:T(8,128)S(1)} %broadcast_in_dim.10.lit_y_ref, f32[2,64,2048]{2,1,0:T(8,128)S(1)} %bitcast.17, f32[32,2,16,128]{3,2,1,0:T(8,128)S(1)} %all-to-all-done.1.refs_0_.wave_ref, ...), custom_call_target="tpu_custom_call" | custom-call | flops 64552960 | bytes 3227648 | tf_op jit(solution)/shard_map/products/pallas_call | solution.py:306
  131.5 9.7 %all-to-all-done.5.refs_1_ = f32[32,2,16,128]{3,2,1,0:T(8,128)S(1)} async-done(((f32[32,2,16,128]{3,2,1,0:T(8,128)}), f32[32,2,16,128]{3,2,1,0:T(8,128)S(1)}, u32[]{:S(2)}, u32[]{:S(2)}) %all-to-all-start.5) | async-done | bytes 524320 | tf_op jit(solution)/shard_map/all_to_all | solution.py:319
  141.3 1.2 copy-done.3
  143.8 2.1 %products.3 = (f32[2,64,2048]{2,1,0:T(8,128)}, f32[2,64,2048]{2,1,0:T(8,128)}) custom-call(f32[2,2048]{1,0:T(2,128)S(1)} %pad_maximum_fusion.1.lit_x_ref, f32[2,64,128]{2,1,0:T(8,128)S(1)} %broadcast_in_dim.23.lit_y_ref, f32[2,64,2048]{2,1,0:T(8,128)S(1)} %bitcast.18, f32[2,64,2048]{2,1,0:T(8,128)S(1)} %bitcast.19, ...), custom_call_target="tpu_custom_call" | custom-call | flops 106496000 | bytes 5324800 | tf_op jit(solution)/shard_map/products/pallas_call | solution.py:306
  (38 shorter events, 9.6 us)
Async XLA Ops:
  0.6 1.2 copy-start
  1.9 10.1 %copy-start.1 = (f32[1,2,64,2048]{3,2,1,0:T(8,128)S(1)}, f32[1,2,64,2048]{3,2,1,0:T(8,128)}, u32[]{:S(2)}) copy-start(f32[1,2,64,2048]{3,2,1,0:T(8,128)} %param.7) | copy-start | bytes 3145732
  3.3 20.2 %all-to-all-start.2 = ((f32[32,2,16,128]{3,2,1,0:T(8,128)}), f32[32,2,16,128]{3,2,1,0:T(8,128)S(1)}, u32[]{:S(2)}, u32[]{:S(2)}) async-start(f32[32,2,16,128]{3,2,1,0:T(8,128)} %enter.3), calls=%async_computation.2 | async-start | bytes 1048576 | tf_op jit(solution)/shard_map/all_to_all | solution.py:319
  23.5 15.3 %all-to-all-start = ((f32[32,2,16,128]{3,2,1,0:T(8,128)}), f32[32,2,16,128]{3,2,1,0:T(8,128)S(1)}, u32[]{:S(2)}, u32[]{:S(2)}) async-start(f32[32,2,16,128]{3,2,1,0:T(8,128)} %enter.2), calls=%async_computation | async-start | bytes 1048576 | tf_op jit(solution)/shard_map/all_to_all | solution.py:319
  38.8 15.3 %all-to-all-start.3 = ((f32[32,2,16,128]{3,2,1,0:T(8,128)}), f32[32,2,16,128]{3,2,1,0:T(8,128)S(1)}, u32[]{:S(2)}, u32[]{:S(2)}) async-start(f32[32,2,16,128]{3,2,1,0:T(8,128)} %columns.5), calls=%async_computation.3 | async-start | bytes 1048576 | tf_op jit(solution)/shard_map/all_to_all | solution.py:319
  42.5 15.3 %copy-start.5 = (f32[1,2,64,2048]{3,2,1,0:T(8,128)S(1)}, f32[1,2,64,2048]{3,2,1,0:T(8,128)}, u32[]{:S(2)}) copy-start(f32[1,2,64,2048]{3,2,1,0:T(8,128)} %param.9) | copy-start | bytes 3145732
  42.5 15.3 %copy-start.6 = (f32[2,64,2048]{2,1,0:T(8,128)S(1)}, f32[2,64,2048]{2,1,0:T(8,128)}, u32[]{:S(2)}) copy-start(f32[2,64,2048]{2,1,0:T(8,128)} %loss_ref.1) | copy-start | bytes 3145732
  54.1 15.3 %all-to-all-start.1 = ((f32[32,2,16,128]{3,2,1,0:T(8,128)}), f32[32,2,16,128]{3,2,1,0:T(8,128)S(1)}, u32[]{:S(2)}, u32[]{:S(2)}) async-start(f32[32,2,16,128]{3,2,1,0:T(8,128)} %columns.4), calls=%async_computation.1 | async-start | bytes 1048576 | tf_op jit(solution)/shard_map/all_to_all | solution.py:319
  58.1 0.8 copy-start.7
  60.2 12.8 %copy-start.8 = (f32[32,2,16,128]{3,2,1,0:T(8,128)S(1)}, f32[32,2,16,128]{3,2,1,0:T(8,128)}, u32[]{:S(2)}) copy-start(f32[32,2,16,128]{3,2,1,0:T(8,128)} %copy-done.7) | copy-start | bytes 1572868
  69.3 15.3 %all-to-all-start.6 = ((f32[32,2,16,128]{3,2,1,0:T(8,128)}), f32[32,2,16,128]{3,2,1,0:T(8,128)S(1)}, u32[]{:S(2)}, u32[]{:S(2)}) async-start(f32[32,2,16,128]{3,2,1,0:T(8,128)} %turn.3), calls=%async_computation.6 | async-start | bytes 1048576 | tf_op jit(solution)/shard_map/all_to_all | solution.py:319
  73.5 17.1 %collective-permute-start = (f32[32,2,16,128]{3,2,1,0:T(8,128)S(1)}, f32[32,2,16,128]{3,2,1,0:T(8,128)}, u32[]{:S(2)}, u32[]{:S(2)}) collective-permute-start(f32[32,2,16,128]{3,2,1,0:T(8,128)S(1)} %turn.2), channel_id=1, source_target_pairs={{0,224},{32,0},{64,32},{96,64},{128,96},{160,128},{192,160},{224,1... | collective-permute-start | bytes 1572872 | tf_op jit(solution)/shard_map/ppermute | solution.py:329
  85.0 14.1 %copy-start.9 = (s32[1,2]{1,0:T(1,128)S(1)}, s32[1,2]{1,0:T(1,128)}, u32[]{:S(2)}) copy-start(s32[1,2]{1,0:T(1,128)} %param.13) | copy-start | bytes 28
  85.0 18.7 %collective-permute-start.1 = (f32[32,2,16,128]{3,2,1,0:T(8,128)S(1)}, f32[32,2,16,128]{3,2,1,0:T(8,128)}, u32[]{:S(2)}, u32[]{:S(2)}) collective-permute-start(f32[32,2,16,128]{3,2,1,0:T(8,128)S(1)} %columns.7), channel_id=1, source_target_pairs={{0,224},{32,0},{64,32},{96,64},{128,96},{160,128},{192,160},{224,1... | collective-permute-start | bytes 1572872 | tf_op jit(solution)/shard_map/ppermute | solution.py:329
  90.7 20.1 %all-to-all-start.4 = ((f32[32,2,16,128]{3,2,1,0:T(8,128)}), f32[32,2,16,128]{3,2,1,0:T(8,128)S(1)}, u32[]{:S(2)}, u32[]{:S(2)}) async-start(f32[32,2,16,128]{3,2,1,0:T(8,128)} %collective-permute-done), calls=%async_computation.4 | async-start | bytes 1048576 | tf_op jit(solution)/shard_map/all_to_all | solution.py:319
  110.7 15.3 %all-to-all-start.7 = ((f32[32,2,16,128]{3,2,1,0:T(8,128)}), f32[32,2,16,128]{3,2,1,0:T(8,128)S(1)}, u32[]{:S(2)}, u32[]{:S(2)}) async-start(f32[32,2,16,128]{3,2,1,0:T(8,128)} %collective-permute-done.1), calls=%async_computation.7 | async-start | bytes 1048576 | tf_op jit(solution)/shard_map/all_to_all | solution.py:319
  115.0 14.8 %copy-start.2 = (f32[1,2,64,2048]{3,2,1,0:T(8,128)S(1)}, f32[1,2,64,2048]{3,2,1,0:T(8,128)}, u32[]{:S(2)}) copy-start(f32[1,2,64,2048]{3,2,1,0:T(8,128)} %param.11) | copy-start | bytes 3145732
  126.0 15.3 %all-to-all-start.5 = ((f32[32,2,16,128]{3,2,1,0:T(8,128)}), f32[32,2,16,128]{3,2,1,0:T(8,128)S(1)}, u32[]{:S(2)}, u32[]{:S(2)}) async-start(f32[32,2,16,128]{3,2,1,0:T(8,128)} %columns.6), calls=%async_computation.5 | async-start | bytes 1048576 | tf_op jit(solution)/shard_map/all_to_all | solution.py:319
  141.3 1.2 copy-start.3
  142.5 1.2 copy-start.4

commit v2 on v1

v2 whole, which is shorter than its diff:
```python
import functools
import math

import jax
import jax.numpy as jnp
import numpy as np
from jax import lax
from jax.experimental import pallas as pl
from jax.experimental.pallas import tpu as pltpu
from jax.sharding import PartitionSpec as P

LED_SIDE = 15
SPREAD = 3
BLOCKS = 32
N = 2048
WIDTH = N // BLOCKS
LANES = 2 * WIDTH
HALF = WIDTH // 2
TILES = HALF // 8
VMEM_LIMIT = 24 * 1024 * 1024

INVERSE = pow(SPREAD, -1, N)
_k = np.arange(N, dtype=np.int64)
GAUSS = np.exp(-2j * np.pi * ((SPREAD * _k * _k) % N) / N).sum() / N


def chirp_gain(distance):
    return complex(GAUSS * np.exp(2j * np.pi * ((INVERSE * distance * distance) % N) / N))


def shift_of(freq):
    pairs = SPREAD * (freq - BLOCKS // 2) % BLOCKS
    return 2 * pairs, chirp_gain(-pairs), chirp_gain(BLOCKS - pairs)


def plus(a, b):
    return (a[0] + b[0], a[1] + b[1])


def minus(a, b):
    return (a[0] - b[0], a[1] - b[1])


def times_i(a):
    return (-a[1], a[0])


def times(a, real, imag):
    return (a[0] * real - a[1] * imag, a[0] * imag + a[1] * real)


def scaled(a, factor):
    return times(a, np.float32(factor.real), np.float32(factor.imag))


def turned(a, step, count, sign):
    step = step * sign % count
    if step == 0:
        return a
    if 2 * step == count:
        return (-a[0], -a[1])
    if 4 * step == count:
        return times_i(a)
    if 4 * step == 3 * count:
        return (a[1], -a[0])
    if 8 * step % count == 0:
        root = np.float32(math.sqrt(0.5))
        eighth = 8 * step // count
        added, taken = (a[0] + a[1]) * root, (a[0] - a[1]) * root
        return {
            1: (taken, added),
            3: (-added, taken),
            5: (-taken, -added),
            7: (added, -taken),
        }[eighth]
    angle = 2.0 * math.pi * step / count
    return scaled(a, complex(math.cos(angle), math.sin(angle)))


def small_dft(values, sign):
    count = len(values)
    if count == 1:
        return values
    if count == 2:
        return [plus(*values), minus(*values)]
    quarter = count // 4
    parts = [small_dft(values[phase::4], sign) for phase in range(4)]
    result = [None] * count
    for j in range(quarter):
        a, b, c, d = (turned(parts[k][j], j * k, count, sign) for k in range(4))
        sum_ac, dif_ac, sum_bd, dif_bd = plus(a, c), minus(a, c), plus(b, d), minus(b, d)
        result[j] = plus(sum_ac, sum_bd)
        result[j + 2 * quarter] = minus(sum_ac, sum_bd)
        up = (dif_ac[0] - dif_bd[1], dif_ac[1] + dif_bd[0])
        down = (dif_ac[0] + dif_bd[1], dif_ac[1] - dif_bd[0])
        result[j + quarter], result[j + 3 * quarter] = (up, down) if sign > 0 else (down, up)
    return result


def lane_ids():
    return lax.broadcasted_iota(jnp.int32, (8, LANES), 1)


def halves(first, second):
    low = lane_ids() < WIDTH
    return (
        jnp.where(low, first, pltpu.roll(second, WIDTH, 1)),
        jnp.where(low, pltpu.roll(first, WIDTH, 1), second),
    )


def tile(index):
    return pl.ds(8 * index, 8)


def get(ref, block, rows):
    return (ref[block, 0, rows, :], ref[block, 1, rows, :])


def put(ref, block, rows, value):
    ref[block, 0, rows, :] = value[0]
    ref[block, 1, rows, :] = value[1]


def block_dft(load, emit, stage, rows, sign):
    for k in range(4):
        for j, value in enumerate(small_dft([load(4 * n + k) for n in range(8)], sign)):
            put(stage, 8 * k + j, rows, turned(value, j * k, BLOCKS, sign))
    for j in range(8):
        outs = small_dft([get(stage, 8 * k + j, rows) for k in range(4)], sign)
        for step, value in enumerate(outs):
            emit(j + 8 * step, value)


def along_lanes(load, store, stage, moved):
    inside = lane_ids() % WIDTH
    for index in range(TILES):
        rows = tile(index)

        def move(freq, value):
            shift, plain, wrapped = shift_of(freq)
            if shift:
                mask = inside >= shift
                value = tuple(
                    jnp.where(mask, pltpu.roll(v, shift, 1), pltpu.roll(v, shift + WIDTH, 1))
                    for v in value
                )
                real = jnp.where(mask, np.float32(plain.real), np.float32(wrapped.real))
                imag = jnp.where(mask, np.float32(plain.imag), np.float32(wrapped.imag))
                value = times(value, real, imag)
            else:
                value = scaled(value, plain)
            put(moved, freq, rows, value)

        block_dft(functools.partial(load, index), move, stage, rows, -1)
        block_dft(
            lambda freq: get(moved, freq, rows), functools.partial(store, index), stage, rows, 1
        )


def along_rows(load, store, stage, held):
    low = lane_ids() < WIDTH
    for index in range(TILES):
        rows = tile(index)

        def hold(freq, value):
            shift, plain, wrapped = shift_of(freq)
            plain = scaled(value, plain)
            wrapped = scaled(value, wrapped) if shift else None
            if shift > HALF:
                put(held, freq, rows, wrapped)
            if shift < HALF:
                put(held, freq, pl.ds(2 * HALF + 8 * index, 8), plain)
            if shift:
                crossed = tuple(
                    pltpu.roll(jnp.where(low, p, w), WIDTH, 1) for p, w in zip(plain, wrapped)
                )
                put(held, freq, pl.ds(HALF + 8 * index, 8), crossed)

        block_dft(functools.partial(load, index), hold, stage, rows, -1)
    for index in range(TILES):
        block_dft(
            lambda freq: get(held, freq, pl.ds(2 * HALF - shift_of(freq)[0] + 8 * index, 8)),
            functools.partial(store, index),
            stage,
            tile(index),
            1,
        )


def natural(index, half):
    return pl.ds(8 * index + HALF * half, 8)


def read_pair(ref, index, pair):
    cols = pl.ds(pair * LANES, LANES)
    parts = [
        halves(ref[part, natural(index, 0), cols], ref[part, natural(index, 1), cols])
        for part in range(2)
    ]
    return [(parts[0][side], parts[1][side]) for side in range(2)]


def read_field(ref, write):
    for index in range(TILES):
        for pair in range(BLOCKS // 2):
            for side, value in enumerate(read_pair(ref, index, pair)):
                write(index, 2 * pair + side, value)


def enter_kernel(first_ref, field_ref, t_ref, loss_ref, out_ref, packed, stage, moved):
    read_field(field_ref, lambda index, block, value: put(packed, block, tile(index), value))
    along_lanes(
        lambda index, block: get(packed, block, tile(index)),
        lambda index, block, value: put(out_ref.at[:, 0], block, tile(index), value),
        stage,
        moved,
    )

    def other(index, block, value):
        put(out_ref.at[:, 1], block, tile(index), value)

    @pl.when(first_ref[0] == 1)
    def _():
        read_field(loss_ref, other)

    @pl.when(first_ref[0] != 1)
    def _():
        read_field(t_ref, other)


def column_kernel(first_ref, in_ref, wave_ref, out_ref, stage, held):
    use_loss = first_ref[0] == 1
    along_rows(
        lambda index, block: get(in_ref.at[:, 0], block, tile(index)),
        lambda index, block, value: put(wave_ref, block, tile(index), value),
        stage,
        held,
    )

    def passing(index, block):
        real, imag = get(wave_ref, block, tile(index))
        t_real, t_imag = get(in_ref.at[:, 1], block, tile(index))
        return (
            jnp.where(use_loss, t_real, real * t_real + imag * t_imag),
            jnp.where(use_loss, t_imag, imag * t_real - real * t_imag),
        )

    along_rows(
        passing,
        lambda index, block, value: put(out_ref, block, tile(index), value),
        stage,
        held,
    )


def write_products(wave, lit_x_ref, lit_y_ref, field_ref, out_ref, t_ref=None, plain_ref=None):
    for index in range(TILES):
        lit_y = [
            (lit_y_ref[0, natural(index, half), :], lit_y_ref[1, natural(index, half), :])
            for half in range(2)
        ]
        for pair in range(BLOCKS // 2):
            cols = pl.ds(pair * LANES, LANES)
            left, right = wave(index, 2 * pair), wave(index, 2 * pair + 1)
            reals, imags = halves(left[0], right[0]), halves(left[1], right[1])
            lit_x = (lit_x_ref[0:1, cols], lit_x_ref[1:2, cols])
            for half in range(2):
                rows = natural(index, half)
                real, imag = reals[half], imags[half]
                if t_ref is not None:
                    t_real, t_imag = t_ref[0, rows, cols], t_ref[1, rows, cols]
                    plain_ref[0, rows, cols] = real * t_real + imag * t_imag
                    plain_ref[1, rows, cols] = imag * t_real - real * t_imag
                lit = times(lit_y[half], *lit_x)
                f_real, f_imag = times(lit, field_ref[0, rows, cols], field_ref[1, rows, cols])
                out_ref[0, rows, cols] = real * f_real + imag * f_imag
                out_ref[1, rows, cols] = imag * f_real - real * f_imag


def entry_kernel(lit_x_ref, lit_y_ref, field_ref, wave_ref, out_ref):
    write_products(
        lambda index, block: get(wave_ref, block, tile(index)),
        lit_x_ref,
        lit_y_ref,
        field_ref,
        out_ref,
    )


def exit_kernel(
    lit_x_ref, lit_y_ref, field_ref, t_ref, in_ref, out_ref, plain_ref, packed, stage, moved
):
    along_lanes(
        lambda index, block: get(in_ref, block, tile(index)),
        lambda index, block, value: put(packed, block, tile(index), value),
        stage,
        moved,
    )
    write_products(
        lambda index, block: get(packed, block, tile(index)),
        lit_x_ref,
        lit_y_ref,
        field_ref,
        out_ref,
        t_ref,
        plain_ref,
    )


WHOLE = pl.BlockSpec(memory_space=pltpu.VMEM)
SCALAR = pl.BlockSpec(memory_space=pltpu.SMEM)
CHAIN = (BLOCKS, 2, HALF, LANES)
PACKED = jax.ShapeDtypeStruct(CHAIN, jnp.float32)
BOTH = jax.ShapeDtypeStruct((BLOCKS, 2, 2, HALF, LANES), jnp.float32)
FIELD = jax.ShapeDtypeStruct((2, WIDTH, N), jnp.float32)
BUFFER = pltpu.VMEM(CHAIN, jnp.float32)
HELD = pltpu.VMEM((BLOCKS, 2, 3 * HALF, LANES), jnp.float32)


def call(kernel, out_shape, operands, name, scratch=(), scalars=0):
    outs = jax.tree.leaves(out_shape)
    size = sum(4 * math.prod(x.shape) for x in outs) + sum(4 * x.size for x in operands)
    return pl.pallas_call(
        kernel,
        out_shape=out_shape,
        in_specs=[SCALAR] * scalars + [WHOLE] * (len(operands) - scalars),
        out_specs=jax.tree.map(lambda _: WHOLE, out_shape),
        scratch_shapes=list(scratch),
        compiler_params=pltpu.CompilerParams(vmem_limit_bytes=VMEM_LIMIT),
        cost_estimate=pl.CostEstimate(flops=20 * size, bytes_accessed=size, transcendentals=0),
        name=name,
    )(*operands)


def exchange(packed):
    return lax.all_to_all(packed, "rows", split_axis=0, concat_axis=0, tiled=True)


def to_previous(value):
    count = lax.axis_size("depth")
    return lax.ppermute(value, "depth", [(s, (s - 1) % count) for s in range(count)])


def light(led_number, row_start):
    shift_col = led_number // LED_SIDE - LED_SIDE // 2
    shift_row = led_number % LED_SIDE - LED_SIDE // 2
    cols = shift_col * jnp.arange(N, dtype=jnp.int32) % N
    rows = shift_row * (row_start + jnp.arange(WIDTH, dtype=jnp.int32)) % N
    angle_x = 2.0 * math.pi / N * cols.astype(jnp.float32)
    angle_y = 2.0 * math.pi / N * rows.astype(jnp.float32)
    lit_x = jnp.stack([jnp.cos(angle_x), jnp.sin(angle_x)])
    lit_y = jnp.stack([jnp.cos(angle_y), jnp.sin(angle_y)])
    return lit_x, jnp.broadcast_to(lit_y[:, :, None], (2, WIDTH, LANES))


def per_device(grad_arriving, loss_grad, t_entry, t_exit, fields_entry, fields_exit, led_index):
    row_start = lax.axis_index("rows") * WIDTH
    first = (lax.axis_index("depth") == 0).astype(jnp.int32).reshape(1)
    both = call(
        enter_kernel,
        BOTH,
        [first, grad_arriving[0], t_entry[0], loss_grad],
        "enter",
        [BUFFER, BUFFER, BUFFER],
        1,
    )
    wave, onward = call(
        column_kernel, (PACKED, PACKED), [first, exchange(both)], "columns", [BUFFER, HELD], 1
    )
    onward = to_previous(onward)
    wave = exchange(wave)
    grad_entry = call(
        entry_kernel,
        FIELD,
        [*light(led_index[0, 0], row_start), fields_entry[0], wave],
        "entry",
    )
    grad_exit, leaving = call(
        exit_kernel,
        (FIELD, FIELD),
        [
            *light(led_index[0, 1], row_start),
            fields_exit[0],
            t_exit[0],
            exchange(onward),
        ],
        "exit",
        [BUFFER, BUFFER, BUFFER],
    )
    return (grad_entry[None], grad_exit[None], leaving[None])


def solution(mesh):
    spread = P("depth", None, "rows", None)
    return jax.shard_map(
        per_device,
        mesh=mesh,
        in_specs=(spread, P(None, "rows", None), spread, spread, spread, spread, P("depth", None)),
        out_specs=(spread, spread, spread),
        check_vma=False,
    )
```

time: 147 us -> 99.9 us (0.68)
  waiting for transfers between devices: 71.8 us -> 28.3 us
  blocking collectives: 0 us -> 36.5 us
  starting transfers between devices: 50.4 us -> 14.5 us
  Pallas kernels: 13 us -> 7.72 us
  local copies, waits for them, and re-layouts: 5.22 us -> 6.86 us
    all_to_all x8 -> x2, waiting for transfers between devices: 71.8 us -> 27.2 us  [exchange(): lax.all_to_all(packed, 'rows', split_axis=0, concat_axis=0, tiled=True)]
    all_to_all x0 -> x1, blocking collectives: none -> 36.5 us  [exchange(): lax.all_to_all(packed, 'rows', split_axis=0, concat_axis=0, tiled=True)]
    all_to_all x8 -> x2, starting transfers between devices: 39.1 us -> 8.9 us  [exchange(): lax.all_to_all(packed, 'rows', split_axis=0, concat_axis=0, tiled=True)]
    ppermute x2 -> x1, starting transfers between devices: 11.3 us -> 5.57 us  [to_previous(): lax.ppermute(value, 'depth', [(s, (s - 1) % count) for s in range(count)])]
    pallas_call x11 -> x4, Pallas kernels: 13 us -> 7.72 us  [call(): pl.pallas_call(kernel, out_shape=out_shape, in_specs=[SCALAR] * scalars +...]
    unnamed x20 -> x14, local copies, waits for them, and re-layouts: 4.49 us -> 6.13 us
  transfers between devices with their start and end apart: 10 -> 3, of which waited for: 8 -> 3; matrix products, arithmetic and copies ran while one was open for 1% -> 1% of each run, Pallas kernels for 6% -> 1%
where the time goes in v2:
time: 99.9 us; the launch traced here: 99.3 us
  blocking collectives  36.5 us (37%)
  waiting for transfers between devices  28.3 us (28%)
  starting transfers between devices  14.5 us (15%)
  Pallas kernels  7.72 us (8%)
  local copies, waits for them, and re-layouts  6.86 us (7%)
  between operations  4.68 us (5%)
    all_to_all x1, blocking collectives, exchange(): lax.all_to_all(packed, 'rows', split_axis=0, concat_axis=0, tiled=True)  36.5 us
    all_to_all x2, waiting for transfers between devices, exchange(): lax.all_to_all(packed, 'rows', split_axis=0, concat_axis=0, tiled=True)  27.2 us
    all_to_all x2, starting transfers between devices, exchange(): lax.all_to_all(packed, 'rows', split_axis=0, concat_axis=0, tiled=True)  8.9 us
    pallas_call x4, Pallas kernels, call(): pl.pallas_call(kernel, out_shape=out_shape, in_specs=[SCALAR] * scalars +...  7.72 us
    unnamed x14, local copies, waits for them, and re-layouts  6.13 us
    ppermute x1, starting transfers between devices, to_previous(): lax.ppermute(value, 'depth', [(s, (s - 1) % count) for s in range(count)])  5.57 us
  transfers between devices with their start and end apart: 3, of which 3 were waited for; matrix products, arithmetic and copies ran while one was open for 1% of the time, Pallas kernels for 1%

profile of v2, /device:TPU:1, one launch (start us, length us, event | category | flops | bytes accessed | tf_op | source)
XLA Modules:
  0.0 99.3 jit_solution(16025267057119840902)
XLA Ops:
  0.6 1.2 %copy-done.3 = f32[1,2,64,2048]{3,2,1,0:T(8,128)S(1)} copy-done((f32[1,2,64,2048]{3,2,1,0:T(8,128)S(1)}, f32[1,2,64,2048]{3,2,1,0:T(8,128)}, u32[]{:S(2)}) %copy-start.3) | copy-done | bytes 1048600
  1.9 1.2 %copy-done.4 = f32[1,2,64,2048]{3,2,1,0:T(8,128)S(1)} copy-done((f32[1,2,64,2048]{3,2,1,0:T(8,128)S(1)}, f32[1,2,64,2048]{3,2,1,0:T(8,128)}, u32[]{:S(2)}) %copy-start.4) | copy-done | bytes 1048600
  3.1 1.2 %copy-done.5 = f32[2,64,2048]{2,1,0:T(8,128)S(1)} copy-done((f32[2,64,2048]{2,1,0:T(8,128)S(1)}, f32[2,64,2048]{2,1,0:T(8,128)}, u32[]{:S(2)}) %copy-start.5) | copy-done | bytes 1048600
  4.3 1.4 %enter.1 = f32[32,2,2,32,128]{4,3,2,1,0:T(8,128)S(1)} custom-call(s32[1]{0:T(128)} %bitcast.4.first_ref, f32[2,64,2048]{2,1,0:T(8,128)S(1)} %bitcast.18, f32[2,64,2048]{2,1,0:T(8,128)S(1)} %bitcast.19, f32[2,64,2048]{2,1,0:T(8,128)S(1)} %copy-done.5), custom_call_target="tpu_custom_call" | custom-call | flops 104857680 | bytes 5242884 | tf_op jit(solution)/shard_map/enter/pallas_call | solution.py:324
  5.7 36.5 %all_to_all.15.in_ref = f32[32,2,2,32,128]{4,3,2,1,0:T(8,128)S(1)} all-to-all(f32[32,2,2,32,128]{4,3,2,1,0:T(8,128)S(1)} %enter.1), channel_id=1, replica_groups=mesh['depth'=8,'rows'=32] {'rows'}, dimensions={0} | all-to-all | bytes 4194304 | tf_op jit(solution)/shard_map/all_to_all | solution.py:337
  42.3 2.4 %columns.1 = (f32[32,2,32,128]{3,2,1,0:T(8,128)}, f32[32,2,32,128]{3,2,1,0:T(8,128)S(1)}) custom-call(s32[1]{0:T(128)} %bitcast.4.first_ref, f32[32,2,2,32,128]{4,3,2,1,0:T(8,128)S(1)} %all_to_all.15.in_ref), custom_call_target="tpu_custom_call" | custom-call | flops 83886160 | bytes 4194308 | tf_op jit(solution)/shard_map/columns/pallas_call | solution.py:324
  44.6 5.6 %collective-permute-start = (f32[32,2,32,128]{3,2,1,0:T(8,128)S(1)}, f32[32,2,32,128]{3,2,1,0:T(8,128)}, u32[]{:S(2)}, u32[]{:S(2)}) collective-permute-start(f32[32,2,32,128]{3,2,1,0:T(8,128)S(1)} %get-tuple-element.8), channel_id=1, source_target_pairs={{0,224},{32,0},{64,32},{96,64},{128,96},{160,128},{192,160},{224,1... | collective-permute-start | bytes 3145736 | tf_op jit(solution)/shard_map/ppermute | solution.py:342
  50.2 4.4 %all-to-all-start.1 = ((f32[32,2,32,128]{3,2,1,0:T(8,128)}), f32[32,2,32,128]{3,2,1,0:T(8,128)S(1)}, u32[]{:S(2)}, u32[]{:S(2)}) async-start(f32[32,2,32,128]{3,2,1,0:T(8,128)} %get-tuple-element.7), calls=%async_computation.1 | async-start | bytes 2097152 | tf_op jit(solution)/shard_map/all_to_all | solution.py:337
  54.6 0.6 fusion.20
  59.1 0.1 fusion.16
  59.2 0.1 fusion.18
  59.2 12.3 %all-to-all-done.1.wave_ref = f32[32,2,32,128]{3,2,1,0:T(8,128)S(1)} async-done(((f32[32,2,32,128]{3,2,1,0:T(8,128)}), f32[32,2,32,128]{3,2,1,0:T(8,128)S(1)}, u32[]{:S(2)}, u32[]{:S(2)}) %all-to-all-start.1) | async-done | bytes 1048608 | tf_op jit(solution)/shard_map/all_to_all | solution.py:337
  71.5 1.1 %collective-permute-done = f32[32,2,32,128]{3,2,1,0:T(8,128)} collective-permute-done((f32[32,2,32,128]{3,2,1,0:T(8,128)S(1)}, f32[32,2,32,128]{3,2,1,0:T(8,128)}, u32[]{:S(2)}, u32[]{:S(2)}) %collective-permute-start) | collective-permute-done | bytes 1048608 | tf_op jit(solution)/shard_map/ppermute | solution.py:342
  72.6 4.5 %all-to-all-start.2 = ((f32[32,2,32,128]{3,2,1,0:T(8,128)}), f32[32,2,32,128]{3,2,1,0:T(8,128)S(1)}, u32[]{:S(2)}, u32[]{:S(2)}) async-start(f32[32,2,32,128]{3,2,1,0:T(8,128)} %collective-permute-done), calls=%async_computation.2 | async-start | bytes 2097152 | tf_op jit(solution)/shard_map/all_to_all | solution.py:337
  77.2 0.3 fusion.6
  77.5 0.3 fusion.8
  77.8 0.1 broadcast_in_dim.10.lit_y_ref
  77.9 0.0 copy-done
  77.9 1.3 %entry.1 = f32[2,64,2048]{2,1,0:T(8,128)} custom-call(f32[2,2048]{1,0:T(2,128)S(1)} %pad_maximum_fusion.lit_x_ref, f32[2,64,128]{2,1,0:T(8,128)S(1)} %broadcast_in_dim.10.lit_y_ref, f32[2,64,2048]{2,1,0:T(8,128)S(1)} %bitcast.15, f32[32,2,32,128]{3,2,1,0:T(8,128)S(1)} %all-to-all-done.1.wave_ref), custom_call_target="tpu_custom_call" | custom-call | flops 64552960 | bytes 3227648 | tf_op jit(solution)/shard_map/entry/pallas_call | solution.py:324
  79.2 14.9 %all-to-all-done.2.in_ref = f32[32,2,32,128]{3,2,1,0:T(8,128)S(1)} async-done(((f32[32,2,32,128]{3,2,1,0:T(8,128)}), f32[32,2,32,128]{3,2,1,0:T(8,128)S(1)}, u32[]{:S(2)}, u32[]{:S(2)}) %all-to-all-start.2) | async-done | bytes 1048608 | tf_op jit(solution)/shard_map/all_to_all | solution.py:337
  94.2 0.1 broadcast_in_dim.23.lit_y_ref
  94.2 1.2 %copy-done.1 = f32[1,2,64,2048]{3,2,1,0:T(8,128)S(1)} copy-done((f32[1,2,64,2048]{3,2,1,0:T(8,128)S(1)}, f32[1,2,64,2048]{3,2,1,0:T(8,128)}, u32[]{:S(2)}) %copy-start.1) | copy-done | bytes 1048600
  95.5 1.2 %copy-done.2 = f32[1,2,64,2048]{3,2,1,0:T(8,128)S(1)} copy-done((f32[1,2,64,2048]{3,2,1,0:T(8,128)S(1)}, f32[1,2,64,2048]{3,2,1,0:T(8,128)}, u32[]{:S(2)}) %copy-start.2) | copy-done | bytes 1048600
  96.7 2.6 %exit.1 = (f32[2,64,2048]{2,1,0:T(8,128)}, f32[2,64,2048]{2,1,0:T(8,128)}) custom-call(f32[2,2048]{1,0:T(2,128)S(1)} %pad_maximum_fusion.1.lit_x_ref, f32[2,64,128]{2,1,0:T(8,128)S(1)} %broadcast_in_dim.23.lit_y_ref, f32[2,64,2048]{2,1,0:T(8,128)S(1)} %bitcast.16, f32[2,64,2048]{2,1,0:T(8,128)S(1)} %bitcast.17, f32[32,2,32,128]{3,2,1,0:T(8,128)S(1)} %all-to-all-done.2.in_ref), custom_call_target="tpu_custom_call" | custom-call | flops 106496000 | bytes 5324800 | tf_op jit(solution)/shard_map/exit/pallas_call | solution.py:324
  (12 shorter events, 0.1 us)
Async XLA Ops:
  0.6 1.2 %copy-start.3 = (f32[1,2,64,2048]{3,2,1,0:T(8,128)S(1)}, f32[1,2,64,2048]{3,2,1,0:T(8,128)}, u32[]{:S(2)}) copy-start(f32[1,2,64,2048]{3,2,1,0:T(8,128)} %param.7) | copy-start | bytes 3145732
  1.9 1.2 %copy-start.4 = (f32[1,2,64,2048]{3,2,1,0:T(8,128)S(1)}, f32[1,2,64,2048]{3,2,1,0:T(8,128)}, u32[]{:S(2)}) copy-start(f32[1,2,64,2048]{3,2,1,0:T(8,128)} %param.9) | copy-start | bytes 3145732
  3.1 1.2 %copy-start.5 = (f32[2,64,2048]{2,1,0:T(8,128)S(1)}, f32[2,64,2048]{2,1,0:T(8,128)}, u32[]{:S(2)}) copy-start(f32[2,64,2048]{2,1,0:T(8,128)} %loss_ref.1) | copy-start | bytes 3145732
  42.3 12.3 %copy-start.6 = (s32[1,2]{1,0:T(1,128)S(1)}, s32[1,2]{1,0:T(1,128)}, u32[]{:S(2)}) copy-start(s32[1,2]{1,0:T(1,128)} %param.13) | copy-start | bytes 28
  44.6 28.0 %collective-permute-start = (f32[32,2,32,128]{3,2,1,0:T(8,128)S(1)}, f32[32,2,32,128]{3,2,1,0:T(8,128)}, u32[]{:S(2)}, u32[]{:S(2)}) collective-permute-start(f32[32,2,32,128]{3,2,1,0:T(8,128)S(1)} %get-tuple-element.8), channel_id=1, source_target_pairs={{0,224},{32,0},{64,32},{96,64},{128,96},{160,128},{192,160},{224,1... | collective-permute-start | bytes 3145736 | tf_op jit(solution)/shard_map/ppermute | solution.py:342
  50.2 27.7 %copy-start = (f32[1,2,64,2048]{3,2,1,0:T(8,128)S(1)}, f32[1,2,64,2048]{3,2,1,0:T(8,128)}, u32[]{:S(2)}) copy-start(f32[1,2,64,2048]{3,2,1,0:T(8,128)} %param.11) | copy-start | bytes 3145732
  50.2 21.3 %all-to-all-start.1 = ((f32[32,2,32,128]{3,2,1,0:T(8,128)}), f32[32,2,32,128]{3,2,1,0:T(8,128)S(1)}, u32[]{:S(2)}, u32[]{:S(2)}) async-start(f32[32,2,32,128]{3,2,1,0:T(8,128)} %get-tuple-element.7), calls=%async_computation.1 | async-start | bytes 2097152 | tf_op jit(solution)/shard_map/all_to_all | solution.py:337
  72.6 21.5 %all-to-all-start.2 = ((f32[32,2,32,128]{3,2,1,0:T(8,128)}), f32[32,2,32,128]{3,2,1,0:T(8,128)S(1)}, u32[]{:S(2)}, u32[]{:S(2)}) async-start(f32[32,2,32,128]{3,2,1,0:T(8,128)} %collective-permute-done), calls=%async_computation.2 | async-start | bytes 2097152 | tf_op jit(solution)/shard_map/all_to_all | solution.py:337
  94.2 1.2 %copy-start.1 = (f32[1,2,64,2048]{3,2,1,0:T(8,128)S(1)}, f32[1,2,64,2048]{3,2,1,0:T(8,128)}, u32[]{:S(2)}) copy-start(f32[1,2,64,2048]{3,2,1,0:T(8,128)} %param.12) | copy-start | bytes 3145732
  95.5 1.2 %copy-start.2 = (f32[1,2,64,2048]{3,2,1,0:T(8,128)S(1)}, f32[1,2,64,2048]{3,2,1,0:T(8,128)}, u32[]{:S(2)}) copy-start(f32[1,2,64,2048]{3,2,1,0:T(8,128)} %param.10) | copy-start | bytes 3145732

commit v3 on v2

--- a/solution.py
+++ b/solution.py
@@ -17,7 +17,7 @@
 LANES = 2 * WIDTH
 HALF = WIDTH // 2
 TILES = HALF // 8
-VMEM_LIMIT = 24 * 1024 * 1024
+VMEM_LIMIT = 16 * 1024 * 1024
 
 INVERSE = pow(SPREAD, -1, N)
 _k = np.arange(N, dtype=np.int64)
@@ -208,7 +208,7 @@
                 write(index, 2 * pair + side, value)
 
 
-def enter_kernel(first_ref, field_ref, t_ref, loss_ref, out_ref, packed, stage, moved):
+def enter_kernel(field_ref, other_ref, out_ref, packed, stage, moved):
     read_field(field_ref, lambda index, block, value: put(packed, block, tile(index), value))
     along_lanes(
         lambda index, block: get(packed, block, tile(index)),
@@ -216,21 +216,13 @@
         stage,
         moved,
     )
-
-    def other(index, block, value):
-        put(out_ref.at[:, 1], block, tile(index), value)
-
-    @pl.when(first_ref[0] == 1)
-    def _():
-        read_field(loss_ref, other)
-
-    @pl.when(first_ref[0] != 1)
-    def _():
-        read_field(t_ref, other)
-
-
-def column_kernel(first_ref, in_ref, wave_ref, out_ref, stage, held):
-    use_loss = first_ref[0] == 1
+    read_field(
+        other_ref, lambda index, block, value: put(out_ref.at[:, 1], block, tile(index), value)
+    )
+
+
+def column_kernel(info_ref, in_ref, wave_ref, out_ref, stage, held):
+    use_loss = info_ref[1] == 1
     along_rows(
         lambda index, block: get(in_ref.at[:, 0], block, tile(index)),
         lambda index, block, value: put(wave_ref, block, tile(index), value),
@@ -254,21 +246,52 @@
     )
 
 
-def write_products(wave, lit_x_ref, lit_y_ref, field_ref, out_ref, t_ref=None, plain_ref=None):
+def light_tables():
+    shifts = np.arange(LED_SIDE) - LED_SIDE // 2
+    along_x = np.exp(2j * np.pi * (shifts[:, None] * np.arange(N) % N) / N)
+    along_y = np.zeros((WIDTH, LANES), np.complex128)
+    along_y[:, :LED_SIDE] = np.exp(2j * np.pi * (np.arange(WIDTH)[:, None] * shifts % N) / N)
+    turns = np.exp(2j * np.pi * np.arange(BLOCKS) / BLOCKS)
+    return (
+        np.concatenate([along_x.real, along_x.imag]).reshape(-1, N // LANES, LANES).astype(np.float32),
+        np.stack([along_y.real, along_y.imag]).astype(np.float32),
+        np.stack([turns.real, turns.imag]).astype(np.float32),
+    )
+
+
+def write_products(
+    tick, led_ref, info_ref, turn_ref, lit_x_ref, lit_y_ref, wave, field_ref, out_ref, *plain
+):
+    led = led_ref[0, tick]
+    column_shift = led // LED_SIDE
+    row_shift = led - column_shift * LED_SIDE
+    turn = (info_ref[0] * (row_shift - LED_SIDE // 2)) & (BLOCKS - 1)
+    turn_real, turn_imag = turn_ref[0, turn], turn_ref[1, turn]
+    chosen = lane_ids() == row_shift
+
+    def lit_rows(rows):
+        pair = tuple(
+            jnp.sum(jnp.where(chosen, lit_y_ref[part, rows, :], 0.0), axis=1, keepdims=True)
+            for part in range(2)
+        )
+        pair = tuple(jnp.broadcast_to(v, (8, LANES)) for v in pair)
+        return times(pair, turn_real, turn_imag)
+
     for index in range(TILES):
-        lit_y = [
-            (lit_y_ref[0, natural(index, half), :], lit_y_ref[1, natural(index, half), :])
-            for half in range(2)
-        ]
+        lit_y = [lit_rows(natural(index, half)) for half in range(2)]
         for pair in range(BLOCKS // 2):
             cols = pl.ds(pair * LANES, LANES)
             left, right = wave(index, 2 * pair), wave(index, 2 * pair + 1)
             reals, imags = halves(left[0], right[0]), halves(left[1], right[1])
-            lit_x = (lit_x_ref[0:1, cols], lit_x_ref[1:2, cols])
+            lit_x = (
+                lit_x_ref[column_shift, pair : pair + 1, :],
+                lit_x_ref[column_shift + LED_SIDE, pair : pair + 1, :],
+            )
             for half in range(2):
                 rows = natural(index, half)
                 real, imag = reals[half], imags[half]
-                if t_ref is not None:
+                if plain:
+                    t_ref, plain_ref = plain
                     t_real, t_imag = t_ref[0, rows, cols], t_ref[1, rows, cols]
                     plain_ref[0, rows, cols] = real * t_real + imag * t_imag
                     plain_ref[1, rows, cols] = imag * t_real - real * t_imag
@@ -278,18 +301,34 @@
                 out_ref[1, rows, cols] = imag * f_real - real * f_imag
 
 
-def entry_kernel(lit_x_ref, lit_y_ref, field_ref, wave_ref, out_ref):
+def entry_kernel(led_ref, info_ref, turn_ref, lit_x_ref, lit_y_ref, field_ref, wave_ref, out_ref):
     write_products(
-        lambda index, block: get(wave_ref, block, tile(index)),
+        0,
+        led_ref,
+        info_ref,
+        turn_ref,
         lit_x_ref,
         lit_y_ref,
+        lambda index, block: get(wave_ref, block, tile(index)),
         field_ref,
         out_ref,
     )
 
 
 def exit_kernel(
-    lit_x_ref, lit_y_ref, field_ref, t_ref, in_ref, out_ref, plain_ref, packed, stage, moved
+    led_ref,
+    info_ref,
+    turn_ref,
+    lit_x_ref,
+    lit_y_ref,
+    field_ref,
+    t_ref,
+    in_ref,
+    out_ref,
+    plain_ref,
+    packed,
+    stage,
+    moved,
 ):
     along_lanes(
         lambda index, block: get(in_ref, block, tile(index)),
@@ -298,9 +337,13 @@
         moved,
     )
     write_products(
-        lambda index, block: get(packed, block, tile(index)),
+        1,
+        led_ref,
+        info_ref,
+        turn_ref,
         lit_x_ref,
         lit_y_ref,
+        lambda index, block: get(packed, block, tile(index)),
         field_ref,
         out_ref,
         t_ref,
@@ -342,51 +385,32 @@
     return lax.ppermute(value, "depth", [(s, (s - 1) % count) for s in range(count)])
 
 
-def light(led_number, row_start):
-    shift_col = led_number // LED_SIDE - LED_SIDE // 2
-    shift_row = led_number % LED_SIDE - LED_SIDE // 2
-    cols = shift_col * jnp.arange(N, dtype=jnp.int32) % N
-    rows = shift_row * (row_start + jnp.arange(WIDTH, dtype=jnp.int32)) % N
-    angle_x = 2.0 * math.pi / N * cols.astype(jnp.float32)
-    angle_y = 2.0 * math.pi / N * rows.astype(jnp.float32)
-    lit_x = jnp.stack([jnp.cos(angle_x), jnp.sin(angle_x)])
-    lit_y = jnp.stack([jnp.cos(angle_y), jnp.sin(angle_y)])
-    return lit_x, jnp.broadcast_to(lit_y[:, :, None], (2, WIDTH, LANES))
-
-
 def per_device(grad_arriving, loss_grad, t_entry, t_exit, fields_entry, fields_exit, led_index):
-    row_start = lax.axis_index("rows") * WIDTH
-    first = (lax.axis_index("depth") == 0).astype(jnp.int32).reshape(1)
+    first = (lax.axis_index("depth") == 0).astype(jnp.int32)
+    info = jnp.stack([lax.axis_index("rows"), first]).astype(jnp.int32)
+    lit_x, lit_y, turns = (jnp.asarray(table) for table in light_tables())
+    lights = [led_index, info, turns, lit_x, lit_y]
     both = call(
         enter_kernel,
         BOTH,
-        [first, grad_arriving[0], t_entry[0], loss_grad],
+        [grad_arriving[0], jnp.where(first == 1, loss_grad, t_entry[0])],
         "enter",
         [BUFFER, BUFFER, BUFFER],
-        1,
     )
     wave, onward = call(
-        column_kernel, (PACKED, PACKED), [first, exchange(both)], "columns", [BUFFER, HELD], 1
+        column_kernel, (PACKED, PACKED), [info, exchange(both)], "columns", [BUFFER, HELD], 1
     )
     onward = to_previous(onward)
     wave = exchange(wave)
-    grad_entry = call(
-        entry_kernel,
-        FIELD,
-        [*light(led_index[0, 0], row_start), fields_entry[0], wave],
-        "entry",
-    )
+    grad_entry = call(entry_kernel, FIELD, [*lights, fields_entry[0], wave], "entry", scalars=3)
+    onward, grad_entry = lax.optimization_barrier((onward, grad_entry))
     grad_exit, leaving = call(
         exit_kernel,
         (FIELD, FIELD),
-        [
-            *light(led_index[0, 1], row_start),
-            fields_exit[0],
-            t_exit[0],
-            exchange(onward),
-        ],
+        [*lights, fields_exit[0], t_exit[0], exchange(onward)],
         "exit",
         [BUFFER, BUFFER, BUFFER],
+        3,
     )
     return (grad_entry[None], grad_exit[None], leaving[None])
 

time: 99.9 us -> 96.7 us (0.968)
  local copies, waits for them, and re-layouts: 6.86 us -> 1.42 us
  blocking collectives: 36.5 us -> 41.5 us
  between operations: 4.68 us -> 0.75 us
  Pallas kernels: 7.72 us -> 8.87 us
  other arithmetic: 0.72 us -> 1.84 us
    all_to_all x1 -> x2, blocking collectives: 36.5 us -> 41.5 us  [exchange(): lax.all_to_all(packed, 'rows', split_axis=0, concat_axis=0, tiled=True)]
    unnamed x14 -> x18, local copies, waits for them, and re-layouts: 6.13 us -> 1.42 us
    select_n x0 -> x1, other arithmetic: none -> 1.76 us  [per_device(): jnp.where(first == 1, loss_grad, t_entry[0])]
    pallas_call x4, Pallas kernels: 7.72 us -> 8.87 us  [call(): pl.pallas_call(kernel, out_shape=out_shape, in_specs=[SCALAR] * scalars +...]
    ppermute x1, waiting for transfers between devices: 1.13 us -> 0.01 us  [to_previous(): lax.ppermute(value, 'depth', [(s, (s - 1) % count) for s in range(count)])]
    all_to_all x2 -> x1, waiting for transfers between devices: 27.2 us -> 28.2 us  [exchange(): lax.all_to_all(packed, 'rows', split_axis=0, concat_axis=0, tiled=True)]
    all_to_all x2 -> x1, starting transfers between devices: 8.9 us -> 8.59 us  [exchange(): lax.all_to_all(packed, 'rows', split_axis=0, concat_axis=0, tiled=True)]
  transfers between devices with their start and end apart: 3 -> 2, of which waited for: 3 -> 1; matrix products, arithmetic and copies ran while one was open for 1% -> 0% of each run, Pallas kernels for 1% -> 2%
where the time goes in v3:
time: 96.7 us; the launch traced here: 96.5 us
  blocking collectives  41.5 us (43%)
  waiting for transfers between devices  28.2 us (29%)
  starting transfers between devices  13.9 us (14%)
  Pallas kernels  8.87 us (9%)
  other arithmetic  1.84 us (2%)
  local copies, waits for them, and re-layouts  1.42 us (1%)
    all_to_all x2, blocking collectives, exchange(): lax.all_to_all(packed, 'rows', split_axis=0, concat_axis=0, tiled=True)  41.5 us
    all_to_all x1, waiting for transfers between devices, exchange(): lax.all_to_all(packed, 'rows', split_axis=0, concat_axis=0, tiled=True)  28.2 us
    pallas_call x4, Pallas kernels, call(): pl.pallas_call(kernel, out_shape=out_shape, in_specs=[SCALAR] * scalars +...  8.87 us
    all_to_all x1, starting transfers between devices, exchange(): lax.all_to_all(packed, 'rows', split_axis=0, concat_axis=0, tiled=True)  8.59 us
    ppermute x1, starting transfers between devices, to_previous(): lax.ppermute(value, 'depth', [(s, (s - 1) % count) for s in range(count)])  5.34 us
  transfers between devices with their start and end apart: 2, of which 1 were waited for; matrix products, arithmetic and copies ran while one was open for 0% of the time, Pallas kernels for 2%

profile of v3, /device:TPU:1, one launch (start us, length us, event | category | flops | bytes accessed | tf_op | source)
XLA Modules:
  0.0 96.5 jit_solution(6219878502988410474)
XLA Ops:
  0.6 0.0 copy-start.4
  0.7 1.8 %bitcast_select_fusion.other_ref = f32[2,64,2048]{2,1,0:T(8,128)S(1)} fusion(f32[2,64,2048]{2,1,0:T(8,128)} %param.11, f32[1,2,64,2048]{3,2,1,0:T(8,128)} %param.12, pred[]{:T(512)S(6)} %eq.7), kind=kLoop, calls=%fused_computation | loop fusion | flops 262144 | bytes 3145729 | tf_op jit(solution)/shard_map/jit(_where)/select_n | solution.py:396
  2.4 0.1 copy-done.4
  2.5 1.3 %enter.1 = f32[32,2,2,32,128]{4,3,2,1,0:T(8,128)S(1)} custom-call(f32[2,64,2048]{2,1,0:T(8,128)S(1)} %bitcast.14, f32[2,64,2048]{2,1,0:T(8,128)S(1)} %bitcast_select_fusion.other_ref), custom_call_target="tpu_custom_call" | custom-call | flops 83886080 | bytes 4194304 | tf_op jit(solution)/shard_map/enter/pallas_call | solution.py:367
  3.8 0.0 copy-start
  3.8 1.3 %copy-done = f32[32,2,2,32,128]{4,3,2,1,0:T(8,128)} copy-done((f32[32,2,2,32,128]{4,3,2,1,0:T(8,128)}, f32[32,2,2,32,128]{4,3,2,1,0:T(8,128)S(1)}, u32[]{:S(2)}) %copy-start) | copy-done | bytes 2097176
  5.1 8.6 %all-to-all-start = ((f32[32,2,2,32,128]{4,3,2,1,0:T(8,128)}), f32[32,2,2,32,128]{4,3,2,1,0:T(8,128)S(1)}, u32[]{:S(2)}, u32[]{:S(2)}) async-start(f32[32,2,2,32,128]{4,3,2,1,0:T(8,128)} %copy-done), calls=%async_computation | async-start | bytes 4194304 | tf_op jit(solution)/shard_map/all_to_all | solution.py:380
  13.7 0.1 pad_add_fusion.info_ref
  13.8 0.0 copy-start.8
  13.8 28.2 %all-to-all-done.in_ref = f32[32,2,2,32,128]{4,3,2,1,0:T(8,128)S(1)} async-done(((f32[32,2,2,32,128]{4,3,2,1,0:T(8,128)}), f32[32,2,2,32,128]{4,3,2,1,0:T(8,128)S(1)}, u32[]{:S(2)}, u32[]{:S(2)}) %all-to-all-start) | async-done | bytes 2097184 | tf_op jit(solution)/shard_map/all_to_all | solution.py:380
  42.0 2.4 %columns.1 = (f32[32,2,32,128]{3,2,1,0:T(8,128)S(1)}, f32[32,2,32,128]{3,2,1,0:T(8,128)S(1)}) custom-call(s32[2]{0:T(128)S(1)} %pad_add_fusion.info_ref, f32[32,2,2,32,128]{4,3,2,1,0:T(8,128)S(1)} %all-to-all-done.in_ref), custom_call_target="tpu_custom_call" | custom-call | flops 83886240 | bytes 4194312 | tf_op jit(solution)/shard_map/columns/pallas_call | solution.py:367
  44.4 5.3 %collective-permute-start = (f32[32,2,32,128]{3,2,1,0:T(8,128)S(1)}, f32[32,2,32,128]{3,2,1,0:T(8,128)S(1)}, u32[]{:S(2)}, u32[]{:S(2)}) collective-permute-start(f32[32,2,32,128]{3,2,1,0:T(8,128)S(1)} %get-tuple-element.9), channel_id=1, source_target_pairs={{0,224},{32,0},{64,32},{96,64},{128,96},{160,128},{192,160},{224,1... | collective-permute-start | bytes 3145736 | tf_op jit(solution)/shard_map/ppermute | solution.py:385
  49.7 20.8 %all_to_all.15.wave_ref = f32[32,2,32,128]{3,2,1,0:T(8,128)S(1)} all-to-all(f32[32,2,32,128]{3,2,1,0:T(8,128)S(1)} %get-tuple-element.10), channel_id=1, replica_groups=mesh['depth'=8,'rows'=32] {'rows'}, dimensions={0} | all-to-all | bytes 2097152 | tf_op jit(solution)/shard_map/all_to_all | solution.py:380
  70.6 0.0 copy-done.1
  70.6 0.0 copy-done.5
  70.6 0.0 copy-done.6
  70.6 0.0 copy-done.7
  70.6 0.0 copy-start.2
  70.6 0.0 copy-start.3
  70.6 2.0 %entry.1 = f32[2,64,2048]{2,1,0:T(8,128)} custom-call(s32[1,2]{1,0:T(1,128)S(1)} %copy-done.8, s32[2]{0:T(128)S(1)} %pad_add_fusion.info_ref, f32[2,32]{1,0:T(2,128)S(1)} %copy-done.7, f32[30,16,128]{2,1,0:T(8,128)S(1)} %copy-done.5, f32[2,64,128]{2,1,0:T(8,128)S(1)} %copy-done.6, f32[2,64,2048]{2,1,0:T(8,128)S(1)} %bitcast.11, ...), custom_call_target="tpu_custom_call" | custom-call | flops 69145920 | bytes 3457296 | tf_op jit(solution)/shard_map/entry/pallas_call | solution.py:367
  72.6 0.0 collective-permute-done
  72.6 20.7 %all_to_all.16.in_ref = f32[32,2,32,128]{3,2,1,0:T(8,128)S(1)} all-to-all(f32[32,2,32,128]{3,2,1,0:T(8,128)S(1)} %collective-permute-done), channel_id=1, replica_groups=mesh['depth'=8,'rows'=32] {'rows'}, dimensions={0} | all-to-all | bytes 2097152 | tf_op jit(solution)/shard_map/all_to_all | solution.py:380
  93.3 0.0 copy-done.2
  93.3 3.2 %exit.1 = (f32[2,64,2048]{2,1,0:T(8,128)}, f32[2,64,2048]{2,1,0:T(8,128)}) custom-call(s32[1,2]{1,0:T(1,128)S(1)} %copy-done.8, s32[2]{0:T(128)S(1)} %pad_add_fusion.info_ref, f32[2,32]{1,0:T(2,128)S(1)} %copy-done.7, f32[30,16,128]{2,1,0:T(8,128)S(1)} %copy-done.5, f32[2,64,128]{2,1,0:T(8,128)S(1)} %copy-done.6, f32[2,64,2048]{2,1,0:T(8,128)S(1)} %bitcast.12, ...), custom_call_target="tpu_custom_call" | custom-call | flops 111088960 | bytes 5554448 | tf_op jit(solution)/shard_map/exit/pallas_call | solution.py:367
  (6 shorter events, 0.0 us)
Async XLA Ops:
  0.6 1.9 %copy-start.4 = (f32[1,2,64,2048]{3,2,1,0:T(8,128)S(1)}, f32[1,2,64,2048]{3,2,1,0:T(8,128)}, u32[]{:S(2)}) copy-start(f32[1,2,64,2048]{3,2,1,0:T(8,128)} %param.10) | copy-start | bytes 3145732
  3.8 1.3 %copy-start = (f32[32,2,2,32,128]{4,3,2,1,0:T(8,128)}, f32[32,2,2,32,128]{4,3,2,1,0:T(8,128)S(1)}, u32[]{:S(2)}) copy-start(f32[32,2,2,32,128]{4,3,2,1,0:T(8,128)S(1)} %enter.1) | copy-start | bytes 6291460
  5.1 36.9 %all-to-all-start = ((f32[32,2,2,32,128]{4,3,2,1,0:T(8,128)}), f32[32,2,2,32,128]{4,3,2,1,0:T(8,128)S(1)}, u32[]{:S(2)}, u32[]{:S(2)}) async-start(f32[32,2,2,32,128]{4,3,2,1,0:T(8,128)} %copy-done), calls=%async_computation | async-start | bytes 4194304 | tf_op jit(solution)/shard_map/all_to_all | solution.py:380
  13.8 56.8 %copy-start.1 = (f32[1,2,64,2048]{3,2,1,0:T(8,128)S(1)}, f32[1,2,64,2048]{3,2,1,0:T(8,128)}, u32[]{:S(2)}) copy-start(f32[1,2,64,2048]{3,2,1,0:T(8,128)} %param.14) | copy-start | bytes 3145732
  13.8 56.8 %copy-start.5 = (f32[30,16,128]{2,1,0:T(8,128)S(1)}, f32[30,16,128]{2,1,0:T(8,128)}, u32[]{:S(2)}) copy-start(f32[30,16,128]{2,1,0:T(8,128)} %constant.19.clone.lit_x_ref) | copy-start | bytes 737284
  13.8 56.8 %copy-start.6 = (f32[2,64,128]{2,1,0:T(8,128)S(1)}, f32[2,64,128]{2,1,0:T(8,128)}, u32[]{:S(2)}) copy-start(f32[2,64,128]{2,1,0:T(8,128)} %constant.20.clone.lit_y_ref) | copy-start | bytes 196612
  13.8 56.8 %copy-start.7 = (f32[2,32]{1,0:T(2,128)S(1)}, f32[2,32]{1,0:T(2,128)}, u32[]{:S(2)}) copy-start(f32[2,32]{1,0:T(2,128)} %constant.21.clone.turn_ref) | copy-start | bytes 772
  13.8 56.8 %copy-start.8 = (s32[1,2]{1,0:T(1,128)S(1)}, s32[1,2]{1,0:T(1,128)}, u32[]{:S(2)}) copy-start(s32[1,2]{1,0:T(1,128)} %led_ref.3) | copy-start | bytes 28
  44.4 28.2 %collective-permute-start = (f32[32,2,32,128]{3,2,1,0:T(8,128)S(1)}, f32[32,2,32,128]{3,2,1,0:T(8,128)S(1)}, u32[]{:S(2)}, u32[]{:S(2)}) collective-permute-start(f32[32,2,32,128]{3,2,1,0:T(8,128)S(1)} %get-tuple-element.9), channel_id=1, source_target_pairs={{0,224},{32,0},{64,32},{96,64},{128,96},{160,128},{192,160},{224,1... | collective-permute-start | bytes 3145736 | tf_op jit(solution)/shard_map/ppermute | solution.py:385
  70.6 22.7 %copy-start.2 = (f32[1,2,64,2048]{3,2,1,0:T(8,128)S(1)}, f32[1,2,64,2048]{3,2,1,0:T(8,128)}, u32[]{:S(2)}) copy-start(f32[1,2,64,2048]{3,2,1,0:T(8,128)} %param.15) | copy-start | bytes 3145732
  70.6 22.7 %copy-start.3 = (f32[1,2,64,2048]{3,2,1,0:T(8,128)S(1)}, f32[1,2,64,2048]{3,2,1,0:T(8,128)}, u32[]{:S(2)}) copy-start(f32[1,2,64,2048]{3,2,1,0:T(8,128)} %param.13) | copy-start | bytes 3145732

commit v4 on v3

--- a/solution.py
+++ b/solution.py
@@ -132,30 +132,33 @@
             emit(j + 8 * step, value)
 
 
-def along_lanes(load, store, stage, moved):
+def along_lanes(index, source, target, stage, moved):
     inside = lane_ids() % WIDTH
-    for index in range(TILES):
-        rows = tile(index)
-
-        def move(freq, value):
-            shift, plain, wrapped = shift_of(freq)
-            if shift:
-                mask = inside >= shift
-                value = tuple(
-                    jnp.where(mask, pltpu.roll(v, shift, 1), pltpu.roll(v, shift + WIDTH, 1))
-                    for v in value
-                )
-                real = jnp.where(mask, np.float32(plain.real), np.float32(wrapped.real))
-                imag = jnp.where(mask, np.float32(plain.imag), np.float32(wrapped.imag))
-                value = times(value, real, imag)
-            else:
-                value = scaled(value, plain)
-            put(moved, freq, rows, value)
-
-        block_dft(functools.partial(load, index), move, stage, rows, -1)
-        block_dft(
-            lambda freq: get(moved, freq, rows), functools.partial(store, index), stage, rows, 1
-        )
+    rows = tile(index)
+
+    def move(freq, value):
+        shift, plain, wrapped = shift_of(freq)
+        if shift:
+            mask = inside >= shift
+            value = tuple(
+                jnp.where(mask, pltpu.roll(v, shift, 1), pltpu.roll(v, shift + WIDTH, 1))
+                for v in value
+            )
+            real = jnp.where(mask, np.float32(plain.real), np.float32(wrapped.real))
+            imag = jnp.where(mask, np.float32(plain.imag), np.float32(wrapped.imag))
+            value = times(value, real, imag)
+        else:
+            value = scaled(value, plain)
+        put(moved, freq, rows, value)
+
+    block_dft(lambda block: get(source, block, rows), move, stage, rows, -1)
+    block_dft(
+        lambda freq: get(moved, freq, rows),
+        lambda block, value: put(target, block, rows, value),
+        stage,
+        rows,
+        1,
+    )
 
 
 def along_rows(load, store, stage, held):
@@ -192,33 +195,54 @@
     return pl.ds(8 * index + HALF * half, 8)
 
 
-def read_pair(ref, index, pair):
-    cols = pl.ds(pair * LANES, LANES)
-    parts = [
-        halves(ref[part, natural(index, 0), cols], ref[part, natural(index, 1), cols])
-        for part in range(2)
+def field_copies(source, target, sems):
+    return [
+        [
+            pltpu.make_async_copy(
+                source.at[part, natural(index, half), :],
+                target.at[part, natural(index, half), :],
+                sems.at[index, part, half],
+            )
+            for part in range(2)
+            for half in range(2)
+        ]
+        for index in range(TILES)
     ]
-    return [(parts[0][side], parts[1][side]) for side in range(2)]
-
-
-def read_field(ref, write):
-    for index in range(TILES):
-        for pair in range(BLOCKS // 2):
-            for side, value in enumerate(read_pair(ref, index, pair)):
-                write(index, 2 * pair + side, value)
-
-
-def enter_kernel(field_ref, other_ref, out_ref, packed, stage, moved):
-    read_field(field_ref, lambda index, block, value: put(packed, block, tile(index), value))
-    along_lanes(
-        lambda index, block: get(packed, block, tile(index)),
-        lambda index, block, value: put(out_ref.at[:, 0], block, tile(index), value),
-        stage,
-        moved,
-    )
-    read_field(
-        other_ref, lambda index, block, value: put(out_ref.at[:, 1], block, tile(index), value)
-    )
+
+
+def start(copies):
+    for tile_copies in copies:
+        for copy in tile_copies:
+            copy.start()
+
+
+def wait(tile_copies):
+    for copy in tile_copies:
+        copy.wait()
+
+
+def read_field(ref, index, write):
+    for pair in range(BLOCKS // 2):
+        cols = pl.ds(pair * LANES, LANES)
+        parts = [
+            halves(ref[part, natural(index, 0), cols], ref[part, natural(index, 1), cols])
+            for part in range(2)
+        ]
+        for side in range(2):
+            write(2 * pair + side, (parts[0][side], parts[1][side]))
+
+
+def enter_kernel(field_ref, other_ref, out_ref, stage, moved):
+    grad_out, other_out = out_ref.at[:, 0], out_ref.at[:, 1]
+    for index in range(TILES):
+        read_field(
+            field_ref, index, lambda block, value: put(grad_out, block, tile(index), value)
+        )
+        along_lanes(index, grad_out, grad_out, stage, moved)
+    for index in range(TILES):
+        read_field(
+            other_ref, index, lambda block, value: put(other_out, block, tile(index), value)
+        )
 
 
 def column_kernel(info_ref, in_ref, wave_ref, out_ref, stage, held):
@@ -259,9 +283,7 @@
     )
 
 
-def write_products(
-    tick, led_ref, info_ref, turn_ref, lit_x_ref, lit_y_ref, wave, field_ref, out_ref, *plain
-):
+def light_rows(tick, led_ref, info_ref, turn_ref, lit_y_ref):
     led = led_ref[0, tick]
     column_shift = led // LED_SIDE
     row_shift = led - column_shift * LED_SIDE
@@ -277,42 +299,54 @@
         pair = tuple(jnp.broadcast_to(v, (8, LANES)) for v in pair)
         return times(pair, turn_real, turn_imag)
 
-    for index in range(TILES):
-        lit_y = [lit_rows(natural(index, half)) for half in range(2)]
-        for pair in range(BLOCKS // 2):
-            cols = pl.ds(pair * LANES, LANES)
-            left, right = wave(index, 2 * pair), wave(index, 2 * pair + 1)
-            reals, imags = halves(left[0], right[0]), halves(left[1], right[1])
-            lit_x = (
-                lit_x_ref[column_shift, pair : pair + 1, :],
-                lit_x_ref[column_shift + LED_SIDE, pair : pair + 1, :],
-            )
-            for half in range(2):
-                rows = natural(index, half)
-                real, imag = reals[half], imags[half]
-                if plain:
-                    t_ref, plain_ref = plain
-                    t_real, t_imag = t_ref[0, rows, cols], t_ref[1, rows, cols]
-                    plain_ref[0, rows, cols] = real * t_real + imag * t_imag
-                    plain_ref[1, rows, cols] = imag * t_real - real * t_imag
-                lit = times(lit_y[half], *lit_x)
-                f_real, f_imag = times(lit, field_ref[0, rows, cols], field_ref[1, rows, cols])
-                out_ref[0, rows, cols] = real * f_real + imag * f_imag
-                out_ref[1, rows, cols] = imag * f_real - real * f_imag
-
-
-def entry_kernel(led_ref, info_ref, turn_ref, lit_x_ref, lit_y_ref, field_ref, wave_ref, out_ref):
-    write_products(
-        0,
-        led_ref,
-        info_ref,
-        turn_ref,
-        lit_x_ref,
-        lit_y_ref,
-        lambda index, block: get(wave_ref, block, tile(index)),
-        field_ref,
-        out_ref,
-    )
+    return column_shift, lit_rows
+
+
+def write_products(index, wave_ref, lights, lit_x_ref, field_ref, out_ref, *plain):
+    column_shift, lit_rows = lights
+    lit_y = [lit_rows(natural(index, half)) for half in range(2)]
+    for pair in range(BLOCKS // 2):
+        cols = pl.ds(pair * LANES, LANES)
+        left = get(wave_ref, 2 * pair, tile(index))
+        right = get(wave_ref, 2 * pair + 1, tile(index))
+        reals, imags = halves(left[0], right[0]), halves(left[1], right[1])
+        lit_x = (
+            lit_x_ref[column_shift, pair : pair + 1, :],
+            lit_x_ref[column_shift + LED_SIDE, pair : pair + 1, :],
+        )
+        for half in range(2):
+            rows = natural(index, half)
+            real, imag = reals[half], imags[half]
+            if plain:
+                t_ref, plain_ref = plain
+                t_real, t_imag = t_ref[0, rows, cols], t_ref[1, rows, cols]
+                plain_ref[0, rows, cols] = real * t_real + imag * t_imag
+                plain_ref[1, rows, cols] = imag * t_real - real * t_imag
+            lit = times(lit_y[half], *lit_x)
+            f_real, f_imag = times(lit, field_ref[0, rows, cols], field_ref[1, rows, cols])
+            out_ref[0, rows, cols] = real * f_real + imag * f_imag
+            out_ref[1, rows, cols] = imag * f_real - real * f_imag
+
+
+def entry_kernel(
+    led_ref,
+    info_ref,
+    turn_ref,
+    lit_x_ref,
+    lit_y_ref,
+    field_ref,
+    wave_ref,
+    out_hbm,
+    out,
+    sems,
+):
+    outs = field_copies(out, out_hbm, sems)
+    lights = light_rows(0, led_ref, info_ref, turn_ref, lit_y_ref)
+    for index in range(TILES):
+        write_products(index, wave_ref, lights, lit_x_ref, field_ref, out)
+        start([outs[index]])
+    for index in range(TILES):
+        wait(outs[index])
 
 
 def exit_kernel(
@@ -324,51 +358,48 @@
     field_ref,
     t_ref,
     in_ref,
-    out_ref,
-    plain_ref,
+    out_hbm,
+    plain_hbm,
     packed,
     stage,
     moved,
+    out,
+    plain,
+    out_sems,
+    plain_sems,
 ):
-    along_lanes(
-        lambda index, block: get(in_ref, block, tile(index)),
-        lambda index, block, value: put(packed, block, tile(index), value),
-        stage,
-        moved,
-    )
-    write_products(
-        1,
-        led_ref,
-        info_ref,
-        turn_ref,
-        lit_x_ref,
-        lit_y_ref,
-        lambda index, block: get(packed, block, tile(index)),
-        field_ref,
-        out_ref,
-        t_ref,
-        plain_ref,
-    )
+    outs = field_copies(out, out_hbm, out_sems)
+    plains = field_copies(plain, plain_hbm, plain_sems)
+    lights = light_rows(1, led_ref, info_ref, turn_ref, lit_y_ref)
+    for index in range(TILES):
+        along_lanes(index, in_ref, packed, stage, moved)
+        write_products(index, packed, lights, lit_x_ref, field_ref, out, t_ref, plain)
+        start([outs[index], plains[index]])
+    for index in range(TILES):
+        wait(outs[index] + plains[index])
 
 
 WHOLE = pl.BlockSpec(memory_space=pltpu.VMEM)
 SCALAR = pl.BlockSpec(memory_space=pltpu.SMEM)
+OUTSIDE = pl.BlockSpec(memory_space=pltpu.HBM)
 CHAIN = (BLOCKS, 2, HALF, LANES)
 PACKED = jax.ShapeDtypeStruct(CHAIN, jnp.float32)
 BOTH = jax.ShapeDtypeStruct((BLOCKS, 2, 2, HALF, LANES), jnp.float32)
 FIELD = jax.ShapeDtypeStruct((2, WIDTH, N), jnp.float32)
+FIELD_BUFFER = pltpu.VMEM(FIELD.shape, jnp.float32)
+SEMS = pltpu.SemaphoreType.DMA((TILES, 2, 2))
 BUFFER = pltpu.VMEM(CHAIN, jnp.float32)
 HELD = pltpu.VMEM((BLOCKS, 2, 3 * HALF, LANES), jnp.float32)
 
 
-def call(kernel, out_shape, operands, name, scratch=(), scalars=0):
+def call(kernel, out_shape, operands, name, scratch=(), scalars=0, out_spec=WHOLE):
     outs = jax.tree.leaves(out_shape)
     size = sum(4 * math.prod(x.shape) for x in outs) + sum(4 * x.size for x in operands)
     return pl.pallas_call(
         kernel,
         out_shape=out_shape,
         in_specs=[SCALAR] * scalars + [WHOLE] * (len(operands) - scalars),
-        out_specs=jax.tree.map(lambda _: WHOLE, out_shape),
+        out_specs=jax.tree.map(lambda _: out_spec, out_shape),
         scratch_shapes=list(scratch),
         compiler_params=pltpu.CompilerParams(vmem_limit_bytes=VMEM_LIMIT),
         cost_estimate=pl.CostEstimate(flops=20 * size, bytes_accessed=size, transcendentals=0),
@@ -389,28 +420,38 @@
     first = (lax.axis_index("depth") == 0).astype(jnp.int32)
     info = jnp.stack([lax.axis_index("rows"), first]).astype(jnp.int32)
     lit_x, lit_y, turns = (jnp.asarray(table) for table in light_tables())
-    lights = [led_index, info, turns, lit_x, lit_y]
     both = call(
         enter_kernel,
         BOTH,
         [grad_arriving[0], jnp.where(first == 1, loss_grad, t_entry[0])],
         "enter",
-        [BUFFER, BUFFER, BUFFER],
-    )
+        [BUFFER, BUFFER],
+    )
+    both, info = lax.optimization_barrier((both, info))
     wave, onward = call(
         column_kernel, (PACKED, PACKED), [info, exchange(both)], "columns", [BUFFER, HELD], 1
     )
     onward = to_previous(onward)
     wave = exchange(wave)
-    grad_entry = call(entry_kernel, FIELD, [*lights, fields_entry[0], wave], "entry", scalars=3)
+    lights = [led_index, info, turns, lit_x, lit_y]
+    grad_entry = call(
+        entry_kernel,
+        FIELD,
+        [*lights, fields_entry[0], wave],
+        "entry",
+        [FIELD_BUFFER, SEMS],
+        3,
+        OUTSIDE,
+    )
     onward, grad_entry = lax.optimization_barrier((onward, grad_entry))
     grad_exit, leaving = call(
         exit_kernel,
         (FIELD, FIELD),
         [*lights, fields_exit[0], t_exit[0], exchange(onward)],
         "exit",
-        [BUFFER, BUFFER, BUFFER],
+        [BUFFER, BUFFER, BUFFER, FIELD_BUFFER, FIELD_BUFFER, SEMS, SEMS],
         3,
+        OUTSIDE,
     )
     return (grad_entry[None], grad_exit[None], leaving[None])
 

time: 96.7 us -> 95.2 us (0.984)
  blocking collectives: 41.5 us -> 78.2 us
  waiting for transfers between devices: 28.2 us -> 0.01 us
  starting transfers between devices: 13.9 us -> 5.34 us
  local copies, waits for them, and re-layouts: 1.42 us -> 0.05 us
    all_to_all x2 -> x3, blocking collectives: 41.5 us -> 78.2 us  [exchange(): lax.all_to_all(packed, 'rows', split_axis=0, concat_axis=0, tiled=True)]
    all_to_all x1 -> x0, waiting for transfers between devices: 28.2 us -> none  [exchange(): lax.all_to_all(packed, 'rows', split_axis=0, concat_axis=0, tiled=True)]
    all_to_all x1 -> x0, starting transfers between devices: 8.59 us -> none  [exchange(): lax.all_to_all(packed, 'rows', split_axis=0, concat_axis=0, tiled=True)]
    unnamed x18 -> x16, local copies, waits for them, and re-layouts: 1.42 us -> 0.05 us
  transfers between devices with their start and end apart: 2 -> 1, of which waited for: 1 -> 0; matrix products, arithmetic and copies ran while one was open for 0% -> 0% of each run, Pallas kernels for 2% -> 2%
where the time goes in v4:
time: 95.2 us; the launch traced here: 95 us
  blocking collectives  78.2 us (82%)
  Pallas kernels  8.92 us (9%)
  starting transfers between devices  5.34 us (6%)
  other arithmetic  1.81 us (2%)
    all_to_all x3, blocking collectives, exchange(): lax.all_to_all(packed, 'rows', split_axis=0, concat_axis=0, tiled=True)  78.2 us
    pallas_call x4, Pallas kernels, call(): pl.pallas_call(kernel, out_shape=out_shape, in_specs=[SCALAR] * scalars +...  8.92 us
    ppermute x1, starting transfers between devices, to_previous(): lax.ppermute(value, 'depth', [(s, (s - 1) % count) for s in range(count)])  5.34 us
  transfers between devices with their start and end apart: 1, of which 0 were waited for; matrix products, arithmetic and copies ran while one was open for 0% of the time, Pallas kernels for 2%

profile of v4, /device:TPU:1, one launch (start us, length us, event | category | flops | bytes accessed | tf_op | source)
XLA Modules:
  0.0 95.0 jit_solution(17794915542695284232)
XLA Ops:
  0.6 0.0 copy-start.3
  0.6 0.1 pad_add_fusion.info_ref
  0.7 1.7 %bitcast_select_fusion.other_ref = f32[2,64,2048]{2,1,0:T(8,128)S(1)} fusion(f32[2,64,2048]{2,1,0:T(8,128)} %param.11, f32[1,2,64,2048]{3,2,1,0:T(8,128)} %param.12, pred[]{:T(512)S(6)} %eq.7), kind=kLoop, calls=%fused_computation | loop fusion | flops 262144 | bytes 3145729 | tf_op jit(solution)/shard_map/jit(_where)/select_n | solution.py:426
  2.5 0.0 copy-done.3
  2.5 1.5 %enter.1 = f32[32,2,2,32,128]{4,3,2,1,0:T(8,128)S(1)} custom-call(f32[2,64,2048]{2,1,0:T(8,128)S(1)} %bitcast.14, f32[2,64,2048]{2,1,0:T(8,128)S(1)} %bitcast_select_fusion.other_ref), custom_call_target="tpu_custom_call" | custom-call | flops 83886080 | bytes 4194304 | tf_op jit(solution)/shard_map/enter/pallas_call | solution.py:398
  4.0 36.5 %all_to_all.15.in_ref = f32[32,2,2,32,128]{4,3,2,1,0:T(8,128)S(1)} all-to-all(f32[32,2,2,32,128]{4,3,2,1,0:T(8,128)S(1)} %enter.1), channel_id=1, replica_groups=mesh['depth'=8,'rows'=32] {'rows'}, dimensions={0} | all-to-all | bytes 4194304 | tf_op jit(solution)/shard_map/all_to_all | solution.py:411
  40.5 0.0 copy-start
  40.5 0.0 copy-start.7
  40.5 2.4 %columns.1 = (f32[32,2,32,128]{3,2,1,0:T(8,128)S(1)}, f32[32,2,32,128]{3,2,1,0:T(8,128)S(1)}) custom-call(s32[2]{0:T(128)S(1)} %pad_add_fusion.info_ref, f32[32,2,2,32,128]{4,3,2,1,0:T(8,128)S(1)} %all_to_all.15.in_ref), custom_call_target="tpu_custom_call" | custom-call | flops 83886240 | bytes 4194312 | tf_op jit(solution)/shard_map/columns/pallas_call | solution.py:398
  43.0 5.3 %collective-permute-start = (f32[32,2,32,128]{3,2,1,0:T(8,128)S(1)}, f32[32,2,32,128]{3,2,1,0:T(8,128)S(1)}, u32[]{:S(2)}, u32[]{:S(2)}) collective-permute-start(f32[32,2,32,128]{3,2,1,0:T(8,128)S(1)} %get-tuple-element.13), channel_id=1, source_target_pairs={{0,224},{32,0},{64,32},{96,64},{128,96},{160,128},{192,160},{224,1... | collective-permute-start | bytes 3145736 | tf_op jit(solution)/shard_map/ppermute | solution.py:416
  48.3 20.9 %all_to_all.16.wave_ref = f32[32,2,32,128]{3,2,1,0:T(8,128)S(1)} all-to-all(f32[32,2,32,128]{3,2,1,0:T(8,128)S(1)} %get-tuple-element.14), channel_id=1, replica_groups=mesh['depth'=8,'rows'=32] {'rows'}, dimensions={0} | all-to-all | bytes 2097152 | tf_op jit(solution)/shard_map/all_to_all | solution.py:411
  69.2 0.0 copy-done
  69.2 0.0 copy-done.4
  69.2 0.0 copy-done.5
  69.2 0.0 copy-done.6
  69.2 0.0 copy-done.7
  69.3 0.0 copy-start.1
  69.3 0.0 copy-start.2
  69.3 1.9 %entry.1 = f32[2,64,2048]{2,1,0:T(8,128)} custom-call(s32[1,2]{1,0:T(1,128)S(1)} %copy-done.7, s32[2]{0:T(128)S(1)} %pad_add_fusion.info_ref, f32[2,32]{1,0:T(2,128)S(1)} %copy-done.6, f32[30,16,128]{2,1,0:T(8,128)S(1)} %copy-done.4, f32[2,64,128]{2,1,0:T(8,128)S(1)} %copy-done.5, f32[2,64,2048]{2,1,0:T(8,128)S(1)} %bitcast.11, ...), custom_call_target="tpu_custom_call" | custom-call | flops 69145920 | bytes 3457296 | tf_op jit(solution)/shard_map/entry/pallas_call | solution.py:398
  71.2 0.0 collective-permute-done
  71.2 20.7 %all_to_all.17.in_ref = f32[32,2,32,128]{3,2,1,0:T(8,128)S(1)} all-to-all(f32[32,2,32,128]{3,2,1,0:T(8,128)S(1)} %collective-permute-done), channel_id=1, replica_groups=mesh['depth'=8,'rows'=32] {'rows'}, dimensions={0} | all-to-all | bytes 2097152 | tf_op jit(solution)/shard_map/all_to_all | solution.py:411
  91.9 0.0 copy-done.1
  91.9 0.0 copy-done.2
  91.9 3.1 %exit.1 = (f32[2,64,2048]{2,1,0:T(8,128)}, f32[2,64,2048]{2,1,0:T(8,128)}) custom-call(s32[1,2]{1,0:T(1,128)S(1)} %copy-done.7, s32[2]{0:T(128)S(1)} %pad_add_fusion.info_ref, f32[2,32]{1,0:T(2,128)S(1)} %copy-done.6, f32[30,16,128]{2,1,0:T(8,128)S(1)} %copy-done.4, f32[2,64,128]{2,1,0:T(8,128)S(1)} %copy-done.5, f32[2,64,2048]{2,1,0:T(8,128)S(1)} %bitcast.12, ...), custom_call_target="tpu_custom_call" | custom-call | flops 111088960 | bytes 5554448 | tf_op jit(solution)/shard_map/exit/pallas_call | solution.py:398
  (3 shorter events, 0.0 us)
Async XLA Ops:
  0.6 1.9 %copy-start.3 = (f32[1,2,64,2048]{3,2,1,0:T(8,128)S(1)}, f32[1,2,64,2048]{3,2,1,0:T(8,128)}, u32[]{:S(2)}) copy-start(f32[1,2,64,2048]{3,2,1,0:T(8,128)} %param.10) | copy-start | bytes 3145732
  40.5 28.7 %copy-start = (f32[1,2,64,2048]{3,2,1,0:T(8,128)S(1)}, f32[1,2,64,2048]{3,2,1,0:T(8,128)}, u32[]{:S(2)}) copy-start(f32[1,2,64,2048]{3,2,1,0:T(8,128)} %param.14) | copy-start | bytes 3145732
  40.5 28.7 %copy-start.4 = (f32[30,16,128]{2,1,0:T(8,128)S(1)}, f32[30,16,128]{2,1,0:T(8,128)}, u32[]{:S(2)}) copy-start(f32[30,16,128]{2,1,0:T(8,128)} %constant.19.clone.lit_x_ref) | copy-start | bytes 737284
  40.5 28.7 %copy-start.5 = (f32[2,64,128]{2,1,0:T(8,128)S(1)}, f32[2,64,128]{2,1,0:T(8,128)}, u32[]{:S(2)}) copy-start(f32[2,64,128]{2,1,0:T(8,128)} %constant.20.clone.lit_y_ref) | copy-start | bytes 196612
  40.5 28.7 %copy-start.6 = (f32[2,32]{1,0:T(2,128)S(1)}, f32[2,32]{1,0:T(2,128)}, u32[]{:S(2)}) copy-start(f32[2,32]{1,0:T(2,128)} %constant.21.clone.turn_ref) | copy-start | bytes 772
  40.5 28.7 %copy-start.7 = (s32[1,2]{1,0:T(1,128)S(1)}, s32[1,2]{1,0:T(1,128)}, u32[]{:S(2)}) copy-start(s32[1,2]{1,0:T(1,128)} %led_ref.3) | copy-start | bytes 28
  43.0 28.2 %collective-permute-start = (f32[32,2,32,128]{3,2,1,0:T(8,128)S(1)}, f32[32,2,32,128]{3,2,1,0:T(8,128)S(1)}, u32[]{:S(2)}, u32[]{:S(2)}) collective-permute-start(f32[32,2,32,128]{3,2,1,0:T(8,128)S(1)} %get-tuple-element.13), channel_id=1, source_target_pairs={{0,224},{32,0},{64,32},{96,64},{128,96},{160,128},{192,160},{224,1... | collective-permute-start | bytes 3145736 | tf_op jit(solution)/shard_map/ppermute | solution.py:416
  69.3 22.6 %copy-start.1 = (f32[1,2,64,2048]{3,2,1,0:T(8,128)S(1)}, f32[1,2,64,2048]{3,2,1,0:T(8,128)}, u32[]{:S(2)}) copy-start(f32[1,2,64,2048]{3,2,1,0:T(8,128)} %param.15) | copy-start | bytes 3145732
  69.3 22.6 %copy-start.2 = (f32[1,2,64,2048]{3,2,1,0:T(8,128)S(1)}, f32[1,2,64,2048]{3,2,1,0:T(8,128)}, u32[]{:S(2)}) copy-start(f32[1,2,64,2048]{3,2,1,0:T(8,128)} %param.13) | copy-start | bytes 3145732

commit v5 on v4

--- a/solution.py
+++ b/solution.py
@@ -162,28 +162,41 @@
 
 
 def along_rows(load, store, stage, held):
+    row_ids = lax.broadcasted_iota(jnp.int32, (8, LANES), 0)
     low = lane_ids() < WIDTH
     for index in range(TILES):
         rows = tile(index)
 
         def hold(freq, value):
-            shift, plain, wrapped = shift_of(freq)
-            plain = scaled(value, plain)
-            wrapped = scaled(value, wrapped) if shift else None
+            shift = shift_of(freq)[0]
             if shift > HALF:
-                put(held, freq, rows, wrapped)
+                put(held, freq, rows, value)
+            if shift:
+                crossed = tuple(pltpu.roll(v, WIDTH, 1) for v in value)
+                put(held, freq, pl.ds(HALF + 8 * index, 8), crossed)
             if shift < HALF:
-                put(held, freq, pl.ds(2 * HALF + 8 * index, 8), plain)
-            if shift:
-                crossed = tuple(
-                    pltpu.roll(jnp.where(low, p, w), WIDTH, 1) for p, w in zip(plain, wrapped)
-                )
-                put(held, freq, pl.ds(HALF + 8 * index, 8), crossed)
+                put(held, freq, pl.ds(2 * HALF + 8 * index, 8), value)
 
         block_dft(functools.partial(load, index), hold, stage, rows, -1)
+
+    def shifted(index, freq):
+        shift, plain, wrapped = shift_of(freq)
+        begin = 2 * HALF - shift + 8 * index
+        value = get(held, freq, pl.ds(begin, 8))
+        if begin >= 2 * HALF:
+            return scaled(value, plain)
+        if begin + 8 <= HALF:
+            return scaled(value, wrapped)
+        mask = row_ids >= jnp.where(low, 2 * HALF - begin, HALF - begin)
+        return times(
+            value,
+            jnp.where(mask, np.float32(plain.real), np.float32(wrapped.real)),
+            jnp.where(mask, np.float32(plain.imag), np.float32(wrapped.imag)),
+        )
+
     for index in range(TILES):
         block_dft(
-            lambda freq: get(held, freq, pl.ds(2 * HALF - shift_of(freq)[0] + 8 * index, 8)),
+            functools.partial(shifted, index),
             functools.partial(store, index),
             stage,
             tile(index),
@@ -328,55 +341,39 @@
             out_ref[1, rows, cols] = imag * f_real - real * f_imag
 
 
-def entry_kernel(
+def last_kernel(
     led_ref,
     info_ref,
     turn_ref,
     lit_x_ref,
     lit_y_ref,
-    field_ref,
+    entry_ref,
+    exit_ref,
+    t_ref,
     wave_ref,
-    out_hbm,
-    out,
-    sems,
-):
-    outs = field_copies(out, out_hbm, sems)
-    lights = light_rows(0, led_ref, info_ref, turn_ref, lit_y_ref)
-    for index in range(TILES):
-        write_products(index, wave_ref, lights, lit_x_ref, field_ref, out)
-        start([outs[index]])
-    for index in range(TILES):
-        wait(outs[index])
-
-
-def exit_kernel(
-    led_ref,
-    info_ref,
-    turn_ref,
-    lit_x_ref,
-    lit_y_ref,
-    field_ref,
-    t_ref,
-    in_ref,
-    out_hbm,
+    onward_ref,
+    entry_hbm,
+    exit_hbm,
     plain_hbm,
     packed,
     stage,
     moved,
-    out,
-    plain,
-    out_sems,
-    plain_sems,
+    entry_out,
+    exit_out,
+    plain_out,
+    *sems,
 ):
-    outs = field_copies(out, out_hbm, out_sems)
-    plains = field_copies(plain, plain_hbm, plain_sems)
-    lights = light_rows(1, led_ref, info_ref, turn_ref, lit_y_ref)
-    for index in range(TILES):
-        along_lanes(index, in_ref, packed, stage, moved)
-        write_products(index, packed, lights, lit_x_ref, field_ref, out, t_ref, plain)
-        start([outs[index], plains[index]])
-    for index in range(TILES):
-        wait(outs[index] + plains[index])
+    results = ((entry_out, entry_hbm), (exit_out, exit_hbm), (plain_out, plain_hbm))
+    outs = [field_copies(*pair, sem) for pair, sem in zip(results, sems)]
+    lights = [light_rows(tick, led_ref, info_ref, turn_ref, lit_y_ref) for tick in range(2)]
+    for index in range(TILES):
+        write_products(index, wave_ref, lights[0], lit_x_ref, entry_ref, entry_out)
+        start([outs[0][index]])
+        along_lanes(index, onward_ref, packed, stage, moved)
+        write_products(index, packed, lights[1], lit_x_ref, exit_ref, exit_out, t_ref, plain_out)
+        start([outs[1][index], outs[2][index]])
+    for index in range(TILES):
+        wait(outs[0][index] + outs[1][index] + outs[2][index])
 
 
 WHOLE = pl.BlockSpec(memory_space=pltpu.VMEM)
@@ -431,25 +428,27 @@
     wave, onward = call(
         column_kernel, (PACKED, PACKED), [info, exchange(both)], "columns", [BUFFER, HELD], 1
     )
+    onward = exchange(onward)
+    wave, onward = lax.optimization_barrier((wave, onward))
     onward = to_previous(onward)
     wave = exchange(wave)
-    lights = [led_index, info, turns, lit_x, lit_y]
-    grad_entry = call(
-        entry_kernel,
-        FIELD,
-        [*lights, fields_entry[0], wave],
-        "entry",
-        [FIELD_BUFFER, SEMS],
-        3,
-        OUTSIDE,
-    )
-    onward, grad_entry = lax.optimization_barrier((onward, grad_entry))
-    grad_exit, leaving = call(
-        exit_kernel,
-        (FIELD, FIELD),
-        [*lights, fields_exit[0], t_exit[0], exchange(onward)],
-        "exit",
-        [BUFFER, BUFFER, BUFFER, FIELD_BUFFER, FIELD_BUFFER, SEMS, SEMS],
+    grad_entry, grad_exit, leaving = call(
+        last_kernel,
+        (FIELD, FIELD, FIELD),
+        [
+            led_index,
+            info,
+            turns,
+            lit_x,
+            lit_y,
+            fields_entry[0],
+            fields_exit[0],
+            t_exit[0],
+            wave,
+            onward,
+        ],
+        "last",
+        [BUFFER] * 3 + [FIELD_BUFFER] * 3 + [SEMS] * 3,
         3,
         OUTSIDE,
     )

time: 95.2 us -> 95.5 us (level)
  waiting for transfers between devices: 0.01 us -> 1.49 us
  Pallas kernels: 8.92 us -> 7.5 us
    ppermute x1, waiting for transfers between devices: 0.01 us -> 1.49 us  [to_previous(): lax.ppermute(value, 'depth', [(s, (s - 1) % count) for s in range(count)])]
    pallas_call x4 -> x3, Pallas kernels: 8.92 us -> 7.5 us  [call(): pl.pallas_call(kernel, out_shape=out_shape, in_specs=[SCALAR] * scalars +...]
  transfers between devices with their start and end apart: 1 -> 1, of which waited for: 0 -> 1; matrix products, arithmetic and copies ran while one was open for 0% -> 0% of each run, Pallas kernels for 2% -> 0%
where the time goes in v5:
time: 95.5 us; the launch traced here: 95.3 us
  blocking collectives  78.4 us (82%)
  Pallas kernels  7.5 us (8%)
  starting transfers between devices  5.26 us (6%)
  other arithmetic  1.81 us (2%)
  waiting for transfers between devices  1.49 us (2%)
    all_to_all x3, blocking collectives, exchange(): lax.all_to_all(packed, 'rows', split_axis=0, concat_axis=0, tiled=True)  78.4 us
    pallas_call x3, Pallas kernels, call(): pl.pallas_call(kernel, out_shape=out_shape, in_specs=[SCALAR] * scalars +...  7.5 us
    ppermute x1, starting transfers between devices, to_previous(): lax.ppermute(value, 'depth', [(s, (s - 1) % count) for s in range(count)])  5.26 us
  transfers between devices with their start and end apart: 1, of which 1 were waited for; matrix products, arithmetic and copies ran while one was open for 0% of the time, Pallas kernels for 0%

profile of v5, /device:TPU:1, one launch (start us, length us, event | category | flops | bytes accessed | tf_op | source)
XLA Modules:
  0.0 95.3 jit_solution(11786362064638806285)
XLA Ops:
  0.6 0.0 copy-start.3
  0.6 0.1 pad_add_fusion.info_ref
  0.7 1.7 %bitcast_select_fusion.other_ref = f32[2,64,2048]{2,1,0:T(8,128)S(1)} fusion(f32[2,64,2048]{2,1,0:T(8,128)} %param.11, f32[1,2,64,2048]{3,2,1,0:T(8,128)} %param.12, pred[]{:T(512)S(6)} %eq.7), kind=kLoop, calls=%fused_computation | loop fusion | flops 262144 | bytes 3145729 | tf_op jit(solution)/shard_map/jit(_where)/select_n | solution.py:423
  2.5 0.0 copy-done.3
  2.5 1.5 %enter.1 = f32[32,2,2,32,128]{4,3,2,1,0:T(8,128)S(1)} custom-call(f32[2,64,2048]{2,1,0:T(8,128)S(1)} %bitcast.14, f32[2,64,2048]{2,1,0:T(8,128)S(1)} %bitcast_select_fusion.other_ref), custom_call_target="tpu_custom_call" | custom-call | flops 83886080 | bytes 4194304 | tf_op jit(solution)/shard_map/enter/pallas_call | solution.py:395
  4.0 36.5 %all_to_all.15.in_ref = f32[32,2,2,32,128]{4,3,2,1,0:T(8,128)S(1)} all-to-all(f32[32,2,2,32,128]{4,3,2,1,0:T(8,128)S(1)} %enter.1), channel_id=1, replica_groups=mesh['depth'=8,'rows'=32] {'rows'}, dimensions={0} | all-to-all | bytes 4194304 | tf_op jit(solution)/shard_map/all_to_all | solution.py:408
  40.5 2.3 %columns.1 = (f32[32,2,32,128]{3,2,1,0:T(8,128)S(1)}, f32[32,2,32,128]{3,2,1,0:T(8,128)S(1)}) custom-call(s32[2]{0:T(128)S(1)} %pad_add_fusion.info_ref, f32[32,2,2,32,128]{4,3,2,1,0:T(8,128)S(1)} %all_to_all.15.in_ref), custom_call_target="tpu_custom_call" | custom-call | flops 83886240 | bytes 4194312 | tf_op jit(solution)/shard_map/columns/pallas_call | solution.py:395
  42.9 0.0 copy-start
  42.9 0.0 copy-start.1
  42.9 0.0 copy-start.2
  42.9 0.0 copy-start.4
  42.9 0.0 copy-start.5
  42.9 0.0 copy-start.6
  42.9 0.0 copy-start.7
  42.9 20.9 %all_to_all.16 = f32[32,2,32,128]{3,2,1,0:T(8,128)S(1)} all-to-all(f32[32,2,32,128]{3,2,1,0:T(8,128)S(1)} %get-tuple-element.15), channel_id=1, replica_groups=mesh['depth'=8,'rows'=32] {'rows'}, dimensions={0} | all-to-all | bytes 2097152 | tf_op jit(solution)/shard_map/all_to_all | solution.py:408
  63.9 5.3 %collective-permute-start = (f32[32,2,32,128]{3,2,1,0:T(8,128)S(1)}, f32[32,2,32,128]{3,2,1,0:T(8,128)S(1)}, u32[]{:S(2)}, u32[]{:S(2)}) collective-permute-start(f32[32,2,32,128]{3,2,1,0:T(8,128)S(1)} %all_to_all.16), channel_id=1, source_target_pairs={{0,224},{32,0},{64,32},{96,64},{128,96},{160,128},{192,160},{224,1... | collective-permute-start | bytes 3145736 | tf_op jit(solution)/shard_map/ppermute | solution.py:413
  69.1 20.9 %all_to_all.17.wave_ref = f32[32,2,32,128]{3,2,1,0:T(8,128)S(1)} all-to-all(f32[32,2,32,128]{3,2,1,0:T(8,128)S(1)} %get-tuple-element.16), channel_id=1, replica_groups=mesh['depth'=8,'rows'=32] {'rows'}, dimensions={0} | all-to-all | bytes 2097152 | tf_op jit(solution)/shard_map/all_to_all | solution.py:408
  90.1 1.5 %collective-permute-done.onward_ref = f32[32,2,32,128]{3,2,1,0:T(8,128)S(1)} collective-permute-done((f32[32,2,32,128]{3,2,1,0:T(8,128)S(1)}, f32[32,2,32,128]{3,2,1,0:T(8,128)S(1)}, u32[]{:S(2)}, u32[]{:S(2)}) %collective-permute-start) | collective-permute-done | bytes 1048608 | tf_op jit(solution)/shard_map/ppermute | solution.py:413
  91.5 0.0 copy-done
  91.6 0.0 copy-done.1
  91.6 0.0 copy-done.2
  91.6 0.0 copy-done.4
  91.6 0.0 copy-done.5
  91.6 3.7 %last.1 = (f32[2,64,2048]{2,1,0:T(8,128)}, f32[2,64,2048]{2,1,0:T(8,128)}, f32[2,64,2048]{2,1,0:T(8,128)}) custom-call(s32[1,2]{1,0:T(1,128)S(1)} %copy-done.7, s32[2]{0:T(128)S(1)} %pad_add_fusion.info_ref, f32[2,32]{1,0:T(2,128)S(1)} %copy-done.6, f32[30,16,128]{2,1,0:T(8,128)S(1)} %copy-done.4, f32[2,64,128]{2,1,0:T(8,128)S(1)} %copy-done.5, ...), custom_call_target="tpu_custom_call" | custom-call | flops 174003520 | bytes 8700176 | tf_op jit(solution)/shard_map/last/pallas_call | solution.py:395
  (2 shorter events, 0.0 us)
Async XLA Ops:
  0.6 1.9 %copy-start.3 = (f32[1,2,64,2048]{3,2,1,0:T(8,128)S(1)}, f32[1,2,64,2048]{3,2,1,0:T(8,128)}, u32[]{:S(2)}) copy-start(f32[1,2,64,2048]{3,2,1,0:T(8,128)} %param.10) | copy-start | bytes 3145732
  42.9 48.7 %copy-start = (f32[1,2,64,2048]{3,2,1,0:T(8,128)S(1)}, f32[1,2,64,2048]{3,2,1,0:T(8,128)}, u32[]{:S(2)}) copy-start(f32[1,2,64,2048]{3,2,1,0:T(8,128)} %param.14) | copy-start | bytes 3145732
  42.9 48.7 %copy-start.1 = (f32[1,2,64,2048]{3,2,1,0:T(8,128)S(1)}, f32[1,2,64,2048]{3,2,1,0:T(8,128)}, u32[]{:S(2)}) copy-start(f32[1,2,64,2048]{3,2,1,0:T(8,128)} %param.15) | copy-start | bytes 3145732
  42.9 48.7 %copy-start.2 = (f32[1,2,64,2048]{3,2,1,0:T(8,128)S(1)}, f32[1,2,64,2048]{3,2,1,0:T(8,128)}, u32[]{:S(2)}) copy-start(f32[1,2,64,2048]{3,2,1,0:T(8,128)} %param.13) | copy-start | bytes 3145732
  42.9 48.7 %copy-start.4 = (f32[30,16,128]{2,1,0:T(8,128)S(1)}, f32[30,16,128]{2,1,0:T(8,128)}, u32[]{:S(2)}) copy-start(f32[30,16,128]{2,1,0:T(8,128)} %constant.19.clone.lit_x_ref) | copy-start | bytes 737284
  42.9 48.7 %copy-start.5 = (f32[2,64,128]{2,1,0:T(8,128)S(1)}, f32[2,64,128]{2,1,0:T(8,128)}, u32[]{:S(2)}) copy-start(f32[2,64,128]{2,1,0:T(8,128)} %constant.20.clone.lit_y_ref) | copy-start | bytes 196612
  42.9 48.7 %copy-start.6 = (f32[2,32]{1,0:T(2,128)S(1)}, f32[2,32]{1,0:T(2,128)}, u32[]{:S(2)}) copy-start(f32[2,32]{1,0:T(2,128)} %constant.21.clone.turn_ref) | copy-start | bytes 772
  42.9 48.7 %copy-start.7 = (s32[1,2]{1,0:T(1,128)S(1)}, s32[1,2]{1,0:T(1,128)}, u32[]{:S(2)}) copy-start(s32[1,2]{1,0:T(1,128)} %led_ref.1) | copy-start | bytes 28
  63.9 27.7 %collective-permute-start = (f32[32,2,32,128]{3,2,1,0:T(8,128)S(1)}, f32[32,2,32,128]{3,2,1,0:T(8,128)S(1)}, u32[]{:S(2)}, u32[]{:S(2)}) collective-permute-start(f32[32,2,32,128]{3,2,1,0:T(8,128)S(1)} %all_to_all.16), channel_id=1, source_target_pairs={{0,224},{32,0},{64,32},{96,64},{128,96},{160,128},{192,160},{224,1... | collective-permute-start | bytes 3145736 | tf_op jit(solution)/shard_map/ppermute | solution.py:413

commit v6 on v5

--- a/solution.py
+++ b/solution.py
@@ -132,9 +132,10 @@
             emit(j + 8 * step, value)
 
 
-def along_lanes(index, source, target, stage, moved):
+def along_lanes(index, source, target, stage, moved, place=None):
     inside = lane_ids() % WIDTH
     rows = tile(index)
+    source_rows = rows if place is None else tile(place)
 
     def move(freq, value):
         shift, plain, wrapped = shift_of(freq)
@@ -151,7 +152,7 @@
             value = scaled(value, plain)
         put(moved, freq, rows, value)
 
-    block_dft(lambda block: get(source, block, rows), move, stage, rows, -1)
+    block_dft(lambda block: get(source, block, source_rows), move, stage, rows, -1)
     block_dft(
         lambda freq: get(moved, freq, rows),
         lambda block, value: put(target, block, rows, value),
@@ -258,17 +259,20 @@
         )
 
 
-def column_kernel(info_ref, in_ref, wave_ref, out_ref, stage, held):
+def column_kernel(info_ref, in_ref, near_ref, far_ref, stage, held):
     use_loss = info_ref[1] == 1
-    along_rows(
-        lambda index, block: get(in_ref.at[:, 0], block, tile(index)),
-        lambda index, block, value: put(wave_ref, block, tile(index), value),
-        stage,
-        held,
-    )
+
+    def put_wave(index, block, value):
+        put(near_ref, block, tile(index), value)
+
+    def put_onward(index, block, value):
+        if index < FAR:
+            put(far_ref, block, tile(index), value)
+        else:
+            put(near_ref, block, tile(TILES + index - FAR), value)
 
     def passing(index, block):
-        real, imag = get(wave_ref, block, tile(index))
+        real, imag = get(near_ref, block, tile(index))
         t_real, t_imag = get(in_ref.at[:, 1], block, tile(index))
         return (
             jnp.where(use_loss, t_real, real * t_real + imag * t_imag),
@@ -276,11 +280,9 @@
         )
 
     along_rows(
-        passing,
-        lambda index, block, value: put(out_ref, block, tile(index), value),
-        stage,
-        held,
-    )
+        lambda index, block: get(in_ref.at[:, 0], block, tile(index)), put_wave, stage, held
+    )
+    along_rows(passing, put_onward, stage, held)
 
 
 def light_tables():
@@ -351,7 +353,8 @@
     exit_ref,
     t_ref,
     wave_ref,
-    onward_ref,
+    far_ref,
+    near_ref,
     entry_hbm,
     exit_hbm,
     plain_hbm,
@@ -369,7 +372,8 @@
     for index in range(TILES):
         write_products(index, wave_ref, lights[0], lit_x_ref, entry_ref, entry_out)
         start([outs[0][index]])
-        along_lanes(index, onward_ref, packed, stage, moved)
+        source, place = (far_ref, index) if index < FAR else (near_ref, index - FAR)
+        along_lanes(index, source, packed, stage, moved, place)
         write_products(index, packed, lights[1], lit_x_ref, exit_ref, exit_out, t_ref, plain_out)
         start([outs[1][index], outs[2][index]])
     for index in range(TILES):
@@ -379,8 +383,10 @@
 WHOLE = pl.BlockSpec(memory_space=pltpu.VMEM)
 SCALAR = pl.BlockSpec(memory_space=pltpu.SMEM)
 OUTSIDE = pl.BlockSpec(memory_space=pltpu.HBM)
+FAR = TILES // 2
 CHAIN = (BLOCKS, 2, HALF, LANES)
-PACKED = jax.ShapeDtypeStruct(CHAIN, jnp.float32)
+NEAR_SHAPE = jax.ShapeDtypeStruct((BLOCKS, 2, 2 * HALF - 8 * FAR, LANES), jnp.float32)
+FAR_SHAPE = jax.ShapeDtypeStruct((BLOCKS, 2, 8 * FAR, LANES), jnp.float32)
 BOTH = jax.ShapeDtypeStruct((BLOCKS, 2, 2, HALF, LANES), jnp.float32)
 FIELD = jax.ShapeDtypeStruct((2, WIDTH, N), jnp.float32)
 FIELD_BUFFER = pltpu.VMEM(FIELD.shape, jnp.float32)
@@ -425,13 +431,18 @@
         [BUFFER, BUFFER],
     )
     both, info = lax.optimization_barrier((both, info))
-    wave, onward = call(
-        column_kernel, (PACKED, PACKED), [info, exchange(both)], "columns", [BUFFER, HELD], 1
-    )
-    onward = exchange(onward)
-    wave, onward = lax.optimization_barrier((wave, onward))
-    onward = to_previous(onward)
-    wave = exchange(wave)
+    near, far = call(
+        column_kernel,
+        (NEAR_SHAPE, FAR_SHAPE),
+        [info, exchange(both)],
+        "columns",
+        [BUFFER, HELD],
+        1,
+    )
+    far = to_previous(far)
+    near = exchange(near)
+    near, far = lax.optimization_barrier((near, far))
+    onward = to_previous(near[:, :, HALF:, :])
     grad_entry, grad_exit, leaving = call(
         last_kernel,
         (FIELD, FIELD, FIELD),
@@ -444,7 +455,8 @@
             fields_entry[0],
             fields_exit[0],
             t_exit[0],
-            wave,
+            near,
+            exchange(far),
             onward,
         ],
         "last",

time: 95.5 us -> 96.4 us (level)
  blocking collectives: 78.4 us -> 52.8 us
  waiting for transfers between devices: 1.49 us -> 17.3 us
  starting transfers between devices: 5.26 us -> 14.8 us
  Pallas kernels: 7.5 us -> 8.54 us
    all_to_all x3 -> x2, blocking collectives: 78.4 us -> 52.8 us  [exchange(): lax.all_to_all(packed, 'rows', split_axis=0, concat_axis=0, tiled=True)]
    ppermute x1 -> x2, waiting for transfers between devices: 1.49 us -> 11.1 us  [to_previous(): lax.ppermute(value, 'depth', [(s, (s - 1) % count) for s in range(count)])]
    all_to_all x0 -> x1, waiting for transfers between devices: none -> 6.25 us  [exchange(): lax.all_to_all(packed, 'rows', split_axis=0, concat_axis=0, tiled=True)]
    ppermute x1 -> x2, starting transfers between devices: 5.26 us -> 10.7 us  [to_previous(): lax.ppermute(value, 'depth', [(s, (s - 1) % count) for s in range(count)])]
    all_to_all x0 -> x1, starting transfers between devices: none -> 4.1 us  [exchange(): lax.all_to_all(packed, 'rows', split_axis=0, concat_axis=0, tiled=True)]
    pallas_call x3, Pallas kernels: 7.5 us -> 8.54 us  [call(): pl.pallas_call(kernel, out_shape=out_shape, in_specs=[SCALAR] * scalars +...]
  transfers between devices with their start and end apart: 1 -> 3, of which waited for: 1 -> 2; matrix products, arithmetic and copies ran while one was open for 0% -> 0% of each run, Pallas kernels for 0% -> 0%
where the time goes in v6:
time: 96.4 us; the launch traced here: 96 us
  blocking collectives  52.8 us (55%)
  waiting for transfers between devices  17.3 us (18%)
  starting transfers between devices  14.8 us (15%)
  Pallas kernels  8.54 us (9%)
  other arithmetic  1.81 us (2%)
    all_to_all x2, blocking collectives, exchange(): lax.all_to_all(packed, 'rows', split_axis=0, concat_axis=0, tiled=True)  52.8 us
    ppermute x2, waiting for transfers between devices, to_previous(): lax.ppermute(value, 'depth', [(s, (s - 1) % count) for s in range(count)])  11.1 us
    ppermute x2, starting transfers between devices, to_previous(): lax.ppermute(value, 'depth', [(s, (s - 1) % count) for s in range(count)])  10.7 us
    pallas_call x3, Pallas kernels, call(): pl.pallas_call(kernel, out_shape=out_shape, in_specs=[SCALAR] * scalars +...  8.54 us
    all_to_all x1, waiting for transfers between devices, exchange(): lax.all_to_all(packed, 'rows', split_axis=0, concat_axis=0, tiled=True)  6.25 us
    all_to_all x1, starting transfers between devices, exchange(): lax.all_to_all(packed, 'rows', split_axis=0, concat_axis=0, tiled=True)  4.1 us
  transfers between devices with their start and end apart: 3, of which 2 were waited for; matrix products, arithmetic and copies ran while one was open for 0% of the time, Pallas kernels for 0%

profile of v6, /device:TPU:1, one launch (start us, length us, event | category | flops | bytes accessed | tf_op | source)
XLA Modules:
  0.0 96.0 jit_solution(4755191571741967153)
XLA Ops:
  0.6 0.0 copy-start
  0.6 0.1 pad_add_fusion.info_ref
  0.7 1.7 %bitcast_select_fusion.other_ref = f32[2,64,2048]{2,1,0:T(8,128)S(1)} fusion(f32[2,64,2048]{2,1,0:T(8,128)} %param.11, f32[1,2,64,2048]{3,2,1,0:T(8,128)} %param.12, pred[]{:T(512)S(6)} %eq.7), kind=kLoop, calls=%fused_computation | loop fusion | flops 262144 | bytes 3145729 | tf_op jit(solution)/shard_map/jit(_where)/select_n | solution.py:429
  2.5 0.0 copy-done
  2.5 1.5 %enter.1 = f32[32,2,2,32,128]{4,3,2,1,0:T(8,128)S(1)} custom-call(f32[2,64,2048]{2,1,0:T(8,128)S(1)} %bitcast.11, f32[2,64,2048]{2,1,0:T(8,128)S(1)} %bitcast_select_fusion.other_ref), custom_call_target="tpu_custom_call" | custom-call | flops 83886080 | bytes 4194304 | tf_op jit(solution)/shard_map/enter/pallas_call | solution.py:401
  4.0 36.5 %all_to_all.15.in_ref = f32[32,2,2,32,128]{4,3,2,1,0:T(8,128)S(1)} all-to-all(f32[32,2,2,32,128]{4,3,2,1,0:T(8,128)S(1)} %enter.1), channel_id=1, replica_groups=mesh['depth'=8,'rows'=32] {'rows'}, dimensions={0} | all-to-all | bytes 4194304 | tf_op jit(solution)/shard_map/all_to_all | solution.py:414
  40.5 3.4 %columns.1 = (f32[32,2,48,128]{3,2,1,0:T(8,128)}, f32[32,2,16,128]{3,2,1,0:T(8,128)S(1)}) custom-call(s32[2]{0:T(128)S(1)} %pad_add_fusion.info_ref, f32[32,2,2,32,128]{4,3,2,1,0:T(8,128)S(1)} %all_to_all.15.in_ref), custom_call_target="tpu_custom_call" | custom-call | flops 83886240 | bytes 4194312 | tf_op jit(solution)/shard_map/columns/pallas_call | solution.py:401
  43.9 0.0 copy-start.1
  43.9 0.0 copy-start.7
  43.9 4.1 %all-to-all-start.1 = ((f32[32,2,48,128]{3,2,1,0:T(8,128)}), f32[32,2,48,128]{3,2,1,0:T(8,128)S(1)}, u32[]{:S(2)}, u32[]{:S(2)}) async-start(f32[32,2,48,128]{3,2,1,0:T(8,128)} %get-tuple-element.14), calls=%async_computation.1 | async-start | bytes 3145728 | tf_op jit(solution)/shard_map/all_to_all | solution.py:414
  48.0 5.3 %collective-permute-start = (f32[32,2,16,128]{3,2,1,0:T(8,128)S(1)}, f32[32,2,16,128]{3,2,1,0:T(8,128)}, u32[]{:S(2)}, u32[]{:S(2)}) collective-permute-start(f32[32,2,16,128]{3,2,1,0:T(8,128)S(1)} %get-tuple-element.15), channel_id=1, source_target_pairs={{0,224},{32,0},{64,32},{96,64},{128,96},{160,128},{192,160},{224,1... | collective-permute-start | bytes 1572872 | tf_op jit(solution)/shard_map/ppermute | solution.py:419
  53.4 11.1 %collective-permute-done = f32[32,2,16,128]{3,2,1,0:T(8,128)} collective-permute-done((f32[32,2,16,128]{3,2,1,0:T(8,128)S(1)}, f32[32,2,16,128]{3,2,1,0:T(8,128)}, u32[]{:S(2)}, u32[]{:S(2)}) %collective-permute-start) | collective-permute-done | bytes 524320 | tf_op jit(solution)/shard_map/ppermute | solution.py:419
  64.5 6.3 %all-to-all-done.1.wave_ref = f32[32,2,48,128]{3,2,1,0:T(8,128)S(1)} async-done(((f32[32,2,48,128]{3,2,1,0:T(8,128)}), f32[32,2,48,128]{3,2,1,0:T(8,128)S(1)}, u32[]{:S(2)}, u32[]{:S(2)}) %all-to-all-start.1) | async-done | bytes 1572896 | tf_op jit(solution)/shard_map/all_to_all | solution.py:414
  70.8 5.3 %collective-permute-start.1 = (f32[32,2,16,128]{3,2,1,0:T(8,128)S(1)}, f32[32,2,16,128]{3,2,1,0:T(8,128)S(1)}, u32[]{:S(2)}, u32[]{:S(2)}) collective-permute-start(f32[32,2,16,128]{3,2,1,0:T(8,128)S(1)} %slice.3), channel_id=1, source_target_pairs={{0,224},{32,0},{64,32},{96,64},{128,96},{160,128},{192,160},{224,1... | collective-permute-start | bytes 1572872 | tf_op jit(solution)/shard_map/ppermute | solution.py:419
  76.1 16.2 %all_to_all.16.far_ref = f32[32,2,16,128]{3,2,1,0:T(8,128)S(1)} all-to-all(f32[32,2,16,128]{3,2,1,0:T(8,128)} %collective-permute-done), channel_id=1, replica_groups=mesh['depth'=8,'rows'=32] {'rows'}, dimensions={0} | all-to-all | bytes 1048576 | tf_op jit(solution)/shard_map/all_to_all | solution.py:414
  92.3 0.0 collective-permute-done.1.near_ref
  92.3 0.0 copy-done.1
  92.3 0.0 copy-done.4
  92.3 0.0 copy-done.5
  92.4 0.0 copy-done.6
  92.4 0.0 copy-done.7
  92.4 0.0 copy-done.2
  92.4 0.0 copy-done.3
  92.4 3.7 %last.1 = (f32[2,64,2048]{2,1,0:T(8,128)}, f32[2,64,2048]{2,1,0:T(8,128)}, f32[2,64,2048]{2,1,0:T(8,128)}) custom-call(s32[1,2]{1,0:T(1,128)S(1)} %copy-done.7, s32[2]{0:T(128)S(1)} %pad_add_fusion.info_ref, f32[2,32]{1,0:T(2,128)S(1)} %copy-done.6, f32[30,16,128]{2,1,0:T(8,128)S(1)} %copy-done.4, f32[2,64,128]{2,1,0:T(8,128)S(1)} %copy-done.5, ...), custom_call_target="tpu_custom_call" | custom-call | flops 184489280 | bytes 9224464 | tf_op jit(solution)/shard_map/last/pallas_call | solution.py:401
  (6 shorter events, 0.0 us)
Async XLA Ops:
  0.6 1.9 %copy-start = (f32[1,2,64,2048]{3,2,1,0:T(8,128)S(1)}, f32[1,2,64,2048]{3,2,1,0:T(8,128)}, u32[]{:S(2)}) copy-start(f32[1,2,64,2048]{3,2,1,0:T(8,128)} %param.10) | copy-start | bytes 3145732
  43.9 48.4 %copy-start.1 = (f32[1,2,64,2048]{3,2,1,0:T(8,128)S(1)}, f32[1,2,64,2048]{3,2,1,0:T(8,128)}, u32[]{:S(2)}) copy-start(f32[1,2,64,2048]{3,2,1,0:T(8,128)} %param.14) | copy-start | bytes 3145732
  43.9 48.4 %copy-start.4 = (f32[30,16,128]{2,1,0:T(8,128)S(1)}, f32[30,16,128]{2,1,0:T(8,128)}, u32[]{:S(2)}) copy-start(f32[30,16,128]{2,1,0:T(8,128)} %constant.19.clone.lit_x_ref) | copy-start | bytes 737284
  43.9 48.4 %copy-start.5 = (f32[2,64,128]{2,1,0:T(8,128)S(1)}, f32[2,64,128]{2,1,0:T(8,128)}, u32[]{:S(2)}) copy-start(f32[2,64,128]{2,1,0:T(8,128)} %constant.20.clone.lit_y_ref) | copy-start | bytes 196612
  43.9 48.4 %copy-start.6 = (f32[2,32]{1,0:T(2,128)S(1)}, f32[2,32]{1,0:T(2,128)}, u32[]{:S(2)}) copy-start(f32[2,32]{1,0:T(2,128)} %constant.21.clone.turn_ref) | copy-start | bytes 772
  43.9 48.4 %copy-start.7 = (s32[1,2]{1,0:T(1,128)S(1)}, s32[1,2]{1,0:T(1,128)}, u32[]{:S(2)}) copy-start(s32[1,2]{1,0:T(1,128)} %led_ref.1) | copy-start | bytes 28
  43.9 26.8 %all-to-all-start.1 = ((f32[32,2,48,128]{3,2,1,0:T(8,128)}), f32[32,2,48,128]{3,2,1,0:T(8,128)S(1)}, u32[]{:S(2)}, u32[]{:S(2)}) async-start(f32[32,2,48,128]{3,2,1,0:T(8,128)} %get-tuple-element.14), calls=%async_computation.1 | async-start | bytes 3145728 | tf_op jit(solution)/shard_map/all_to_all | solution.py:414
  48.0 16.4 %collective-permute-start = (f32[32,2,16,128]{3,2,1,0:T(8,128)S(1)}, f32[32,2,16,128]{3,2,1,0:T(8,128)}, u32[]{:S(2)}, u32[]{:S(2)}) collective-permute-start(f32[32,2,16,128]{3,2,1,0:T(8,128)S(1)} %get-tuple-element.15), channel_id=1, source_target_pairs={{0,224},{32,0},{64,32},{96,64},{128,96},{160,128},{192,160},{224,1... | collective-permute-start | bytes 1572872 | tf_op jit(solution)/shard_map/ppermute | solution.py:419
  70.7 21.7 %copy-start.2 = (f32[1,2,64,2048]{3,2,1,0:T(8,128)S(1)}, f32[1,2,64,2048]{3,2,1,0:T(8,128)}, u32[]{:S(2)}) copy-start(f32[1,2,64,2048]{3,2,1,0:T(8,128)} %param.15) | copy-start | bytes 3145732
  70.7 21.7 %copy-start.3 = (f32[1,2,64,2048]{3,2,1,0:T(8,128)S(1)}, f32[1,2,64,2048]{3,2,1,0:T(8,128)}, u32[]{:S(2)}) copy-start(f32[1,2,64,2048]{3,2,1,0:T(8,128)} %param.13) | copy-start | bytes 3145732
  70.8 21.6 %collective-permute-start.1 = (f32[32,2,16,128]{3,2,1,0:T(8,128)S(1)}, f32[32,2,16,128]{3,2,1,0:T(8,128)S(1)}, u32[]{:S(2)}, u32[]{:S(2)}) collective-permute-start(f32[32,2,16,128]{3,2,1,0:T(8,128)S(1)} %slice.3), channel_id=1, source_target_pairs={{0,224},{32,0},{64,32},{96,64},{128,96},{160,128},{192,160},{224,1... | collective-permute-start | bytes 1572872 | tf_op jit(solution)/shard_map/ppermute | solution.py:419

commit v7 on v4

--- a/solution.py
+++ b/solution.py
@@ -162,28 +162,41 @@
 
 
 def along_rows(load, store, stage, held):
+    row_ids = lax.broadcasted_iota(jnp.int32, (8, LANES), 0)
     low = lane_ids() < WIDTH
     for index in range(TILES):
         rows = tile(index)
 
         def hold(freq, value):
-            shift, plain, wrapped = shift_of(freq)
-            plain = scaled(value, plain)
-            wrapped = scaled(value, wrapped) if shift else None
+            shift = shift_of(freq)[0]
             if shift > HALF:
-                put(held, freq, rows, wrapped)
+                put(held, freq, rows, value)
+            if shift:
+                crossed = tuple(pltpu.roll(v, WIDTH, 1) for v in value)
+                put(held, freq, pl.ds(HALF + 8 * index, 8), crossed)
             if shift < HALF:
-                put(held, freq, pl.ds(2 * HALF + 8 * index, 8), plain)
-            if shift:
-                crossed = tuple(
-                    pltpu.roll(jnp.where(low, p, w), WIDTH, 1) for p, w in zip(plain, wrapped)
-                )
-                put(held, freq, pl.ds(HALF + 8 * index, 8), crossed)
+                put(held, freq, pl.ds(2 * HALF + 8 * index, 8), value)
 
         block_dft(functools.partial(load, index), hold, stage, rows, -1)
+
+    def shifted(index, freq):
+        shift, plain, wrapped = shift_of(freq)
+        begin = 2 * HALF - shift + 8 * index
+        value = get(held, freq, pl.ds(begin, 8))
+        if begin >= 2 * HALF:
+            return scaled(value, plain)
+        if begin + 8 <= HALF:
+            return scaled(value, wrapped)
+        mask = row_ids >= jnp.where(low, 2 * HALF - begin, HALF - begin)
+        return times(
+            value,
+            jnp.where(mask, np.float32(plain.real), np.float32(wrapped.real)),
+            jnp.where(mask, np.float32(plain.imag), np.float32(wrapped.imag)),
+        )
+
     for index in range(TILES):
         block_dft(
-            lambda freq: get(held, freq, pl.ds(2 * HALF - shift_of(freq)[0] + 8 * index, 8)),
+            functools.partial(shifted, index),
             functools.partial(store, index),
             stage,
             tile(index),
@@ -245,7 +258,20 @@
         )
 
 
-def column_kernel(info_ref, in_ref, wave_ref, out_ref, stage, held):
+def column_kernel(
+    led_ref,
+    info_ref,
+    turn_ref,
+    all_x_ref,
+    all_y_ref,
+    in_ref,
+    wave_ref,
+    out_ref,
+    lit_x_ref,
+    lit_y_ref,
+    stage,
+    held,
+):
     use_loss = info_ref[1] == 1
     along_rows(
         lambda index, block: get(in_ref.at[:, 0], block, tile(index)),
@@ -268,6 +294,8 @@
         stage,
         held,
     )
+    for tick in range(2):
+        write_light(tick, led_ref, info_ref, turn_ref, all_x_ref, all_y_ref, lit_x_ref, lit_y_ref)
 
 
 def light_tables():
@@ -279,41 +307,45 @@
     return (
         np.concatenate([along_x.real, along_x.imag]).reshape(-1, N // LANES, LANES).astype(np.float32),
         np.stack([along_y.real, along_y.imag]).astype(np.float32),
-        np.stack([turns.real, turns.imag]).astype(np.float32),
-    )
-
-
-def light_rows(tick, led_ref, info_ref, turn_ref, lit_y_ref):
+        np.stack([np.tile(part[:, None], LANES) for part in (turns.real, turns.imag)]).astype(
+            np.float32
+        ),
+    )
+
+
+def write_light(
+    tick, led_ref, info_ref, turn_ref, all_x_ref, all_y_ref, lit_x_ref, lit_y_ref
+):
     led = led_ref[0, tick]
     column_shift = led // LED_SIDE
     row_shift = led - column_shift * LED_SIDE
     turn = (info_ref[0] * (row_shift - LED_SIDE // 2)) & (BLOCKS - 1)
-    turn_real, turn_imag = turn_ref[0, turn], turn_ref[1, turn]
+    turns = [turn_ref[part, pl.ds(turn, 1), :] for part in range(2)]
     chosen = lane_ids() == row_shift
-
-    def lit_rows(rows):
+    for part in range(2):
+        lit_x_ref[tick, part] = all_x_ref[column_shift + part * LED_SIDE]
+    for index in range(WIDTH // 8):
+        rows = tile(index)
         pair = tuple(
-            jnp.sum(jnp.where(chosen, lit_y_ref[part, rows, :], 0.0), axis=1, keepdims=True)
+            jnp.sum(jnp.where(chosen, all_y_ref[part, rows, :], 0.0), axis=1, keepdims=True)
             for part in range(2)
         )
-        pair = tuple(jnp.broadcast_to(v, (8, LANES)) for v in pair)
-        return times(pair, turn_real, turn_imag)
-
-    return column_shift, lit_rows
-
-
-def write_products(index, wave_ref, lights, lit_x_ref, field_ref, out_ref, *plain):
-    column_shift, lit_rows = lights
-    lit_y = [lit_rows(natural(index, half)) for half in range(2)]
+        pair = times(tuple(jnp.broadcast_to(v, (8, LANES)) for v in pair), *turns)
+        for part in range(2):
+            lit_y_ref[tick, part, rows, :] = pair[part]
+
+
+def write_products(tick, index, wave_ref, lit_x_ref, lit_y_ref, field_ref, out_ref, *plain):
+    lit_y = [
+        [lit_y_ref[tick, part, natural(index, half), :] for part in range(2)]
+        for half in range(2)
+    ]
     for pair in range(BLOCKS // 2):
         cols = pl.ds(pair * LANES, LANES)
         left = get(wave_ref, 2 * pair, tile(index))
         right = get(wave_ref, 2 * pair + 1, tile(index))
         reals, imags = halves(left[0], right[0]), halves(left[1], right[1])
-        lit_x = (
-            lit_x_ref[column_shift, pair : pair + 1, :],
-            lit_x_ref[column_shift + LED_SIDE, pair : pair + 1, :],
-        )
+        lit_x = [lit_x_ref[tick, part, pair : pair + 1, :] for part in range(2)]
         for half in range(2):
             rows = natural(index, half)
             real, imag = reals[half], imags[half]
@@ -328,31 +360,16 @@
             out_ref[1, rows, cols] = imag * f_real - real * f_imag
 
 
-def entry_kernel(
-    led_ref,
-    info_ref,
-    turn_ref,
-    lit_x_ref,
-    lit_y_ref,
-    field_ref,
-    wave_ref,
-    out_hbm,
-    out,
-    sems,
-):
+def entry_kernel(lit_x_ref, lit_y_ref, field_ref, wave_ref, out_hbm, out, sems):
     outs = field_copies(out, out_hbm, sems)
-    lights = light_rows(0, led_ref, info_ref, turn_ref, lit_y_ref)
-    for index in range(TILES):
-        write_products(index, wave_ref, lights, lit_x_ref, field_ref, out)
+    for index in range(TILES):
+        write_products(0, index, wave_ref, lit_x_ref, lit_y_ref, field_ref, out)
         start([outs[index]])
     for index in range(TILES):
         wait(outs[index])
 
 
 def exit_kernel(
-    led_ref,
-    info_ref,
-    turn_ref,
     lit_x_ref,
     lit_y_ref,
     field_ref,
@@ -370,10 +387,9 @@
 ):
     outs = field_copies(out, out_hbm, out_sems)
     plains = field_copies(plain, plain_hbm, plain_sems)
-    lights = light_rows(1, led_ref, info_ref, turn_ref, lit_y_ref)
     for index in range(TILES):
         along_lanes(index, in_ref, packed, stage, moved)
-        write_products(index, packed, lights, lit_x_ref, field_ref, out, t_ref, plain)
+        write_products(1, index, packed, lit_x_ref, lit_y_ref, field_ref, out, t_ref, plain)
         start([outs[index], plains[index]])
     for index in range(TILES):
         wait(outs[index] + plains[index])
@@ -384,6 +400,8 @@
 OUTSIDE = pl.BlockSpec(memory_space=pltpu.HBM)
 CHAIN = (BLOCKS, 2, HALF, LANES)
 PACKED = jax.ShapeDtypeStruct(CHAIN, jnp.float32)
+LIT_X = jax.ShapeDtypeStruct((2, 2, N // LANES, LANES), jnp.float32)
+LIT_Y = jax.ShapeDtypeStruct((2, 2, WIDTH, LANES), jnp.float32)
 BOTH = jax.ShapeDtypeStruct((BLOCKS, 2, 2, HALF, LANES), jnp.float32)
 FIELD = jax.ShapeDtypeStruct((2, WIDTH, N), jnp.float32)
 FIELD_BUFFER = pltpu.VMEM(FIELD.shape, jnp.float32)
@@ -419,7 +437,7 @@
 def per_device(grad_arriving, loss_grad, t_entry, t_exit, fields_entry, fields_exit, led_index):
     first = (lax.axis_index("depth") == 0).astype(jnp.int32)
     info = jnp.stack([lax.axis_index("rows"), first]).astype(jnp.int32)
-    lit_x, lit_y, turns = (jnp.asarray(table) for table in light_tables())
+    all_x, all_y, turns = (jnp.asarray(table) for table in light_tables())
     both = call(
         enter_kernel,
         BOTH,
@@ -428,30 +446,32 @@
         [BUFFER, BUFFER],
     )
     both, info = lax.optimization_barrier((both, info))
-    wave, onward = call(
-        column_kernel, (PACKED, PACKED), [info, exchange(both)], "columns", [BUFFER, HELD], 1
+    wave, onward, lit_x, lit_y = call(
+        column_kernel,
+        (PACKED, PACKED, LIT_X, LIT_Y),
+        [led_index, info, turns, all_x, all_y, exchange(both)],
+        "columns",
+        [BUFFER, HELD],
+        2,
     )
     onward = to_previous(onward)
     wave = exchange(wave)
-    lights = [led_index, info, turns, lit_x, lit_y]
     grad_entry = call(
         entry_kernel,
         FIELD,
-        [*lights, fields_entry[0], wave],
+        [lit_x, lit_y, fields_entry[0], wave],
         "entry",
         [FIELD_BUFFER, SEMS],
-        3,
-        OUTSIDE,
+        out_spec=OUTSIDE,
     )
     onward, grad_entry = lax.optimization_barrier((onward, grad_entry))
     grad_exit, leaving = call(
         exit_kernel,
         (FIELD, FIELD),
-        [*lights, fields_exit[0], t_exit[0], exchange(onward)],
+        [lit_x, lit_y, fields_exit[0], t_exit[0], exchange(onward)],
         "exit",
         [BUFFER, BUFFER, BUFFER, FIELD_BUFFER, FIELD_BUFFER, SEMS, SEMS],
-        3,
-        OUTSIDE,
+        out_spec=OUTSIDE,
     )
     return (grad_entry[None], grad_exit[None], leaving[None])
 

time: 95.2 us -> 94.8 us (level)
  Pallas kernels: 8.92 us -> 7.67 us
    pallas_call x4, Pallas kernels: 8.92 us -> 7.67 us  [call(): pl.pallas_call(kernel, out_shape=out_shape, in_specs=[SCALAR] * scalars +...]
  transfers between devices with their start and end apart: 1 -> 1, of which waited for: 0 -> 1; matrix products, arithmetic and copies ran while one was open for 0% -> 0% of each run, Pallas kernels for 2% -> 1%
where the time goes in v7:
time: 94.8 us; the launch traced here: 94.6 us
  blocking collectives  78.8 us (83%)
  Pallas kernels  7.67 us (8%)
  starting transfers between devices  5.34 us (6%)
  other arithmetic  1.81 us (2%)
    all_to_all x3, blocking collectives, exchange(): lax.all_to_all(packed, 'rows', split_axis=0, concat_axis=0, tiled=True)  78.8 us
    pallas_call x4, Pallas kernels, call(): pl.pallas_call(kernel, out_shape=out_shape, in_specs=[SCALAR] * scalars +...  7.67 us
    ppermute x1, starting transfers between devices, to_previous(): lax.ppermute(value, 'depth', [(s, (s - 1) % count) for s in range(count)])  5.34 us
  transfers between devices with their start and end apart: 1, of which 1 were waited for; matrix products, arithmetic and copies ran while one was open for 0% of the time, Pallas kernels for 1%

profile of v7, /device:TPU:1, one launch (start us, length us, event | category | flops | bytes accessed | tf_op | source)
XLA Modules:
  0.0 94.6 jit_solution(8233123360850015367)
XLA Ops:
  0.6 0.0 copy-start.3
  0.6 0.1 pad_add_fusion.info_ref
  0.7 1.7 %bitcast_select_fusion.other_ref = f32[2,64,2048]{2,1,0:T(8,128)S(1)} fusion(f32[2,64,2048]{2,1,0:T(8,128)} %param.11, f32[1,2,64,2048]{3,2,1,0:T(8,128)} %param.12, pred[]{:T(512)S(6)} %eq.7), kind=kLoop, calls=%fused_computation | loop fusion | flops 262144 | bytes 3145729 | tf_op jit(solution)/shard_map/jit(_where)/select_n | solution.py:444
  2.5 0.0 copy-done.3
  2.5 1.5 %enter.1 = f32[32,2,2,32,128]{4,3,2,1,0:T(8,128)S(1)} custom-call(f32[2,64,2048]{2,1,0:T(8,128)S(1)} %bitcast.14, f32[2,64,2048]{2,1,0:T(8,128)S(1)} %bitcast_select_fusion.other_ref), custom_call_target="tpu_custom_call" | custom-call | flops 83886080 | bytes 4194304 | tf_op jit(solution)/shard_map/enter/pallas_call | solution.py:416
  4.0 0.0 copy-start.4
  4.0 0.0 copy-start.5
  4.0 0.0 copy-start.6
  4.0 0.0 copy-start.7
  4.0 36.7 %all_to_all.15.in_ref = f32[32,2,2,32,128]{4,3,2,1,0:T(8,128)S(1)} all-to-all(f32[32,2,2,32,128]{4,3,2,1,0:T(8,128)S(1)} %enter.1), channel_id=1, replica_groups=mesh['depth'=8,'rows'=32] {'rows'}, dimensions={0} | all-to-all | bytes 4194304 | tf_op jit(solution)/shard_map/all_to_all | solution.py:429
  40.7 0.0 copy-done.4
  40.7 0.0 copy-done.5
  40.7 0.0 copy-done.6
  40.7 0.0 copy-done.7
  40.7 0.0 copy-start
  40.7 2.4 %columns.1 = (f32[32,2,32,128]{3,2,1,0:T(8,128)S(1)}, f32[32,2,32,128]{3,2,1,0:T(8,128)S(1)}, f32[2,2,16,128]{3,2,1,0:T(8,128)S(1)}, f32[2,2,64,128]{3,2,1,0:T(8,128)S(1)}) custom-call(s32[1,2]{1,0:T(1,128)S(1)} %copy-done.7, s32[2]{0:T(128)S(1)} %pad_add_fusion.info_ref, f32[2,32,128]{2,1,0:T(8,128)S(1)} %copy-done.6, f32[30,16,128]{2,1,0:T(8,128)S(1)} %copy-done.4, ...), custom_call_target="tpu_custom_call" | custom-call | flops 94044480 | bytes 4702224 | tf_op jit(solution)/shard_map/columns/pallas_call | solution.py:416
  43.1 5.3 %collective-permute-start = (f32[32,2,32,128]{3,2,1,0:T(8,128)S(1)}, f32[32,2,32,128]{3,2,1,0:T(8,128)S(1)}, u32[]{:S(2)}, u32[]{:S(2)}) collective-permute-start(f32[32,2,32,128]{3,2,1,0:T(8,128)S(1)} %get-tuple-element.15), channel_id=1, source_target_pairs={{0,224},{32,0},{64,32},{96,64},{128,96},{160,128},{192,160},{224,1... | collective-permute-start | bytes 3145736 | tf_op jit(solution)/shard_map/ppermute | solution.py:434
  48.5 20.9 %all_to_all.16.wave_ref = f32[32,2,32,128]{3,2,1,0:T(8,128)S(1)} all-to-all(f32[32,2,32,128]{3,2,1,0:T(8,128)S(1)} %get-tuple-element.18), channel_id=1, replica_groups=mesh['depth'=8,'rows'=32] {'rows'}, dimensions={0} | all-to-all | bytes 2097152 | tf_op jit(solution)/shard_map/all_to_all | solution.py:429
  69.4 0.0 copy-done
  69.4 1.2 %entry.1 = f32[2,64,2048]{2,1,0:T(8,128)} custom-call(f32[2,2,16,128]{3,2,1,0:T(8,128)S(1)} %get-tuple-element.16.lit_x_ref, f32[2,2,64,128]{3,2,1,0:T(8,128)S(1)} %get-tuple-element.17.lit_y_ref, f32[2,64,2048]{2,1,0:T(8,128)S(1)} %bitcast.11, f32[32,2,32,128]{3,2,1,0:T(8,128)S(1)} %all_to_all.16.wave_ref), custom_call_target="tpu_custom_call" | custom-call | flops 66191360 | bytes 3309568 | tf_op jit(solution)/shard_map/entry/pallas_call | solution.py:416
  70.7 0.2 collective-permute-done
  70.9 21.2 %all_to_all.17.in_ref = f32[32,2,32,128]{3,2,1,0:T(8,128)S(1)} all-to-all(f32[32,2,32,128]{3,2,1,0:T(8,128)S(1)} %collective-permute-done), channel_id=1, replica_groups=mesh['depth'=8,'rows'=32] {'rows'}, dimensions={0} | all-to-all | bytes 2097152 | tf_op jit(solution)/shard_map/all_to_all | solution.py:429
  92.1 0.0 copy-done.1
  92.1 2.6 %exit.1 = (f32[2,64,2048]{2,1,0:T(8,128)}, f32[2,64,2048]{2,1,0:T(8,128)}) custom-call(f32[2,2,16,128]{3,2,1,0:T(8,128)S(1)} %get-tuple-element.16.lit_x_ref, f32[2,2,64,128]{3,2,1,0:T(8,128)S(1)} %get-tuple-element.17.lit_y_ref, f32[2,64,2048]{2,1,0:T(8,128)S(1)} %bitcast.12, f32[2,64,2048]{2,1,0:T(8,128)S(1)} %bitcast.13, ...), custom_call_target="tpu_custom_call" | custom-call | flops 108134400 | bytes 5406720 | tf_op jit(solution)/shard_map/exit/pallas_call | solution.py:416
  (3 shorter events, 0.0 us)
Async XLA Ops:
  0.6 1.9 %copy-start.3 = (f32[1,2,64,2048]{3,2,1,0:T(8,128)S(1)}, f32[1,2,64,2048]{3,2,1,0:T(8,128)}, u32[]{:S(2)}) copy-start(f32[1,2,64,2048]{3,2,1,0:T(8,128)} %param.10) | copy-start | bytes 3145732
  4.0 36.7 %copy-start.4 = (f32[30,16,128]{2,1,0:T(8,128)S(1)}, f32[30,16,128]{2,1,0:T(8,128)}, u32[]{:S(2)}) copy-start(f32[30,16,128]{2,1,0:T(8,128)} %constant.19.clone.all_x_ref) | copy-start | bytes 737284
  4.0 36.7 %copy-start.5 = (f32[2,64,128]{2,1,0:T(8,128)S(1)}, f32[2,64,128]{2,1,0:T(8,128)}, u32[]{:S(2)}) copy-start(f32[2,64,128]{2,1,0:T(8,128)} %constant.20.clone.all_y_ref) | copy-start | bytes 196612
  4.0 36.7 %copy-start.6 = (f32[2,32,128]{2,1,0:T(8,128)S(1)}, f32[2,32,128]{2,1,0:T(8,128)}, u32[]{:S(2)}) copy-start(f32[2,32,128]{2,1,0:T(8,128)} %constant.21.clone.turn_ref) | copy-start | bytes 98308
  4.0 36.7 %copy-start.7 = (s32[1,2]{1,0:T(1,128)S(1)}, s32[1,2]{1,0:T(1,128)}, u32[]{:S(2)}) copy-start(s32[1,2]{1,0:T(1,128)} %led_ref.1) | copy-start | bytes 28
  40.7 28.7 %copy-start = (f32[1,2,64,2048]{3,2,1,0:T(8,128)S(1)}, f32[1,2,64,2048]{3,2,1,0:T(8,128)}, u32[]{:S(2)}) copy-start(f32[1,2,64,2048]{3,2,1,0:T(8,128)} %param.14) | copy-start | bytes 3145732
  43.1 27.8 %collective-permute-start = (f32[32,2,32,128]{3,2,1,0:T(8,128)S(1)}, f32[32,2,32,128]{3,2,1,0:T(8,128)S(1)}, u32[]{:S(2)}, u32[]{:S(2)}) collective-permute-start(f32[32,2,32,128]{3,2,1,0:T(8,128)S(1)} %get-tuple-element.15), channel_id=1, source_target_pairs={{0,224},{32,0},{64,32},{96,64},{128,96},{160,128},{192,160},{224,1... | collective-permute-start | bytes 3145736 | tf_op jit(solution)/shard_map/ppermute | solution.py:434
  69.4 22.7 %copy-start.1 = (f32[1,2,64,2048]{3,2,1,0:T(8,128)S(1)}, f32[1,2,64,2048]{3,2,1,0:T(8,128)}, u32[]{:S(2)}) copy-start(f32[1,2,64,2048]{3,2,1,0:T(8,128)} %param.15) | copy-start | bytes 3145732
  69.4 22.7 %copy-start.2 = (f32[1,2,64,2048]{3,2,1,0:T(8,128)S(1)}, f32[1,2,64,2048]{3,2,1,0:T(8,128)}, u32[]{:S(2)}) copy-start(f32[1,2,64,2048]{3,2,1,0:T(8,128)} %param.13) | copy-start | bytes 3145732

commit v8 on v7

--- a/solution.py
+++ b/solution.py
@@ -123,13 +123,14 @@
 
 
 def block_dft(load, emit, stage, rows, sign):
-    for k in range(4):
-        for j, value in enumerate(small_dft([load(4 * n + k) for n in range(8)], sign)):
-            put(stage, 8 * k + j, rows, turned(value, j * k, BLOCKS, sign))
-    for j in range(8):
-        outs = small_dft([get(stage, 8 * k + j, rows) for k in range(4)], sign)
-        for step, value in enumerate(outs):
-            emit(j + 8 * step, value)
+    half = BLOCKS // 2
+    for j, value in enumerate(small_dft([load(2 * n) for n in range(half)], sign)):
+        put(stage, j, rows, value)
+    odd = small_dft([load(2 * n + 1) for n in range(half)], sign)
+    for j, value in enumerate(odd):
+        even, value = get(stage, j, rows), turned(value, j, BLOCKS, sign)
+        emit(j, plus(even, value))
+        emit(j + half, minus(even, value))
 
 
 def along_lanes(index, source, target, stage, moved):

time: 94.8 us -> 94.9 us (level)
  no operation moved by 1% of the time
where the time goes in v8:
time: 94.9 us; the launch traced here: 94.7 us
  blocking collectives  78.8 us (83%)
  Pallas kernels  7.76 us (8%)
  starting transfers between devices  5.34 us (6%)
  other arithmetic  1.81 us (2%)
    all_to_all x3, blocking collectives, exchange(): lax.all_to_all(packed, 'rows', split_axis=0, concat_axis=0, tiled=True)  78.8 us
    pallas_call x4, Pallas kernels, call(): pl.pallas_call(kernel, out_shape=out_shape, in_specs=[SCALAR] * scalars +...  7.76 us
    ppermute x1, starting transfers between devices, to_previous(): lax.ppermute(value, 'depth', [(s, (s - 1) % count) for s in range(count)])  5.34 us
  transfers between devices with their start and end apart: 1, of which 1 were waited for; matrix products, arithmetic and copies ran while one was open for 0% of the time, Pallas kernels for 1%

profile of v8, /device:TPU:1, one launch (start us, length us, event | category | flops | bytes accessed | tf_op | source)
XLA Modules:
  0.0 94.7 jit_solution(12502501350289811534)
XLA Ops:
  0.6 0.0 copy-start.3
  0.6 0.1 pad_add_fusion.info_ref
  0.7 1.7 %bitcast_select_fusion.other_ref = f32[2,64,2048]{2,1,0:T(8,128)S(1)} fusion(f32[2,64,2048]{2,1,0:T(8,128)} %param.11, f32[1,2,64,2048]{3,2,1,0:T(8,128)} %param.12, pred[]{:T(512)S(6)} %eq.7), kind=kLoop, calls=%fused_computation | loop fusion | flops 262144 | bytes 3145729 | tf_op jit(solution)/shard_map/jit(_where)/select_n | solution.py:445
  2.5 0.0 copy-done.3
  2.5 1.5 %enter.1 = f32[32,2,2,32,128]{4,3,2,1,0:T(8,128)S(1)} custom-call(f32[2,64,2048]{2,1,0:T(8,128)S(1)} %bitcast.14, f32[2,64,2048]{2,1,0:T(8,128)S(1)} %bitcast_select_fusion.other_ref), custom_call_target="tpu_custom_call" | custom-call | flops 83886080 | bytes 4194304 | tf_op jit(solution)/shard_map/enter/pallas_call | solution.py:417
  4.0 0.0 copy-start.4
  4.0 0.0 copy-start.5
  4.0 0.0 copy-start.6
  4.0 0.0 copy-start.7
  4.1 36.7 %all_to_all.15.in_ref = f32[32,2,2,32,128]{4,3,2,1,0:T(8,128)S(1)} all-to-all(f32[32,2,2,32,128]{4,3,2,1,0:T(8,128)S(1)} %enter.1), channel_id=1, replica_groups=mesh['depth'=8,'rows'=32] {'rows'}, dimensions={0} | all-to-all | bytes 4194304 | tf_op jit(solution)/shard_map/all_to_all | solution.py:430
  40.7 0.0 copy-done.4
  40.7 0.0 copy-done.5
  40.7 0.0 copy-done.6
  40.7 0.0 copy-done.7
  40.7 0.0 copy-start
  40.8 2.4 %columns.1 = (f32[32,2,32,128]{3,2,1,0:T(8,128)S(1)}, f32[32,2,32,128]{3,2,1,0:T(8,128)S(1)}, f32[2,2,16,128]{3,2,1,0:T(8,128)S(1)}, f32[2,2,64,128]{3,2,1,0:T(8,128)S(1)}) custom-call(s32[1,2]{1,0:T(1,128)S(1)} %copy-done.7, s32[2]{0:T(128)S(1)} %pad_add_fusion.info_ref, f32[2,32,128]{2,1,0:T(8,128)S(1)} %copy-done.6, f32[30,16,128]{2,1,0:T(8,128)S(1)} %copy-done.4, ...), custom_call_target="tpu_custom_call" | custom-call | flops 94044480 | bytes 4702224 | tf_op jit(solution)/shard_map/columns/pallas_call | solution.py:417
  43.2 5.3 %collective-permute-start = (f32[32,2,32,128]{3,2,1,0:T(8,128)S(1)}, f32[32,2,32,128]{3,2,1,0:T(8,128)S(1)}, u32[]{:S(2)}, u32[]{:S(2)}) collective-permute-start(f32[32,2,32,128]{3,2,1,0:T(8,128)S(1)} %get-tuple-element.15), channel_id=1, source_target_pairs={{0,224},{32,0},{64,32},{96,64},{128,96},{160,128},{192,160},{224,1... | collective-permute-start | bytes 3145736 | tf_op jit(solution)/shard_map/ppermute | solution.py:435
  48.5 20.9 %all_to_all.16.wave_ref = f32[32,2,32,128]{3,2,1,0:T(8,128)S(1)} all-to-all(f32[32,2,32,128]{3,2,1,0:T(8,128)S(1)} %get-tuple-element.18), channel_id=1, replica_groups=mesh['depth'=8,'rows'=32] {'rows'}, dimensions={0} | all-to-all | bytes 2097152 | tf_op jit(solution)/shard_map/all_to_all | solution.py:430
  69.5 0.0 copy-done
  69.5 1.2 %entry.1 = f32[2,64,2048]{2,1,0:T(8,128)} custom-call(f32[2,2,16,128]{3,2,1,0:T(8,128)S(1)} %get-tuple-element.16.lit_x_ref, f32[2,2,64,128]{3,2,1,0:T(8,128)S(1)} %get-tuple-element.17.lit_y_ref, f32[2,64,2048]{2,1,0:T(8,128)S(1)} %bitcast.11, f32[32,2,32,128]{3,2,1,0:T(8,128)S(1)} %all_to_all.16.wave_ref), custom_call_target="tpu_custom_call" | custom-call | flops 66191360 | bytes 3309568 | tf_op jit(solution)/shard_map/entry/pallas_call | solution.py:417
  70.7 0.2 collective-permute-done
  70.9 21.2 %all_to_all.17.in_ref = f32[32,2,32,128]{3,2,1,0:T(8,128)S(1)} all-to-all(f32[32,2,32,128]{3,2,1,0:T(8,128)S(1)} %collective-permute-done), channel_id=1, replica_groups=mesh['depth'=8,'rows'=32] {'rows'}, dimensions={0} | all-to-all | bytes 2097152 | tf_op jit(solution)/shard_map/all_to_all | solution.py:430
  92.1 0.0 copy-done.1
  92.1 2.6 %exit.1 = (f32[2,64,2048]{2,1,0:T(8,128)}, f32[2,64,2048]{2,1,0:T(8,128)}) custom-call(f32[2,2,16,128]{3,2,1,0:T(8,128)S(1)} %get-tuple-element.16.lit_x_ref, f32[2,2,64,128]{3,2,1,0:T(8,128)S(1)} %get-tuple-element.17.lit_y_ref, f32[2,64,2048]{2,1,0:T(8,128)S(1)} %bitcast.12, f32[2,64,2048]{2,1,0:T(8,128)S(1)} %bitcast.13, ...), custom_call_target="tpu_custom_call" | custom-call | flops 108134400 | bytes 5406720 | tf_op jit(solution)/shard_map/exit/pallas_call | solution.py:417
  (3 shorter events, 0.0 us)
Async XLA Ops:
  0.6 1.9 %copy-start.3 = (f32[1,2,64,2048]{3,2,1,0:T(8,128)S(1)}, f32[1,2,64,2048]{3,2,1,0:T(8,128)}, u32[]{:S(2)}) copy-start(f32[1,2,64,2048]{3,2,1,0:T(8,128)} %param.10) | copy-start | bytes 3145732
  4.0 36.7 %copy-start.4 = (f32[30,16,128]{2,1,0:T(8,128)S(1)}, f32[30,16,128]{2,1,0:T(8,128)}, u32[]{:S(2)}) copy-start(f32[30,16,128]{2,1,0:T(8,128)} %constant.19.clone.all_x_ref) | copy-start | bytes 737284
  4.0 36.7 %copy-start.5 = (f32[2,64,128]{2,1,0:T(8,128)S(1)}, f32[2,64,128]{2,1,0:T(8,128)}, u32[]{:S(2)}) copy-start(f32[2,64,128]{2,1,0:T(8,128)} %constant.20.clone.all_y_ref) | copy-start | bytes 196612
  4.0 36.7 %copy-start.6 = (f32[2,32,128]{2,1,0:T(8,128)S(1)}, f32[2,32,128]{2,1,0:T(8,128)}, u32[]{:S(2)}) copy-start(f32[2,32,128]{2,1,0:T(8,128)} %constant.21.clone.turn_ref) | copy-start | bytes 98308
  4.0 36.7 %copy-start.7 = (s32[1,2]{1,0:T(1,128)S(1)}, s32[1,2]{1,0:T(1,128)}, u32[]{:S(2)}) copy-start(s32[1,2]{1,0:T(1,128)} %led_ref.1) | copy-start | bytes 28
  40.7 28.7 %copy-start = (f32[1,2,64,2048]{3,2,1,0:T(8,128)S(1)}, f32[1,2,64,2048]{3,2,1,0:T(8,128)}, u32[]{:S(2)}) copy-start(f32[1,2,64,2048]{3,2,1,0:T(8,128)} %param.14) | copy-start | bytes 3145732
  43.2 27.8 %collective-permute-start = (f32[32,2,32,128]{3,2,1,0:T(8,128)S(1)}, f32[32,2,32,128]{3,2,1,0:T(8,128)S(1)}, u32[]{:S(2)}, u32[]{:S(2)}) collective-permute-start(f32[32,2,32,128]{3,2,1,0:T(8,128)S(1)} %get-tuple-element.15), channel_id=1, source_target_pairs={{0,224},{32,0},{64,32},{96,64},{128,96},{160,128},{192,160},{224,1... | collective-permute-start | bytes 3145736 | tf_op jit(solution)/shard_map/ppermute | solution.py:435
  69.5 22.7 %copy-start.1 = (f32[1,2,64,2048]{3,2,1,0:T(8,128)S(1)}, f32[1,2,64,2048]{3,2,1,0:T(8,128)}, u32[]{:S(2)}) copy-start(f32[1,2,64,2048]{3,2,1,0:T(8,128)} %param.15) | copy-start | bytes 3145732
  69.5 22.7 %copy-start.2 = (f32[1,2,64,2048]{3,2,1,0:T(8,128)S(1)}, f32[1,2,64,2048]{3,2,1,0:T(8,128)}, u32[]{:S(2)}) copy-start(f32[1,2,64,2048]{3,2,1,0:T(8,128)} %param.13) | copy-start | bytes 3145732
